TPU v7x, 256 devices: a whole 4x4x8 slice. The times are simulated.
256 devices in a mesh: branch: 2 (over z_lo), seq: 8 (over x, core), dp: 16 (over y, z_hi).
Axes of the slice: x: 4, y: 4, z: 8 (z_hi: 4, z_lo: 2; z = z_hi * 2 + z_lo), core: 2. Of those that a mesh axis runs over, the one named last changes fastest.
Arguments:
- queries: bfloat16 [2, 16, 1024, 3072], P('branch', 'dp', 'seq'), may hold values from -8 to 8
- keys: bfloat16 [2, 16, 1024, 3072], P('branch', 'dp', 'seq'), may hold values from -8 to 8
- values: bfloat16 [2, 16, 1024, 3072], P('branch', 'dp', 'seq'), may hold values from -6 to 6
- cotangent: bfloat16 [2, 16, 1024, 5120], P('branch', 'dp', 'seq'), may hold values from -3 to 3
- gate: float32 [2, 16, 5120], P('branch', 'dp'), may hold values from 0.1 to 1.9
- w_out: bfloat16 [2, 3072, 5120], P('branch', ('seq', 'dp')), may hold values from -0.109375 to 0.109375
Outputs:
- grad_queries: bfloat16 [2, 16, 1024, 3072], P('branch', 'dp', 'seq')
- grad_keys: bfloat16 [2, 16, 1024, 3072], P('branch', 'dp', 'seq')
- grad_values: bfloat16 [2, 16, 1024, 3072], P('branch', 'dp', 'seq')
- grad_weight: float32 [2, 3072, 5120], P('branch', ('seq', 'dp'))
All inputs are finite; a program needn't handle non-finite values.
Results may differ from a plain program's by a relative error of at most 0.0088.
Values may be sent and summed in bfloat16 or wider, within the bound.
No kernel may reach another device: no remote copies, remote signals or barrier semaphores. Data moves between devices by JAX's collectives and lax.ppermute only.
A program may use at most 128 MiB of HBM per device.

v0:
```python
import functools

import jax
import jax.numpy as jnp
from jax import lax
from jax.experimental import pallas as pl
from jax.experimental.pallas import tpu as pltpu
from jax.sharding import Mesh, PartitionSpec as P

HD = 128
XS, CS, YS, ZS = 4, 2, 4, 4
RANKS = XS * CS
TOK = 128
SEQ = RANKS * TOK
NH = 3
WIDTH = NH * HD
D = 5120
QB = 256
TILE = 512
SCALE = HD**-0.5
LOG2E = 1.4426950408889634
F32 = jnp.float32
BF16 = jnp.bfloat16
NT = (((1,), (1,)), ((), ()))
NN = (((1,), (0,)), ((), ()))
VMEM_LIMIT = 56 * 1024 * 1024


def dot(a, b, dims=NN):
    return lax.dot_general(a, b, dims, preferred_element_type=F32)


def params(**more):
    return pltpu.CompilerParams(vmem_limit_bytes=VMEM_LIMIT, **more)


def cost(flops, nbytes, trans=0):
    return pl.CostEstimate(flops=flops, bytes_accessed=nbytes, transcendentals=trans)


def pack_body(q_ref, k_ref, v_ref, out_ref):
    out_ref[0, 0] = q_ref[...]
    out_ref[0, 1] = k_ref[...]
    out_ref[0, 2] = v_ref[...]


def pack(q, k, v):
    spec = pl.BlockSpec((TOK, WIDTH), lambda j: (0, j))
    return pl.pallas_call(
        pack_body,
        grid=(RANKS,),
        in_specs=[spec] * 3,
        out_specs=pl.BlockSpec((1, 3, TOK, WIDTH), lambda j: (j, 0, 0, 0)),
        out_shape=jax.ShapeDtypeStruct((RANKS, 3, TOK, WIDTH), BF16),
        compiler_params=params(),
        cost_estimate=cost(0, 2 * 3 * 2 * SEQ * WIDTH),
        name="pack",
    )(q, k, v)


def unpack_body(a_ref, b_ref, q_ref, k_ref, v_ref):
    split = a_ref.shape[-1]
    for i, ref in enumerate((q_ref, k_ref, v_ref)):
        ref[:, :split] = a_ref[0, i]
        ref[:, split:] = b_ref[0, i]


def unpack(a, b):
    def spec(array):
        return pl.BlockSpec((1, 3, TOK, array.shape[-1]), lambda j: (j, 0, 0, 0))

    out = pl.BlockSpec((TOK, WIDTH), lambda j: (0, j))
    return pl.pallas_call(
        unpack_body,
        grid=(RANKS,),
        in_specs=[spec(a), spec(b)],
        out_specs=[out] * 3,
        out_shape=[jax.ShapeDtypeStruct((TOK, RANKS * WIDTH), BF16)] * 3,
        compiler_params=params(),
        cost_estimate=cost(0, 2 * 3 * 2 * SEQ * WIDTH),
        name="unpack",
    )(a, b)


def forward_body(slot_ref, qkv_ref, prob_ref, att_ref, q_s, k_s, vt_s):
    block = pl.program_id(1)

    @pl.when(block == 0)
    def _():
        for s in range(RANKS):
            rows = pl.ds(s * TOK, TOK)
            piece = slot_ref[s]
            q_s[rows, :] = qkv_ref[piece, 0]
            k_s[rows, :] = qkv_ref[piece, 1]
            vt_s[:, rows] = qkv_ref[piece, 2].astype(F32).T.astype(BF16)

    q = q_s[pl.ds(pl.multiple_of(block * QB, QB), QB), :]
    scores = dot(k_s[...], q, NT)
    top = jnp.max(scores, axis=0, keepdims=True)
    e = jnp.exp2((scores - top) * (SCALE * LOG2E))
    norm = 1.0 / jnp.sum(e, axis=0, keepdims=True)
    prob = (e * norm).astype(BF16)
    prob_ref[0] = prob
    att_ref[...] = dot(vt_s[...], prob).astype(BF16)


def forward(slots, qkv):
    return pl.pallas_call(
        forward_body,
        grid_spec=pltpu.PrefetchScalarGridSpec(
            num_scalar_prefetch=1,
            grid=(NH, SEQ // QB),
            in_specs=[pl.BlockSpec((RANKS, 3, TOK, HD), lambda h, b, s: (0, 0, 0, h))],
            out_specs=[
                pl.BlockSpec((1, SEQ, QB), lambda h, b, s: (h, 0, b)),
                pl.BlockSpec((HD, QB), lambda h, b, s: (h, b)),
            ],
            scratch_shapes=[
                pltpu.VMEM((SEQ, HD), BF16),
                pltpu.VMEM((SEQ, HD), BF16),
                pltpu.VMEM((HD, SEQ), BF16),
            ],
        ),
        out_shape=[
            jax.ShapeDtypeStruct((NH, SEQ, SEQ), BF16),
            jax.ShapeDtypeStruct((WIDTH, SEQ), BF16),
        ],
        compiler_params=params(),
        cost_estimate=cost(4 * NH * SEQ * SEQ * HD, 2 * NH * SEQ * SEQ + 8 * SEQ * WIDTH, NH * SEQ * SEQ),
        name="forward",
    )(slots, qkv)


def backward_body(slot_ref, qkv_ref, prob_ref, gt_ref, att_ref, out_ref, q_s, v_s, kt_s, dk_s, dv_s):
    block = pl.program_id(1)
    last = pl.num_programs(1) - 1

    @pl.when(block == 0)
    def _():
        for s in range(RANKS):
            rows = pl.ds(s * TOK, TOK)
            piece = slot_ref[s]
            q_s[rows, :] = qkv_ref[piece, 0]
            kt_s[:, rows] = qkv_ref[piece, 1].astype(F32).T.astype(BF16)
            v_s[rows, :] = qkv_ref[piece, 2]
        dk_s[...] = jnp.zeros_like(dk_s)
        dv_s[...] = jnp.zeros_like(dv_s)

    gt = gt_ref[...]
    prob = prob_ref[0]
    delta = jnp.sum(gt.astype(F32) * att_ref[...].astype(F32), axis=0, keepdims=True)
    dprob = dot(v_s[...], gt)
    dscore = (prob.astype(F32) * ((dprob - delta) * SCALE)).astype(BF16)
    q = q_s[pl.ds(pl.multiple_of(block * QB, QB), QB), :]
    dv_s[...] += dot(prob, gt, NT)
    dk_s[...] += dot(dscore, q)
    dq = dot(kt_s[...], dscore).T.astype(BF16)
    for i in range(QB // TOK):
        out_ref[slot_ref[block * (QB // TOK) + i], 0] = dq[i * TOK : (i + 1) * TOK]

    @pl.when(block == last)
    def _():
        for s in range(RANKS):
            rows = pl.ds(s * TOK, TOK)
            out_ref[slot_ref[s], 1] = dk_s[rows, :].astype(BF16)
            out_ref[slot_ref[s], 2] = dv_s[rows, :].astype(BF16)


def backward(slots, qkv, prob, gt, att, first, count):
    return pl.pallas_call(
        backward_body,
        grid_spec=pltpu.PrefetchScalarGridSpec(
            num_scalar_prefetch=1,
            grid=(count, SEQ // QB),
            in_specs=[
                pl.BlockSpec((RANKS, 3, TOK, HD), lambda h, b, s: (0, 0, 0, h + first)),
                pl.BlockSpec((1, SEQ, QB), lambda h, b, s: (h + first, 0, b)),
                pl.BlockSpec((HD, QB), lambda h, b, s: (h + first, b)),
                pl.BlockSpec((HD, QB), lambda h, b, s: (h + first, b)),
            ],
            out_specs=pl.BlockSpec((RANKS, 3, TOK, HD), lambda h, b, s: (0, 0, 0, h)),
            scratch_shapes=[
                pltpu.VMEM((SEQ, HD), BF16),
                pltpu.VMEM((SEQ, HD), BF16),
                pltpu.VMEM((HD, SEQ), BF16),
                pltpu.VMEM((SEQ, HD), F32),
                pltpu.VMEM((SEQ, HD), F32),
            ],
        ),
        out_shape=jax.ShapeDtypeStruct((RANKS, 3, TOK, count * HD), BF16),
        compiler_params=params(),
        cost_estimate=cost(8 * count * SEQ * SEQ * HD, 2 * count * SEQ * (SEQ + 8 * HD), 0),
        name="backward",
    )(slots, qkv, prob, gt, att)


def weight_body(att_ref, *refs):
    out_ref = refs[-1]
    rows = jnp.concatenate([ref[...] for ref in refs[:-1]], axis=0)
    out_ref[...] = dot(att_ref[...], rows).astype(BF16)


def weight_grad(att, pieces):
    wide = pieces[0].shape[1]
    piece = pl.BlockSpec((TOK, TILE), lambda j: (0, j))
    return pl.pallas_call(
        weight_body,
        grid=(wide // TILE,),
        in_specs=[pl.BlockSpec((WIDTH, SEQ), lambda j: (0, 0))] + [piece] * RANKS,
        out_specs=pl.BlockSpec((WIDTH, TILE), lambda j: (0, j)),
        out_shape=jax.ShapeDtypeStruct((WIDTH, wide), BF16),
        compiler_params=params(),
        cost_estimate=cost(2 * WIDTH * SEQ * wide, 2 * (WIDTH * SEQ + SEQ * wide + WIDTH * wide)),
        name="weight_grad",
    )(att, *pieces)


def heads_body(count, carry, w_ref, *refs):
    acc_ref = refs[-1]
    out_ref = refs[-2]
    step = pl.program_id(0)

    @pl.when(step == 0)
    def _():
        acc_ref[...] = refs[RANKS][...] if carry else jnp.zeros_like(acc_ref)

    rows = jnp.concatenate([ref[...] for ref in refs[:RANKS]], axis=0)
    acc_ref[...] += dot(w_ref[...], rows, NT)

    @pl.when(step == count - 1)
    def _():
        out_ref[...] = acc_ref[...].astype(out_ref.dtype)


def heads_grad(weights, offset, pieces, carry, dtype):
    wide = pieces[0].shape[1]
    count = wide // TILE
    first = offset // TILE
    piece = pl.BlockSpec((TOK, TILE), lambda j: (0, j))
    whole = pl.BlockSpec((WIDTH, SEQ), lambda j: (0, 0))
    extra = [] if carry is None else [carry]
    return pl.pallas_call(
        functools.partial(heads_body, count, carry is not None),
        grid=(count,),
        in_specs=[pl.BlockSpec((WIDTH, TILE), lambda j: (0, j + first))]
        + [piece] * RANKS
        + [whole] * len(extra),
        out_specs=whole,
        out_shape=jax.ShapeDtypeStruct((WIDTH, SEQ), dtype),
        scratch_shapes=[pltpu.VMEM((WIDTH, SEQ), F32)],
        compiler_params=params(),
        cost_estimate=cost(2 * WIDTH * SEQ * wide, 2 * (WIDTH * SEQ + SEQ * wide + WIDTH * wide)),
        name="heads_grad",
    )(weights, *pieces, *extra)


def rank(x, c):
    return (x % XS) * CS + c


ONWARD = [(rank(x, c), rank(x + 1 - 2 * c, c)) for x in range(XS) for c in range(CS)]
SIBLING = [(rank(x, c), rank(x, 1 - c)) for x in range(XS) for c in range(CS)]


def gather_rows(own):
    seq = ("x", "c")
    send = lambda value, perm: lax.ppermute(value, seq, perm)
    near = send(own, ONWARD)
    sib = send(own, SIBLING)
    near_sib = send(sib, ONWARD)
    far = send(near, ONWARD)
    back = send(near, SIBLING)
    back_sib = send(near_sib, SIBLING)
    far_sib = send(far, SIBLING)
    return [own, sib, near, near_sib, back, back_sib, far, far_sib]


def slot_table():
    x, c = lax.axis_index("x"), lax.axis_index("c")
    step = 1 - 2 * c
    at = lambda xx, cc: lax.rem(xx + 2 * XS, XS) * CS + cc
    return jnp.stack(
        [
            at(x, c),
            at(x, 1 - c),
            at(x - step, c),
            at(x - step, 1 - c),
            at(x + step, 1 - c),
            at(x + step, c),
            at(x + 2, c),
            at(x + 2, 1 - c),
        ]
    ).astype(jnp.int32)


def exchange(value, axis):
    return lax.all_to_all(value, axis, split_axis=0, concat_axis=0, tiled=True)


def scatter_sum(term):
    wide = term.shape[1]
    got = exchange(term.reshape(YS, WIDTH // YS, wide), "y")
    part = jnp.sum(got.astype(F32), axis=0).astype(BF16)
    got = exchange(part.reshape(ZS, WIDTH // (YS * ZS), wide), "z")
    return jnp.sum(got.astype(F32), axis=0)


def local(queries, keys, values, cotangent, gate, w_out):
    slots = slot_table()
    cot = cotangent[0, 0]
    chunks = (2560, 2560)
    starts = (0, 2560)

    weights = lax.all_gather(w_out[0], ("y", "z"), axis=0, tiled=True)
    qkv = exchange(pack(queries[0, 0], keys[0, 0], values[0, 0]), ("x", "c"))
    pieces = []
    for start, wide in zip(starts, chunks):
        mine = cot[:, start : start + wide]
        other = lax.ppermute(mine, "b", [(0, 1)])
        total = mine.astype(F32) + other.astype(F32)
        grad_out = (gate[0, :, start : start + wide] * total).astype(BF16)
        pieces.append(gather_rows(grad_out))
    prob, att = forward(slots, qkv)
    grad_weight = [scatter_sum(weight_grad(att, p)) for p in pieces]
    acc = heads_grad(weights, starts[0], pieces[0], None, F32)
    gt = heads_grad(weights, starts[1], pieces[1], acc, BF16)
    home = [
        exchange(backward(slots, qkv, prob, gt, att, first, count), ("x", "c"))
        for first, count in ((0, 1), (1, 2))
    ]
    dq, dk, dv = unpack(*home)
    return (
        dq[None, None],
        dk[None, None],
        dv[None, None],
        jnp.concatenate(grad_weight, axis=1)[None],
    )


def solution(mesh):
    fine = Mesh(mesh.devices.reshape(2, XS, CS, YS, ZS), ("b", "x", "c", "y", "z"))
    tokens = P("b", ("y", "z"), ("x", "c"), None)
    weight = P("b", ("x", "c", "y", "z"), None)
    return jax.shard_map(
        local,
        mesh=fine,
        in_specs=(tokens, tokens, tokens, tokens, P("b", ("y", "z"), None), weight),
        out_specs=(tokens, tokens, tokens, weight),
        check_vma=False,
    )
```

profile of v0, /device:TPU:1, one launch (start us, length us, event | category | flops | bytes accessed | tf_op | source)
XLA Modules:
  0.0 274.5 jit_solution(3948121634964271032)
XLA Ops:
  7.2 0.0 all-gather.3.cloned.1.call-start
  7.2 2.2 fusion
  9.4 5.2 %collective-permute-start.8 = (bf16[128,2560]{1,0:T(8,128)(2,1)}, bf16[128,2560]{1,0:T(8,128)(2,1)}, u32[]{:S(2)}, u32[]{:S(2)}) collective-permute-start(bf16[128,2560]{1,0:T(8,128)(2,1)} %get-tuple-element.18), channel_id=1, source_target_pairs={{0,128},{1,129},{2,130},{3,131},{4,132},{5,133},{6,134},{7,135},{8... | collective-permute-start | bytes 1966088 | tf_op jit(solution)/shard_map/ppermute | solution.py:319
  14.6 2.1 collective-permute-start
  16.8 0.0 all-gather.3.cloned.1.call-update
  16.8 5.9 %pack.1 = bf16[8,3,128,384]{3,2,1,0:T(8,128)(2,1)} custom-call(bf16[128,3072]{1,0:T(8,128)(2,1)} %bitcast.28, bf16[128,3072]{1,0:T(8,128)(2,1)} %bitcast.29, bf16[128,3072]{1,0:T(8,128)(2,1)} %bitcast.30), custom_call_target="tpu_custom_call" | custom-call | bytes 4718592 | tf_op jit(solution)/shard_map/pack/pallas_call | solution.py:49
  22.7 5.4 %all-to-all-start = ((bf16[8,3,128,384]{3,2,1,0:T(8,128)(2,1)}), bf16[8,3,128,384]{3,2,1,0:T(8,128)(2,1)S(1)}, u32[]{:S(2)}, u32[]{:S(2)}) async-start(bf16[8,3,128,384]{3,2,1,0:T(8,128)(2,1)} %pack.1), calls=%async_computation | async-start | bytes 4718592 | tf_op jit(solution)/shard_map/all_to_all | solution.py:297
  28.1 0.1 slice_reduce_fusion
  28.2 20.8 %collective-permute-done = bf16[128,2560]{1,0:T(8,128)(2,1)} collective-permute-done((bf16[128,2560]{1,0:T(8,128)(2,1)S(1)}, bf16[128,2560]{1,0:T(8,128)(2,1)}, u32[]{:S(2)}, u32[]{:S(2)}) %collective-permute-start) | collective-permute-done | bytes 655392 | tf_op jit(solution)/shard_map/ppermute | solution.py:319
  49.0 2.9 %multiply_convert_fusion = (bf16[128,2560]{1,0:T(8,128)(2,1)}, bf16[128,2560]{1,0:T(8,128)(2,1)S(1)}) fusion(bf16[128,2560]{1,0:T(8,128)(2,1)} %collective-permute-done.8, f32[2560]{0:T(1024)S(1)} %get-tuple-element.14, bf16[128,5120]{1,0:T(8,128)(2,1)} %bitcast.27, bf16[128,2560]{1,0:T(8,128)(2,1)} %collective-permute-done, f32[2560]{0:T(1024)S(1)} %get-tuple-element.15), kind=kLoop, calls=%fused_computation | loop fusion | flops 3276800 | bytes 3952640 | tf_op jit(solution)/shard_map/convert_element_type | solution.py:321
  51.9 2.6 collective-permute-start.2
  54.5 0.7 collective-permute-start.1
  55.3 8.1 %collective-permute-done.2.refs_2_ = bf16[128,2560]{1,0:T(8,128)(2,1)} collective-permute-done((bf16[128,2560]{1,0:T(8,128)(2,1)S(1)}, bf16[128,2560]{1,0:T(8,128)(2,1)}, u32[]{:S(2)}, u32[]{:S(2)}) %collective-permute-start.2) | collective-permute-done | bytes 655392 | tf_op jit(solution)/shard_map/ppermute | solution.py:267
  63.3 2.3 collective-permute-start.6
  65.6 0.0 collective-permute-done.1.refs_1_
  65.6 0.9 copy-done.4
  66.5 0.4 collective-permute-start.3
  66.9 1.2 collective-permute-start.10
  68.1 1.4 collective-permute-start.9
  69.5 4.2 %collective-permute-done.6.refs_6_ = bf16[128,2560]{1,0:T(8,128)(2,1)} collective-permute-done((bf16[128,2560]{1,0:T(8,128)(2,1)}, bf16[128,2560]{1,0:T(8,128)(2,1)}, u32[]{:S(2)}, u32[]{:S(2)}) %collective-permute-start.6) | collective-permute-done | bytes 655392 | tf_op jit(solution)/shard_map/ppermute | solution.py:267
  73.7 4.1 %collective-permute-start.7 = (bf16[128,2560]{1,0:T(8,128)(2,1)}, bf16[128,2560]{1,0:T(8,128)(2,1)}, u32[]{:S(2)}, u32[]{:S(2)}) collective-permute-start(bf16[128,2560]{1,0:T(8,128)(2,1)} %collective-permute-done.6.refs_6_), channel_id=1, source_target_pairs={{0,16},{16,0},{32,48},{48,32},{64,80},{80,64},{96,112},{112,96},{1... | collective-permute-start | bytes 1966088 | tf_op jit(solution)/shard_map/ppermute | solution.py:267
  77.8 3.0 %collective-permute-done.3.refs_3_ = bf16[128,2560]{1,0:T(8,128)(2,1)} collective-permute-done((bf16[128,2560]{1,0:T(8,128)(2,1)S(1)}, bf16[128,2560]{1,0:T(8,128)(2,1)}, u32[]{:S(2)}, u32[]{:S(2)}) %collective-permute-start.3) | collective-permute-done | bytes 655392 | tf_op jit(solution)/shard_map/ppermute | solution.py:267
  80.7 4.1 %collective-permute-start.5 = (bf16[128,2560]{1,0:T(8,128)(2,1)}, bf16[128,2560]{1,0:T(8,128)(2,1)}, u32[]{:S(2)}, u32[]{:S(2)}) collective-permute-start(bf16[128,2560]{1,0:T(8,128)(2,1)} %collective-permute-done.3.refs_3_), channel_id=1, source_target_pairs={{0,16},{16,0},{32,48},{48,32},{64,80},{80,64},{96,112},{112,96},{1... | collective-permute-start | bytes 1966088 | tf_op jit(solution)/shard_map/ppermute | solution.py:267
  84.8 0.7 stack.35.slot_ref
  85.5 2.3 collective-permute-done.10.refs_2_
  87.8 3.1 %collective-permute-start.14 = (bf16[128,2560]{1,0:T(8,128)(2,1)}, bf16[128,2560]{1,0:T(8,128)(2,1)}, u32[]{:S(2)}, u32[]{:S(2)}) collective-permute-start(bf16[128,2560]{1,0:T(8,128)(2,1)} %collective-permute-done.10.refs_2_), channel_id=1, source_target_pairs={{0,32},{16,112},{32,64},{48,16},{64,96},{80,48},{96,0},{112,80},{1... | collective-permute-start | bytes 1966088 | tf_op jit(solution)/shard_map/ppermute | solution.py:267
  90.9 0.0 collective-permute-start.11
  90.9 1.4 copy-done
  92.4 14.4 %forward.1 = (bf16[3,1024,1024]{2,1,0:T(8,128)(2,1)}, bf16[384,1024]{1,0:T(8,128)(2,1)}) custom-call(s32[8]{0:T(128)} %stack.35.slot_ref, bf16[8,3,128,384]{3,2,1,0:T(8,128)(2,1)} %copy-done), custom_call_target="tpu_custom_call" | custom-call | flops 1610612736 | bytes 9437184 | tf_op jit(solution)/shard_map/forward/pallas_call | solution.py:108
  106.7 0.0 collective-permute-done.7.refs_7_
  106.7 0.0 collective-permute-done.5.refs_5_
  106.8 7.1 %weight_grad.3 = bf16[384,2560]{1,0:T(8,128)(2,1)} custom-call(bf16[384,1024]{1,0:T(8,128)(2,1)} %get-tuple-element.10.att_ref, bf16[128,2560]{1,0:T(8,128)(2,1)} %copy-done.2, bf16[128,2560]{1,0:T(8,128)(2,1)} %copy-done.4, bf16[128,2560]{1,0:T(8,128)(2,1)} %collective-permute-done.2.refs_2_, bf16[128,2560]{1,0:T(8,128)(2,1)} %collective-permute-done.3.refs_3_, ...), custom_call_target="tpu_custom_call" | custom-call | flops 2013265920 | bytes 7995392 | tf_op jit(solution)/shard_map/weight_grad/pallas_call | solution.py:206
  113.9 4.4 %all-to-all-start.5 = ((bf16[4,96,2560]{2,1,0:T(8,128)(2,1)}), bf16[4,96,2560]{2,1,0:T(8,128)(2,1)S(1)}, u32[]{:S(2)}, u32[]{:S(2)}) async-start(bf16[4,96,2560]{2,1,0:T(8,128)(2,1)} %bitcast.24), calls=%async_computation.5 | async-start | bytes 3932160 | tf_op jit(solution)/shard_map/all_to_all | solution.py:297
  118.3 1.5 collective-permute-start.12
  119.8 0.1 collective-permute-start.15
  119.9 0.0 collective-permute-done.11.refs_3_
  119.9 0.4 collective-permute-start.13
  120.3 1.4 collective-permute-done.12.refs_4_
  121.7 0.9 collective-permute-done.15.refs_7_
  122.7 0.9 collective-permute-done.13.refs_5_
  123.6 0.9 copy-done.7
  124.5 7.1 %weight_grad.2 = bf16[384,2560]{1,0:T(8,128)(2,1)} custom-call(bf16[384,1024]{1,0:T(8,128)(2,1)} %get-tuple-element.10.att_ref, bf16[128,2560]{1,0:T(8,128)(2,1)} %get-tuple-element.16.refs_0_, bf16[128,2560]{1,0:T(8,128)(2,1)} %collective-permute-done.9.refs_1_, bf16[128,2560]{1,0:T(8,128)(2,1)} %collective-permute-done.10.refs_2_, ...), custom_call_target="tpu_custom_call" | custom-call | flops 2013265920 | bytes 7995392 | tf_op jit(solution)/shard_map/weight_grad/pallas_call | solution.py:206
  131.6 10.1 %all-to-all-done.5 = bf16[4,96,2560]{2,1,0:T(8,128)(2,1)S(1)} async-done(((bf16[4,96,2560]{2,1,0:T(8,128)(2,1)}), bf16[4,96,2560]{2,1,0:T(8,128)(2,1)S(1)}, u32[]{:S(2)}, u32[]{:S(2)}) %all-to-all-start.5) | async-done | bytes 1966112 | tf_op jit(solution)/shard_map/all_to_all | solution.py:297
  141.7 4.6 %all-to-all-start.3 = ((bf16[4,96,2560]{2,1,0:T(8,128)(2,1)}), bf16[4,96,2560]{2,1,0:T(8,128)(2,1)}, u32[]{:S(2)}, u32[]{:S(2)}) async-start(bf16[4,96,2560]{2,1,0:T(8,128)(2,1)} %bitcast.25), calls=%async_computation.3 | async-start | bytes 3932160 | tf_op jit(solution)/shard_map/all_to_all | solution.py:297
  146.4 1.2 reduce_sum.44
  147.6 21.2 %all-to-all-done.3 = bf16[4,96,2560]{2,1,0:T(8,128)(2,1)} async-done(((bf16[4,96,2560]{2,1,0:T(8,128)(2,1)}), bf16[4,96,2560]{2,1,0:T(8,128)(2,1)}, u32[]{:S(2)}, u32[]{:S(2)}) %all-to-all-start.3) | async-done | bytes 1966112 | tf_op jit(solution)/shard_map/all_to_all | solution.py:297
  168.8 7.8 %all-to-all-start.6 = ((bf16[4,24,2560]{2,1,0:T(8,128)(2,1)}), bf16[4,24,2560]{2,1,0:T(8,128)(2,1)S(1)}, u32[]{:S(2)}, u32[]{:S(2)}) async-start(bf16[4,24,2560]{2,1,0:T(8,128)(2,1)} %bitcast.19), calls=%async_computation.6 | async-start | bytes 983040 | tf_op jit(solution)/shard_map/all_to_all | solution.py:297
  176.5 2.8 %reduce_sum.42 = bf16[96,2560]{1,0:T(8,128)(2,1)} reduce(bf16[4,96,2560]{2,1,0:T(8,128)(2,1)} %all-to-all-done.3, bf16[]{:T(256)} %constant.34.clone.1), dimensions={0}, to_apply=%region_0.0 | reduce | flops 737280 | bytes 2457602 | tf_op jit(solution)/shard_map/reduce_sum | solution.py:303
  179.3 7.7 %all-to-all-done.6 = bf16[4,24,2560]{2,1,0:T(8,128)(2,1)S(1)} async-done(((bf16[4,24,2560]{2,1,0:T(8,128)(2,1)}), bf16[4,24,2560]{2,1,0:T(8,128)(2,1)S(1)}, u32[]{:S(2)}, u32[]{:S(2)}) %all-to-all-start.6) | async-done | bytes 491552 | tf_op jit(solution)/shard_map/all_to_all | solution.py:297
  187.0 4.3 %all-to-all-start.4 = ((bf16[4,24,2560]{2,1,0:T(8,128)(2,1)}), bf16[4,24,2560]{2,1,0:T(8,128)(2,1)S(1)}, u32[]{:S(2)}, u32[]{:S(2)}) async-start(bf16[4,24,2560]{2,1,0:T(8,128)(2,1)} %bitcast.17), calls=%async_computation.4 | async-start | bytes 983040 | tf_op jit(solution)/shard_map/all_to_all | solution.py:297
  191.3 7.4 %heads_grad.2.refs_8_ = f32[384,1024]{1,0:T(8,128)} custom-call(bf16[384,5120]{1,0:T(8,128)(2,1)} %bitcast.22, bf16[128,2560]{1,0:T(8,128)(2,1)} %get-tuple-element.16.refs_0_, bf16[128,2560]{1,0:T(8,128)(2,1)} %collective-permute-done.9.refs_1_, bf16[128,2560]{1,0:T(8,128)(2,1)} %collective-permute-done.10.refs_2_, ...), custom_call_target="tpu_custom_call" | custom-call | flops 2013265920 | bytes 7995392 | tf_op jit(solution)/shard_map/heads_grad/pallas_call | solution.py:242
  198.7 7.8 %heads_grad.3.gt_ref = bf16[384,1024]{1,0:T(8,128)(2,1)} custom-call(bf16[384,5120]{1,0:T(8,128)(2,1)} %bitcast.23, bf16[128,2560]{1,0:T(8,128)(2,1)} %copy-done.2, bf16[128,2560]{1,0:T(8,128)(2,1)} %copy-done.4, bf16[128,2560]{1,0:T(8,128)(2,1)} %collective-permute-done.2.refs_2_, bf16[128,2560]{1,0:T(8,128)(2,1)} %collective-permute-done.3.refs_3_, ...), custom_call_target="tpu_custom_call" | custom-call | flops 2013265920 | bytes 7995392 | tf_op jit(solution)/shard_map/heads_grad/pallas_call | solution.py:242
  206.5 6.5 %backward.2 = bf16[8,3,128,128]{3,2,1,0:T(8,128)(2,1)} custom-call(s32[8]{0:T(128)} %stack.35.slot_ref, bf16[8,3,128,384]{3,2,1,0:T(8,128)(2,1)} %copy-done, bf16[3,1024,1024]{2,1,0:T(8,128)(2,1)} %get-tuple-element.9.prob_ref, bf16[384,1024]{1,0:T(8,128)(2,1)} %heads_grad.3.gt_ref, bf16[384,1024]{1,0:T(8,128)(2,1)} %get-tuple-element.10.att_ref), custom_call_target="tpu_custom_call" | custom-call | flops 1073741824 | bytes 4194304 | tf_op jit(solution)/shard_map/backward/pallas_call | solution.py:170
  212.9 9.3 %all-to-all-start.1 = ((bf16[8,3,128,128]{3,2,1,0:T(8,128)(2,1)}), bf16[8,3,128,128]{3,2,1,0:T(8,128)(2,1)S(1)}, u32[]{:S(2)}, u32[]{:S(2)}) async-start(bf16[8,3,128,128]{3,2,1,0:T(8,128)(2,1)} %backward.2), calls=%async_computation.1 | async-start | bytes 1572864 | tf_op jit(solution)/shard_map/all_to_all | solution.py:297
  222.3 10.5 %backward.3 = bf16[8,3,128,256]{3,2,1,0:T(8,128)(2,1)} custom-call(s32[8]{0:T(128)} %stack.35.slot_ref, bf16[8,3,128,384]{3,2,1,0:T(8,128)(2,1)} %copy-done, bf16[3,1024,1024]{2,1,0:T(8,128)(2,1)} %get-tuple-element.9.prob_ref, bf16[384,1024]{1,0:T(8,128)(2,1)} %heads_grad.3.gt_ref, bf16[384,1024]{1,0:T(8,128)(2,1)} %get-tuple-element.10.att_ref), custom_call_target="tpu_custom_call" | custom-call | flops 2147483648 | bytes 8388608 | tf_op jit(solution)/shard_map/backward/pallas_call | solution.py:170
  232.8 1.8 all-to-all-done.1.a_ref
  234.6 0.9 copy-done.3
  235.5 4.4 %all-to-all-start.2 = ((bf16[8,3,128,256]{3,2,1,0:T(8,128)(2,1)}), bf16[8,3,128,256]{3,2,1,0:T(8,128)(2,1)S(1)}, u32[]{:S(2)}, u32[]{:S(2)}) async-start(bf16[8,3,128,256]{3,2,1,0:T(8,128)(2,1)} %backward.3), calls=%async_computation.2 | async-start | bytes 3145728 | tf_op jit(solution)/shard_map/all_to_all | solution.py:297
  239.8 0.1 convert_reduce_fusion
  239.9 0.1 convert_reduce_fusion.1
  240.0 0.8 maximum_bitcast_fusion
  240.8 19.8 %all-to-all-done.2.b_ref = bf16[8,3,128,256]{3,2,1,0:T(8,128)(2,1)S(1)} async-done(((bf16[8,3,128,256]{3,2,1,0:T(8,128)(2,1)}), bf16[8,3,128,256]{3,2,1,0:T(8,128)(2,1)S(1)}, u32[]{:S(2)}, u32[]{:S(2)}) %all-to-all-start.2) | async-done | bytes 1572896 | tf_op jit(solution)/shard_map/all_to_all | solution.py:297
  260.6 1.2 copy-done.1
  261.7 5.9 %unpack.1 = (bf16[128,3072]{1,0:T(8,128)(2,1)}, bf16[128,3072]{1,0:T(8,128)(2,1)}, bf16[128,3072]{1,0:T(8,128)(2,1)}) custom-call(bf16[8,3,128,128]{3,2,1,0:T(8,128)(2,1)} %copy-done.3, bf16[8,3,128,256]{3,2,1,0:T(8,128)(2,1)} %copy-done.1), custom_call_target="tpu_custom_call" | custom-call | bytes 4718592 | tf_op jit(solution)/shard_map/unpack/pallas_call | solution.py:73
  (21 shorter events, 0.0 us)
Async XLA Ops:
  7.2 184.1 %all-gather.3.cloned.1.call-start = ((), (), s32[]{:S(2)}) async-start(), calls=%async_computation.7 | async-start | bytes 4177920 | tf_op jit(solution)/shard_map/all_gather | solution.py:314
  9.4 18.8 %collective-permute-start.8 = (bf16[128,2560]{1,0:T(8,128)(2,1)}, bf16[128,2560]{1,0:T(8,128)(2,1)}, u32[]{:S(2)}, u32[]{:S(2)}) collective-permute-start(bf16[128,2560]{1,0:T(8,128)(2,1)} %get-tuple-element.18), channel_id=1, source_target_pairs={{0,128},{1,129},{2,130},{3,131},{4,132},{5,133},{6,134},{7,135},{8... | collective-permute-start | bytes 1966088 | tf_op jit(solution)/shard_map/ppermute | solution.py:319
  14.6 34.4 %collective-permute-start = (bf16[128,2560]{1,0:T(8,128)(2,1)S(1)}, bf16[128,2560]{1,0:T(8,128)(2,1)}, u32[]{:S(2)}, u32[]{:S(2)}) collective-permute-start(bf16[128,2560]{1,0:T(8,128)(2,1)S(1)} %get-tuple-element.19), channel_id=1, source_target_pairs={{0,128},{1,129},{2,130},{3,131},{4,132},{5,133},{6,134},{7,135},{8... | collective-permute-start | bytes 1966088 | tf_op jit(solution)/shard_map/ppermute | solution.py:319
  22.7 5.4 %copy-start.8 = (f32[1,1,5120]{2,1,0:T(1,128)S(1)}, f32[1,1,5120]{2,1,0:T(1,128)}, u32[]{:S(2)}) copy-start(f32[1,1,5120]{2,1,0:T(1,128)} %param.10) | copy-start | bytes 61444
  22.7 68.2 %all-to-all-start = ((bf16[8,3,128,384]{3,2,1,0:T(8,128)(2,1)}), bf16[8,3,128,384]{3,2,1,0:T(8,128)(2,1)S(1)}, u32[]{:S(2)}, u32[]{:S(2)}) async-start(bf16[8,3,128,384]{3,2,1,0:T(8,128)(2,1)} %pack.1), calls=%async_computation | async-start | bytes 4718592 | tf_op jit(solution)/shard_map/all_to_all | solution.py:297
  51.9 54.9 %copy-start.2 = (bf16[128,2560]{1,0:T(8,128)(2,1)}, bf16[128,2560]{1,0:T(8,128)(2,1)S(1)}, u32[]{:S(2)}) copy-start(bf16[128,2560]{1,0:T(8,128)(2,1)S(1)} %get-tuple-element.17.refs_0_) | copy-start | bytes 1966084
  51.9 11.5 %collective-permute-start.2 = (bf16[128,2560]{1,0:T(8,128)(2,1)S(1)}, bf16[128,2560]{1,0:T(8,128)(2,1)}, u32[]{:S(2)}, u32[]{:S(2)}) collective-permute-start(bf16[128,2560]{1,0:T(8,128)(2,1)S(1)} %get-tuple-element.17.refs_0_), channel_id=1, source_target_pairs={{0,32},{16,112},{32,64},{48,16},{64,96},{80,48},{96,0},{112,80},{1... | collective-permute-start | bytes 1966088 | tf_op jit(solution)/shard_map/ppermute | solution.py:267
  54.5 11.1 %collective-permute-start.1 = (bf16[128,2560]{1,0:T(8,128)(2,1)S(1)}, bf16[128,2560]{1,0:T(8,128)(2,1)S(1)}, u32[]{:S(2)}, u32[]{:S(2)}) collective-permute-start(bf16[128,2560]{1,0:T(8,128)(2,1)S(1)} %get-tuple-element.17.refs_0_), channel_id=1, source_target_pairs={{0,16},{16,0},{32,48},{48,32},{64,80},{80,64},{96,112},{112,96},{1... | collective-permute-start | bytes 1966088 | tf_op jit(solution)/shard_map/ppermute | solution.py:267
  63.3 10.4 %collective-permute-start.6 = (bf16[128,2560]{1,0:T(8,128)(2,1)}, bf16[128,2560]{1,0:T(8,128)(2,1)}, u32[]{:S(2)}, u32[]{:S(2)}) collective-permute-start(bf16[128,2560]{1,0:T(8,128)(2,1)} %collective-permute-done.2.refs_2_), channel_id=1, source_target_pairs={{0,32},{16,112},{32,64},{48,16},{64,96},{80,48},{96,0},{112,80},{1... | collective-permute-start | bytes 1966088 | tf_op jit(solution)/shard_map/ppermute | solution.py:267
  65.6 0.9 copy-start.4
  66.5 14.3 %collective-permute-start.3 = (bf16[128,2560]{1,0:T(8,128)(2,1)S(1)}, bf16[128,2560]{1,0:T(8,128)(2,1)}, u32[]{:S(2)}, u32[]{:S(2)}) collective-permute-start(bf16[128,2560]{1,0:T(8,128)(2,1)S(1)} %collective-permute-done.1.refs_1_), channel_id=1, source_target_pairs={{0,32},{16,112},{32,64},{48,16},{64,96},{80,48},{96,0},{112,80},{1... | collective-permute-start | bytes 1966088 | tf_op jit(solution)/shard_map/ppermute | solution.py:267
  66.9 20.9 %collective-permute-start.10 = (bf16[128,2560]{1,0:T(8,128)(2,1)}, bf16[128,2560]{1,0:T(8,128)(2,1)}, u32[]{:S(2)}, u32[]{:S(2)}) collective-permute-start(bf16[128,2560]{1,0:T(8,128)(2,1)} %get-tuple-element.16.refs_0_), channel_id=1, source_target_pairs={{0,32},{16,112},{32,64},{48,16},{64,96},{80,48},{96,0},{112,80},{1... | collective-permute-start | bytes 1966088 | tf_op jit(solution)/shard_map/ppermute | solution.py:267
  68.1 22.8 %collective-permute-start.9 = (bf16[128,2560]{1,0:T(8,128)(2,1)}, bf16[128,2560]{1,0:T(8,128)(2,1)}, u32[]{:S(2)}, u32[]{:S(2)}) collective-permute-start(bf16[128,2560]{1,0:T(8,128)(2,1)} %get-tuple-element.16.refs_0_), channel_id=1, source_target_pairs={{0,16},{16,0},{32,48},{48,32},{64,80},{80,64},{96,112},{112,96},{1... | collective-permute-start | bytes 1966088 | tf_op jit(solution)/shard_map/ppermute | solution.py:267
  69.5 37.2 %collective-permute-start.4 = (bf16[128,2560]{1,0:T(8,128)(2,1)}, bf16[128,2560]{1,0:T(8,128)(2,1)}, u32[]{:S(2)}, u32[]{:S(2)}) collective-permute-start(bf16[128,2560]{1,0:T(8,128)(2,1)} %collective-permute-done.2.refs_2_), channel_id=1, source_target_pairs={{0,16},{16,0},{32,48},{48,32},{64,80},{80,64},{96,112},{112,96},{1... | collective-permute-start | bytes 1966088 | tf_op jit(solution)/shard_map/ppermute | solution.py:267
  73.7 33.0 %collective-permute-start.7 = (bf16[128,2560]{1,0:T(8,128)(2,1)}, bf16[128,2560]{1,0:T(8,128)(2,1)}, u32[]{:S(2)}, u32[]{:S(2)}) collective-permute-start(bf16[128,2560]{1,0:T(8,128)(2,1)} %collective-permute-done.6.refs_6_), channel_id=1, source_target_pairs={{0,16},{16,0},{32,48},{48,32},{64,80},{80,64},{96,112},{112,96},{1... | collective-permute-start | bytes 1966088 | tf_op jit(solution)/shard_map/ppermute | solution.py:267
  80.7 26.0 %collective-permute-start.5 = (bf16[128,2560]{1,0:T(8,128)(2,1)}, bf16[128,2560]{1,0:T(8,128)(2,1)}, u32[]{:S(2)}, u32[]{:S(2)}) collective-permute-start(bf16[128,2560]{1,0:T(8,128)(2,1)} %collective-permute-done.3.refs_3_), channel_id=1, source_target_pairs={{0,16},{16,0},{32,48},{48,32},{64,80},{80,64},{96,112},{112,96},{1... | collective-permute-start | bytes 1966088 | tf_op jit(solution)/shard_map/ppermute | solution.py:267
  87.8 32.0 %collective-permute-start.14 = (bf16[128,2560]{1,0:T(8,128)(2,1)}, bf16[128,2560]{1,0:T(8,128)(2,1)}, u32[]{:S(2)}, u32[]{:S(2)}) collective-permute-start(bf16[128,2560]{1,0:T(8,128)(2,1)} %collective-permute-done.10.refs_2_), channel_id=1, source_target_pairs={{0,32},{16,112},{32,64},{48,16},{64,96},{80,48},{96,0},{112,80},{1... | collective-permute-start | bytes 1966088 | tf_op jit(solution)/shard_map/ppermute | solution.py:267
  90.9 29.0 %collective-permute-start.11 = (bf16[128,2560]{1,0:T(8,128)(2,1)}, bf16[128,2560]{1,0:T(8,128)(2,1)}, u32[]{:S(2)}, u32[]{:S(2)}) collective-permute-start(bf16[128,2560]{1,0:T(8,128)(2,1)} %collective-permute-done.9.refs_1_), channel_id=1, source_target_pairs={{0,32},{16,112},{32,64},{48,16},{64,96},{80,48},{96,0},{112,80},{1... | collective-permute-start | bytes 1966088 | tf_op jit(solution)/shard_map/ppermute | solution.py:267
  90.9 1.4 copy-start
  113.9 27.9 %all-to-all-start.5 = ((bf16[4,96,2560]{2,1,0:T(8,128)(2,1)}), bf16[4,96,2560]{2,1,0:T(8,128)(2,1)S(1)}, u32[]{:S(2)}, u32[]{:S(2)}) async-start(bf16[4,96,2560]{2,1,0:T(8,128)(2,1)} %bitcast.24), calls=%async_computation.5 | async-start | bytes 3932160 | tf_op jit(solution)/shard_map/all_to_all | solution.py:297
  118.3 3.4 %collective-permute-start.12 = (bf16[128,2560]{1,0:T(8,128)(2,1)}, bf16[128,2560]{1,0:T(8,128)(2,1)S(1)}, u32[]{:S(2)}, u32[]{:S(2)}) collective-permute-start(bf16[128,2560]{1,0:T(8,128)(2,1)} %collective-permute-done.10.refs_2_), channel_id=1, source_target_pairs={{0,16},{16,0},{32,48},{48,32},{64,80},{80,64},{96,112},{112,96},{1... | collective-permute-start | bytes 1966088 | tf_op jit(solution)/shard_map/ppermute | solution.py:267
  119.8 2.9 %collective-permute-start.15 = (bf16[128,2560]{1,0:T(8,128)(2,1)}, bf16[128,2560]{1,0:T(8,128)(2,1)S(1)}, u32[]{:S(2)}, u32[]{:S(2)}) collective-permute-start(bf16[128,2560]{1,0:T(8,128)(2,1)} %collective-permute-done.14.refs_6_), channel_id=1, source_target_pairs={{0,16},{16,0},{32,48},{48,32},{64,80},{80,64},{96,112},{112,96},{1... | collective-permute-start | bytes 1966088 | tf_op jit(solution)/shard_map/ppermute | solution.py:267
  119.9 3.7 %collective-permute-start.13 = (bf16[128,2560]{1,0:T(8,128)(2,1)}, bf16[128,2560]{1,0:T(8,128)(2,1)S(1)}, u32[]{:S(2)}, u32[]{:S(2)}) collective-permute-start(bf16[128,2560]{1,0:T(8,128)(2,1)} %collective-permute-done.11.refs_3_), channel_id=1, source_target_pairs={{0,16},{16,0},{32,48},{48,32},{64,80},{80,64},{96,112},{112,96},{1... | collective-permute-start | bytes 1966088 | tf_op jit(solution)/shard_map/ppermute | solution.py:267
  121.7 1.9 copy-start.5
  122.7 0.9 copy-start.6
  123.6 0.9 copy-start.7
  141.7 27.1 %all-to-all-start.3 = ((bf16[4,96,2560]{2,1,0:T(8,128)(2,1)}), bf16[4,96,2560]{2,1,0:T(8,128)(2,1)}, u32[]{:S(2)}, u32[]{:S(2)}) async-start(bf16[4,96,2560]{2,1,0:T(8,128)(2,1)} %bitcast.25), calls=%async_computation.3 | async-start | bytes 3932160 | tf_op jit(solution)/shard_map/all_to_all | solution.py:297
  168.8 18.2 %all-to-all-start.6 = ((bf16[4,24,2560]{2,1,0:T(8,128)(2,1)}), bf16[4,24,2560]{2,1,0:T(8,128)(2,1)S(1)}, u32[]{:S(2)}, u32[]{:S(2)}) async-start(bf16[4,24,2560]{2,1,0:T(8,128)(2,1)} %bitcast.19), calls=%async_computation.6 | async-start | bytes 983040 | tf_op jit(solution)/shard_map/all_to_all | solution.py:297
  187.0 26.0 %all-to-all-start.4 = ((bf16[4,24,2560]{2,1,0:T(8,128)(2,1)}), bf16[4,24,2560]{2,1,0:T(8,128)(2,1)S(1)}, u32[]{:S(2)}, u32[]{:S(2)}) async-start(bf16[4,24,2560]{2,1,0:T(8,128)(2,1)} %bitcast.17), calls=%async_computation.4 | async-start | bytes 983040 | tf_op jit(solution)/shard_map/all_to_all | solution.py:297
  212.9 21.6 %all-to-all-start.1 = ((bf16[8,3,128,128]{3,2,1,0:T(8,128)(2,1)}), bf16[8,3,128,128]{3,2,1,0:T(8,128)(2,1)S(1)}, u32[]{:S(2)}, u32[]{:S(2)}) async-start(bf16[8,3,128,128]{3,2,1,0:T(8,128)(2,1)} %backward.2), calls=%async_computation.1 | async-start | bytes 1572864 | tf_op jit(solution)/shard_map/all_to_all | solution.py:297
  234.6 0.9 copy-start.3
  235.5 25.1 %all-to-all-start.2 = ((bf16[8,3,128,256]{3,2,1,0:T(8,128)(2,1)}), bf16[8,3,128,256]{3,2,1,0:T(8,128)(2,1)S(1)}, u32[]{:S(2)}, u32[]{:S(2)}) async-start(bf16[8,3,128,256]{3,2,1,0:T(8,128)(2,1)} %backward.3), calls=%async_computation.2 | async-start | bytes 3145728 | tf_op jit(solution)/shard_map/all_to_all | solution.py:297
  260.6 1.2 copy-start.1
Sparse Core Ops, SparseCore 0:
  16.9 77.1 all-gather.2
where the time goes:
time: 276 us; the launch traced here: 274 us
  waiting for transfers between devices  102 us (37%)
  Pallas kernels  72.5 us (26%)
  starting transfers between devices  69.5 us (25%)
  between operations  14.1 us (5%)
  local copies, waits for them, and re-layouts  8.2 us (3%)
  other arithmetic  7.79 us (3%)
    all_to_all x7, waiting for transfers between devices, exchange(): return lax.all_to_all(value, axis, split_axis=0, concat_axis=0, tiled=True)  60.6 us
    all_to_all x7, starting transfers between devices, exchange(): return lax.all_to_all(value, axis, split_axis=0, concat_axis=0, tiled=True)  40.2 us
    ppermute x14, starting transfers between devices, gather_rows(): send = lambda value, perm: lax.ppermute(value, seq, perm)  22 us
    ppermute x14, waiting for transfers between devices, gather_rows(): send = lambda value, perm: lax.ppermute(value, seq, perm)  20.9 us
    ppermute x2, waiting for transfers between devices, local(): other = lax.ppermute(mine, 'b', [(0, 1)])  20.8 us
    pallas_call x2, Pallas kernels, backward(): pl.pallas_call(backward_body, grid_spec=pltpu.PrefetchScalarGridSpec(num_...  17 us
    pallas_call x2, Pallas kernels, heads_grad(): pl.pallas_call(functools.partial(heads_body, count, carry is not None), g...  15.2 us
    pallas_call x1, Pallas kernels, forward(): pl.pallas_call(forward_body, grid_spec=pltpu.PrefetchScalarGridSpec(num_s...  14.4 us
  transfers between devices with their start and end apart: 24, of which 13 were waited for; matrix products, arithmetic and copies ran while one was open for 3% of the time, Pallas kernels for 24%

commit v1 on v0

v1 whole, which is shorter than its diff:
```python
import functools

import jax
import jax.numpy as jnp
from jax import lax
from jax.experimental import pallas as pl
from jax.experimental.pallas import tpu as pltpu
from jax.sharding import Mesh, PartitionSpec as P

HD = 128
XS, CS, YS, ZS = 4, 2, 4, 4
RANKS = XS * CS
TOK = 128
SEQ = RANKS * TOK
NH = 3
WIDTH = NH * HD
D = 5120
QB = 256
TILE = 512
SCALE = HD**-0.5
LOG2E = 1.4426950408889634
F32 = jnp.float32
BF16 = jnp.bfloat16
NT = (((1,), (1,)), ((), ()))
NN = (((1,), (0,)), ((), ()))
CHUNKS = (2560, 2560)
STARTS = tuple(sum(CHUNKS[:i]) for i in range(len(CHUNKS)))
GROUPS = ((0, 1), (1, 2))
VMEM_LIMIT = 56 * 1024 * 1024


def dot(a, b, dims=NN):
    return lax.dot_general(a, b, dims, preferred_element_type=F32)


def params(**more):
    return pltpu.CompilerParams(vmem_limit_bytes=VMEM_LIMIT, **more)


def cost(flops, nbytes, trans=0):
    return pl.CostEstimate(flops=flops, bytes_accessed=nbytes, transcendentals=trans)


def hbm(count):
    return [pl.BlockSpec(memory_space=pl.ANY)] * count


def pack_body(col_ref, q_ref, k_ref, v_ref, *out_refs):
    for s, out in enumerate(out_refs):
        cols = pl.ds(pl.multiple_of(col_ref[s] * WIDTH, WIDTH), WIDTH)
        for i, ref in enumerate((q_ref, k_ref, v_ref)):
            out[i] = ref[:, cols]


def pack(targets, q, k, v):
    whole = pl.BlockSpec((TOK, RANKS * WIDTH), lambda j, s: (0, 0))
    return pl.pallas_call(
        pack_body,
        grid_spec=pltpu.PrefetchScalarGridSpec(
            num_scalar_prefetch=1,
            grid=(1,),
            in_specs=[whole] * 3,
            out_specs=[pl.BlockSpec((3, TOK, WIDTH), lambda j, s: (0, 0, 0))] * RANKS,
        ),
        out_shape=[jax.ShapeDtypeStruct((3, TOK, WIDTH), BF16)] * RANKS,
        compiler_params=params(),
        cost_estimate=cost(0, 2 * 3 * 2 * SEQ * WIDTH),
        name="pack",
    )(targets, q, k, v)


def unpack_body(widths, col_ref, *refs):
    outs = refs[-3:]
    for s in range(RANKS):
        base = pl.multiple_of(col_ref[s] * WIDTH, WIDTH)
        at = 0
        for g, wide in enumerate(widths):
            cols = pl.ds(pl.multiple_of(base + at, HD), wide)
            for i, out in enumerate(outs):
                out[:, cols] = refs[g * RANKS + s][i]
            at += wide


def unpack(targets, groups):
    widths = tuple(g[0].shape[-1] for g in groups)
    pieces = [p for g in groups for p in g]
    whole = pl.BlockSpec((TOK, RANKS * WIDTH), lambda j, s: (0, 0))
    return pl.pallas_call(
        functools.partial(unpack_body, widths),
        grid_spec=pltpu.PrefetchScalarGridSpec(
            num_scalar_prefetch=1,
            grid=(1,),
            in_specs=[pl.BlockSpec(p.shape, lambda j, s: (0, 0, 0)) for p in pieces],
            out_specs=[whole] * 3,
        ),
        out_shape=[jax.ShapeDtypeStruct((TOK, RANKS * WIDTH), BF16)] * 3,
        compiler_params=params(),
        cost_estimate=cost(0, 2 * 3 * 2 * SEQ * WIDTH),
        name="unpack",
    )(targets, *pieces)


def gate_body(gate_ref, mine_ref, other_ref, out_ref):
    total = mine_ref[...].astype(F32) + other_ref[...].astype(F32)
    out_ref[...] = (gate_ref[...] * total).astype(BF16)


def gated(gate, cot, other, start):
    wide = other.shape[1]
    at = start // TILE
    return pl.pallas_call(
        gate_body,
        grid=(wide // TILE,),
        in_specs=[
            pl.BlockSpec((1, TILE), lambda j: (0, j + at)),
            pl.BlockSpec((TOK, TILE), lambda j: (0, j + at)),
            pl.BlockSpec((TOK, TILE), lambda j: (0, j)),
        ],
        out_specs=pl.BlockSpec((TOK, TILE), lambda j: (0, j)),
        out_shape=jax.ShapeDtypeStruct((TOK, wide), BF16),
        compiler_params=params(),
        cost_estimate=cost(2 * TOK * wide, 6 * TOK * wide),
        name="gated",
    )(gate, cot, other)


def forward_body(*refs):
    pieces = refs[:RANKS]
    prob_ref, att_ref, q_s, k_s, vt_s = refs[-5:]
    block = pl.program_id(1)

    @pl.when(block == 0)
    def _():
        for s, piece in enumerate(pieces):
            rows = pl.ds(s * TOK, TOK)
            q_s[rows, :] = piece[0]
            k_s[rows, :] = piece[1]
            vt_s[:, rows] = piece[2].astype(F32).T.astype(BF16)

    q = q_s[pl.ds(pl.multiple_of(block * QB, QB), QB), :]
    scores = dot(k_s[...], q, NT)
    top = jnp.max(scores, axis=0, keepdims=True)
    e = jnp.exp2((scores - top) * (SCALE * LOG2E))
    norm = 1.0 / jnp.sum(e, axis=0, keepdims=True)
    prob = (e * norm).astype(BF16)
    prob_ref[0] = prob
    att_ref[...] = dot(vt_s[...], prob).astype(BF16)


def forward(qkv, after=()):
    return pl.pallas_call(
        forward_body,
        grid=(NH, SEQ // QB),
        in_specs=[pl.BlockSpec((3, TOK, HD), lambda h, b: (0, 0, h))] * RANKS + hbm(len(after)),
        out_specs=[
            pl.BlockSpec((1, SEQ, QB), lambda h, b: (h, 0, b)),
            pl.BlockSpec((HD, QB), lambda h, b: (h, b)),
        ],
        scratch_shapes=[
            pltpu.VMEM((SEQ, HD), BF16),
            pltpu.VMEM((SEQ, HD), BF16),
            pltpu.VMEM((HD, SEQ), BF16),
        ],
        out_shape=[
            jax.ShapeDtypeStruct((NH, SEQ, SEQ), BF16),
            jax.ShapeDtypeStruct((WIDTH, SEQ), BF16),
        ],
        compiler_params=params(),
        cost_estimate=cost(4 * NH * SEQ * SEQ * HD, 2 * NH * SEQ * SEQ + 8 * SEQ * WIDTH, NH * SEQ * SEQ),
        name="forward",
    )(*qkv, *after)


def backward_body(*refs):
    pieces = refs[:RANKS]
    prob_ref, gt_ref, att_ref = refs[RANKS : RANKS + 3]
    outs = refs[-5 - RANKS : -5]
    q_s, v_s, kt_s, dk_s, dv_s = refs[-5:]
    block = pl.program_id(1)
    last = pl.num_programs(1) - 1

    @pl.when(block == 0)
    def _():
        for s, piece in enumerate(pieces):
            rows = pl.ds(s * TOK, TOK)
            q_s[rows, :] = piece[0]
            kt_s[:, rows] = piece[1].astype(F32).T.astype(BF16)
            v_s[rows, :] = piece[2]
        dk_s[...] = jnp.zeros_like(dk_s)
        dv_s[...] = jnp.zeros_like(dv_s)

    gt = gt_ref[...]
    prob = prob_ref[0]
    delta = jnp.sum(gt.astype(F32) * att_ref[...].astype(F32), axis=0, keepdims=True)
    dprob = dot(v_s[...], gt)
    dscore = (prob.astype(F32) * ((dprob - delta) * SCALE)).astype(BF16)
    q = q_s[pl.ds(pl.multiple_of(block * QB, QB), QB), :]
    dv_s[...] += dot(prob, gt, NT)
    dk_s[...] += dot(dscore, q)
    dq = dot(kt_s[...], dscore).T.astype(BF16)
    for s, out in enumerate(outs):
        i = s % (QB // TOK)

        @pl.when(block == s // (QB // TOK))
        def _():
            out[0] = dq[i * TOK : (i + 1) * TOK]

    @pl.when(block == last)
    def _():
        for s, out in enumerate(outs):
            rows = pl.ds(s * TOK, TOK)
            out[1] = dk_s[rows, :].astype(BF16)
            out[2] = dv_s[rows, :].astype(BF16)


def backward(qkv, prob, gt, att, first, count, after=()):
    return pl.pallas_call(
        backward_body,
        grid=(count, SEQ // QB),
        in_specs=[pl.BlockSpec((3, TOK, HD), lambda h, b: (0, 0, h + first))] * RANKS
        + [
            pl.BlockSpec((1, SEQ, QB), lambda h, b: (h + first, 0, b)),
            pl.BlockSpec((HD, QB), lambda h, b: (h + first, b)),
            pl.BlockSpec((HD, QB), lambda h, b: (h + first, b)),
        ]
        + hbm(len(after)),
        out_specs=[pl.BlockSpec((3, TOK, HD), lambda h, b: (0, 0, h))] * RANKS,
        scratch_shapes=[
            pltpu.VMEM((SEQ, HD), BF16),
            pltpu.VMEM((SEQ, HD), BF16),
            pltpu.VMEM((HD, SEQ), BF16),
            pltpu.VMEM((SEQ, HD), F32),
            pltpu.VMEM((SEQ, HD), F32),
        ],
        out_shape=[jax.ShapeDtypeStruct((3, TOK, count * HD), BF16)] * RANKS,
        compiler_params=params(),
        cost_estimate=cost(8 * count * SEQ * SEQ * HD, 2 * count * SEQ * (SEQ + 8 * HD), 0),
        name="backward",
    )(*qkv, prob, gt, att, *after)


def weight_body(count, at_ref, att_ref, *refs):
    outs, wide_s, att_s = refs[-2 - YS : -2], refs[-2], refs[-1]
    block, row = WIDTH // YS, WIDTH // (YS * ZS)

    @pl.when(pl.program_id(0) == 0)
    def _():
        wide_s[...] = att_ref[...].astype(F32)
        for i in range(YS * ZS):
            start = pl.multiple_of(at_ref[i] * row, 8)
            att_s[pl.ds(i * row, row), :] = wide_s[pl.ds(start, row), :]

    rows = jnp.concatenate([ref[...] for ref in refs[:RANKS]], axis=0)
    term = dot(att_s[...].astype(BF16), rows).astype(BF16)
    for i, out in enumerate(outs):
        out[...] = term[i * block : (i + 1) * block]


def weight_grad(order, att, pieces, after=()):
    wide = pieces[0].shape[1]
    piece = pl.BlockSpec((TOK, TILE), lambda j, o: (0, j))
    block = WIDTH // YS
    return pl.pallas_call(
        functools.partial(weight_body, wide // TILE),
        grid_spec=pltpu.PrefetchScalarGridSpec(
            num_scalar_prefetch=1,
            grid=(wide // TILE,),
            in_specs=[pl.BlockSpec((WIDTH, SEQ), lambda j, o: (0, 0))] + [piece] * RANKS + hbm(len(after)),
            out_specs=[pl.BlockSpec((block, TILE), lambda j, o: (0, j))] * YS,
            scratch_shapes=[pltpu.VMEM((WIDTH, SEQ), F32), pltpu.VMEM((WIDTH, SEQ), F32)],
        ),
        out_shape=[jax.ShapeDtypeStruct((block, wide), BF16)] * YS,
        compiler_params=params(),
        cost_estimate=cost(2 * WIDTH * SEQ * wide, 2 * (WIDTH * SEQ + SEQ * wide + WIDTH * wide)),
        name="weight_grad",
    )(order, att, *pieces, *after)


def heads_body(count, carry, w_ref, *refs):
    acc_ref = refs[-1]
    out_ref = refs[-2]
    step = pl.program_id(0)

    @pl.when(step == 0)
    def _():
        acc_ref[...] = refs[RANKS][...] if carry else jnp.zeros_like(acc_ref)

    rows = jnp.concatenate([ref[...] for ref in refs[:RANKS]], axis=0)
    acc_ref[...] += dot(w_ref[...], rows, NT)

    @pl.when(step == count - 1)
    def _():
        out_ref[...] = acc_ref[...].astype(out_ref.dtype)


def heads_grad(weights, offset, pieces, carry, dtype, after=()):
    wide = pieces[0].shape[1]
    count = wide // TILE
    first = offset // TILE
    piece = pl.BlockSpec((TOK, TILE), lambda j: (0, j))
    whole = pl.BlockSpec((WIDTH, SEQ), lambda j: (0, 0))
    extra = [] if carry is None else [carry]
    return pl.pallas_call(
        functools.partial(heads_body, count, carry is not None),
        grid=(count,),
        in_specs=[pl.BlockSpec((WIDTH, TILE), lambda j: (0, j + first))]
        + [piece] * RANKS
        + [whole] * len(extra)
        + hbm(len(after)),
        out_specs=whole,
        out_shape=jax.ShapeDtypeStruct((WIDTH, SEQ), dtype),
        scratch_shapes=[pltpu.VMEM((WIDTH, SEQ), F32)],
        compiler_params=params(),
        cost_estimate=cost(2 * WIDTH * SEQ * wide, 2 * (WIDTH * SEQ + SEQ * wide + WIDTH * wide)),
        name="heads_grad",
    )(weights, *pieces, *extra, *after)


def rank(x, c):
    return (x % XS) * CS + c


ONWARD = [(rank(x, c), rank(x + 1 - 2 * c, c)) for x in range(XS) for c in range(CS)]
SIBLING = [(rank(x, c), rank(x, 1 - c)) for x in range(XS) for c in range(CS)]


def gather_rows(own):
    seq = ("x", "c")
    send = lambda value, perm: lax.ppermute(value, seq, perm)
    near = send(own, ONWARD)
    sib = send(own, SIBLING)
    near_sib = send(sib, ONWARD)
    far = send(near, ONWARD)
    back = send(near, SIBLING)
    back_sib = send(near_sib, SIBLING)
    far_sib = send(far, SIBLING)
    return [own, sib, near, near_sib, back, back_sib, far, far_sib]


def source(slot, x, c):
    step = 1 - 2 * c
    dx = (0, 0, -step, -step, step, step, 2, 2)[slot]
    other = (0, 1, 0, 1, 1, 0, 0, 1)[slot]
    return (x + dx + XS) % XS * CS + (c + other) % CS


def target(slot, x, c):
    return source({2: 5, 5: 2}.get(slot, slot), x, c)


PLACES = [(x, c) for x in range(XS) for c in range(CS)]
INWARD = [[(source(s, x, c), rank(x, c)) for x, c in PLACES] for s in range(RANKS)]
OUTWARD = [[(rank(x, c), source(s, x, c)) for x, c in PLACES] for s in range(RANKS)]


def targets_table():
    x, c = lax.axis_index("x"), lax.axis_index("c")
    return jnp.stack([target(s, x, c) for s in range(RANKS)]).astype(jnp.int32)


def clip_order():
    y, z = lax.axis_index("y"), lax.axis_index("z")
    return jnp.stack(
        [(y + i) % YS * ZS + (z + j) % ZS for i in range(YS) for j in range(ZS)]
    ).astype(jnp.int32)


def swap(pieces, perms):
    return [pieces[0]] + [lax.ppermute(p, ("x", "c"), q) for p, q in zip(pieces[1:], perms[1:])]


def around(parts, axis, size):
    return [parts[0]] + [
        lax.ppermute(parts[i], axis, [(a, (a + i) % size) for a in range(size)]) for i in range(1, size)
    ]


def total(parts):
    return functools.reduce(jnp.add, [p.astype(F32) for p in parts])


def scatter_sum(parts):
    row = WIDTH // (YS * ZS)
    part = total(around(parts, "y", YS)).astype(BF16)
    return total(around([part[i * row : (i + 1) * row] for i in range(ZS)], "z", ZS))


def local(queries, keys, values, cotangent, gate, w_out):
    targets = targets_table()
    order = clip_order()
    cot = cotangent[0, 0]
    mine = [cot[:, a : a + n] for a, n in zip(STARTS, CHUNKS)]
    other = [lax.ppermute(m, "b", [(0, 1)]) for m in mine]
    weights = lax.all_gather(w_out[0], ("y", "z"), axis=0, tiled=True)
    qkv = swap(pack(targets, queries[0, 0], keys[0, 0], values[0, 0]), INWARD)
    pieces = [gather_rows(gated(gate[0], cot, o, a)) for o, a in zip(other, STARTS)]
    prob, att = forward(qkv)
    terms = [weight_grad(order, att, pieces[0])]
    carry = heads_grad(weights, STARTS[0], pieces[0], None, F32, after=terms[-1][:1])
    for a, p in zip(STARTS[1:], pieces[1:]):
        terms.append(weight_grad(order, att, p, after=[carry]))
        last = a == STARTS[-1]
        carry = heads_grad(weights, a, p, carry, BF16 if last else F32, after=terms[-1][:1])
    grad_weight = [scatter_sum(t) for t in terms]
    groups, after = [], ()
    for first, count in GROUPS:
        home = backward(qkv, prob, carry, att, first, count, after)
        after = home[:1]
        groups.append(swap(home, OUTWARD))
    dq, dk, dv = unpack(targets, groups)
    return (
        dq[None, None],
        dk[None, None],
        dv[None, None],
        jnp.concatenate(grad_weight, axis=1)[None],
    )


def solution(mesh):
    fine = Mesh(mesh.devices.reshape(2, XS, CS, YS, ZS), ("b", "x", "c", "y", "z"))
    tokens = P("b", ("y", "z"), ("x", "c"), None)
    weight = P("b", ("x", "c", "y", "z"), None)
    return jax.shard_map(
        local,
        mesh=fine,
        in_specs=(tokens, tokens, tokens, tokens, P("b", ("y", "z"), None), weight),
        out_specs=(tokens, tokens, tokens, weight),
        check_vma=False,
    )
```

time: 276 us -> 265 us (0.960); the launches traced: 274 us -> 260 us
  waiting for transfers between devices: 102 us -> 72.7 us
  starting transfers between devices: 69.5 us -> 85.4 us
  Pallas kernels: 72.5 us -> 77 us
  other arithmetic: 7.79 us -> 3.43 us
    ppermute x2 -> x35, starting transfers between devices: 7.34 us -> 69.1 us  [the longest x12 33.5 us: around(): lax.ppermute(parts[i], axis, [(a, (a + i) % size) for a in range(size)])]
    all_to_all x7 -> x0, waiting for transfers between devices: 60.6 us -> none  [exchange(): return lax.all_to_all(value, axis, split_axis=0, concat_axis=0, tiled=True)]
    ppermute x2 -> x35, waiting for transfers between devices: 20.8 us -> 71.1 us  [the longest x21 41.3 us: swap(): lax.ppermute(p, ('x', 'c'), q)]
    all_to_all x7 -> x0, starting transfers between devices: 40.2 us -> none  [exchange(): return lax.all_to_all(value, axis, split_axis=0, concat_axis=0, tiled=True)]
    ppermute x14, waiting for transfers between devices: 20.9 us -> 0.95 us  [gather_rows(): send = lambda value, perm: lax.ppermute(value, seq, perm)]
    ppermute x14, starting transfers between devices: 22 us -> 16.3 us  [gather_rows(): send = lambda value, perm: lax.ppermute(value, seq, perm)]
    pallas_call x7 -> x9, Pallas kernels: 57.3 us -> 61.7 us  [the longest x2 16.3 us: backward(): pl.pallas_call(backward_body, grid=(count, SEQ // QB), in_specs=[pl.Block...]
    reduce_sum x4 -> x0, other arithmetic: 4.08 us -> none  [the longest x2 3.94 us: scatter_sum(): part = jnp.sum(got.astype(F32), axis=0).astype(BF16)]
  transfers between devices with their start and end apart: 24 -> 50, of which waited for: 13 -> 16; matrix products, arithmetic and copies ran while one was open for 3% -> 2% of each run, Pallas kernels for 24% -> 30%
where the time goes in v1:
time: 265 us; the launch traced here: 260 us
  starting transfers between devices  85.4 us (32%)
  Pallas kernels  77 us (29%)
  waiting for transfers between devices  72.7 us (27%)
  between operations  14.7 us (6%)
  local copies, waits for them, and re-layouts  6.6 us (2%)
  other arithmetic  3.43 us (1%)
    ppermute x21, waiting for transfers between devices, swap(): lax.ppermute(p, ('x', 'c'), q)  41.3 us
    ppermute x12, starting transfers between devices, around(): lax.ppermute(parts[i], axis, [(a, (a + i) % size) for a in range(size)])  33.5 us
    ppermute x21, starting transfers between devices, swap(): lax.ppermute(p, ('x', 'c'), q)  27 us
    ppermute x12, waiting for transfers between devices, around(): lax.ppermute(parts[i], axis, [(a, (a + i) % size) for a in range(size)])  16.5 us
    ppermute x14, starting transfers between devices, gather_rows(): send = lambda value, perm: lax.ppermute(value, seq, perm)  16.3 us
    pallas_call x2, Pallas kernels, backward(): pl.pallas_call(backward_body, grid=(count, SEQ // QB), in_specs=[pl.Block...  16.3 us
    pallas_call x2, Pallas kernels, weight_grad(): pl.pallas_call(functools.partial(weight_body, wide // TILE), grid_spec=pl...  15.4 us
    pallas_call x2, Pallas kernels, heads_grad(): pl.pallas_call(functools.partial(heads_body, count, carry is not None), g...  15.3 us
  transfers between devices with their start and end apart: 50, of which 16 were waited for; matrix products, arithmetic and copies ran while one was open for 2% of the time, Pallas kernels for 30%

profile of v1, /device:TPU:1, one launch (start us, length us, event | category | flops | bytes accessed | tf_op | source)
XLA Modules:
  0.0 259.9 jit_solution(9135347646339703717)
XLA Ops:
  7.9 1.4 fusion
  9.3 4.4 %collective-permute-start.15 = (bf16[128,2560]{1,0:T(8,128)(2,1)S(1)}, bf16[128,2560]{1,0:T(8,128)(2,1)S(1)}, u32[]{:S(2)}, u32[]{:S(2)}) collective-permute-start(bf16[128,2560]{1,0:T(8,128)(2,1)S(1)} %get-tuple-element.78), channel_id=1, source_target_pairs={{0,128},{1,129},{2,130},{3,131},{4,132},{5,133},{6,134},{7,135},{8... | collective-permute-start | bytes 1966088 | tf_op jit(solution)/shard_map/ppermute | solution.py:393
  13.7 13.3 %collective-permute-done.15.other_ref = bf16[128,2560]{1,0:T(8,128)(2,1)S(1)} collective-permute-done((bf16[128,2560]{1,0:T(8,128)(2,1)S(1)}, bf16[128,2560]{1,0:T(8,128)(2,1)S(1)}, u32[]{:S(2)}, u32[]{:S(2)}) %collective-permute-start.15) | collective-permute-done | bytes 655392 | tf_op jit(solution)/shard_map/ppermute | solution.py:393
  27.0 0.8 copy-done.16
  27.9 4.0 %gated.3.refs_0_ = bf16[128,2560]{1,0:T(8,128)(2,1)} custom-call(f32[1,5120]{1,0:T(1,128)} %bitcast.43, bf16[128,5120]{1,0:T(8,128)(2,1)} %bitcast.38, bf16[128,2560]{1,0:T(8,128)(2,1)} %copy-done.16), custom_call_target="tpu_custom_call" | custom-call | flops 655360 | bytes 1966080 | tf_op jit(solution)/shard_map/gated/pallas_call | solution.py:111
  31.8 2.5 collective-permute-start.17
  34.3 1.0 collective-permute-start.16
  35.3 4.2 %collective-permute-start.7 = (bf16[128,2560]{1,0:T(8,128)(2,1)S(1)}, bf16[128,2560]{1,0:T(8,128)(2,1)S(1)}, u32[]{:S(2)}, u32[]{:S(2)}) collective-permute-start(bf16[128,2560]{1,0:T(8,128)(2,1)S(1)} %get-tuple-element.79), channel_id=1, source_target_pairs={{0,128},{1,129},{2,130},{3,131},{4,132},{5,133},{6,134},{7,135},{8... | collective-permute-start | bytes 1966088 | tf_op jit(solution)/shard_map/ppermute | solution.py:393
  40.1 3.9 %pack.1 = (bf16[3,128,384]{2,1,0:T(8,128)(2,1)}, bf16[3,128,384]{2,1,0:T(8,128)(2,1)}, bf16[3,128,384]{2,1,0:T(8,128)(2,1)}, bf16[3,128,384]{2,1,0:T(8,128)(2,1)...) custom-call(s32[8]{0:T(128)} %stack.86.col_ref, ...), custom_call_target="tpu_custom_call" | custom-call | bytes 4718592 | tf_op jit(solution)/shard_map/pack/pallas_call | solution.py:57
  44.3 1.4 collective-permute-start.1
  45.8 1.4 collective-permute-start.21
  47.6 1.1 collective-permute-start.2
  48.8 1.6 collective-permute-done.1.refs_2_
  50.4 2.4 collective-permute-start.3
  52.8 4.8 %collective-permute-done.2.refs_3_ = bf16[3,128,384]{2,1,0:T(8,128)(2,1)S(1)} collective-permute-done((bf16[3,128,384]{2,1,0:T(8,128)(2,1)}, bf16[3,128,384]{2,1,0:T(8,128)(2,1)S(1)}, u32[]{:S(2)}, u32[]{:S(2)}) %collective-permute-start.2) | collective-permute-done | bytes 294944 | tf_op jit(solution)/shard_map/ppermute | solution.py:369
  57.6 1.0 collective-permute-start.4
  58.6 17.3 %collective-permute-done.3.refs_4_ = bf16[3,128,384]{2,1,0:T(8,128)(2,1)S(1)} collective-permute-done((bf16[3,128,384]{2,1,0:T(8,128)(2,1)}, bf16[3,128,384]{2,1,0:T(8,128)(2,1)S(1)}, u32[]{:S(2)}, u32[]{:S(2)}) %collective-permute-start.3) | collective-permute-done | bytes 294944 | tf_op jit(solution)/shard_map/ppermute | solution.py:369
  75.9 1.3 collective-permute-start.5
  78.1 4.0 %gated.2.refs_0_ = bf16[128,2560]{1,0:T(8,128)(2,1)} custom-call(f32[1,5120]{1,0:T(1,128)} %bitcast.44, bf16[128,5120]{1,0:T(8,128)(2,1)} %bitcast.39, bf16[128,2560]{1,0:T(8,128)(2,1)} %copy-done.15), custom_call_target="tpu_custom_call" | custom-call | flops 655360 | bytes 1966080 | tf_op jit(solution)/shard_map/gated/pallas_call | solution.py:111
  82.0 2.1 collective-permute-start.9
  84.2 2.6 %collective-permute-done.5.refs_6_ = bf16[3,128,384]{2,1,0:T(8,128)(2,1)S(1)} collective-permute-done((bf16[3,128,384]{2,1,0:T(8,128)(2,1)}, bf16[3,128,384]{2,1,0:T(8,128)(2,1)S(1)}, u32[]{:S(2)}, u32[]{:S(2)}) %collective-permute-start.5) | collective-permute-done | bytes 294944 | tf_op jit(solution)/shard_map/ppermute | solution.py:369
  86.8 4.1 %collective-permute-done.6.refs_7_ = bf16[3,128,384]{2,1,0:T(8,128)(2,1)S(1)} collective-permute-done((bf16[3,128,384]{2,1,0:T(8,128)(2,1)}, bf16[3,128,384]{2,1,0:T(8,128)(2,1)S(1)}, u32[]{:S(2)}, u32[]{:S(2)}) %collective-permute-start.6) | collective-permute-done | bytes 294944 | tf_op jit(solution)/shard_map/ppermute | solution.py:369
  90.8 2.6 collective-permute-start.19
  94.9 14.1 %forward.1 = (bf16[3,1024,1024]{2,1,0:T(8,128)(2,1)}, bf16[384,1024]{1,0:T(8,128)(2,1)}) custom-call(bf16[3,128,384]{2,1,0:T(8,128)(2,1)} %get-tuple-element.41.refs_0_, bf16[3,128,384]{2,1,0:T(8,128)(2,1)} %copy-done.8, bf16[3,128,384]{2,1,0:T(8,128)(2,1)} %copy-done.9, bf16[3,128,384]{2,1,0:T(8,128)(2,1)} %copy-done.10, bf16[3,128,384]{2,1,0:T(8,128)(2,1)} %copy-done.11, ...), custom_call_target="tpu_custom_call" | custom-call | flops 1610612736 | bytes 9437184 | tf_op jit(solution)/shard_map/forward/pallas_call | solution.py:151
  109.0 1.4 collective-permute-start.13
  110.6 7.7 %weight_grad.2 = (bf16[96,2560]{1,0:T(8,128)(2,1)}, bf16[96,2560]{1,0:T(8,128)(2,1)}, bf16[96,2560]{1,0:T(8,128)(2,1)}, bf16[96,2560]{1,0:T(8,128)(2,1)}) custom-call(s32[16]{0:T(128)} %stack.103.at_ref, bf16[384,1024]{1,0:T(8,128)(2,1)} %get-tuple-element.50.att_ref.refs_10_, bf16[128,2560]{1,0:T(8,128)(2,1)} %gated.3.refs_0_, ...), custom_call_target="tpu_custom_call" | custom-call | flops 2013265920 | bytes 7995392 | tf_op jit(solution)/shard_map/weight_grad/pallas_call | solution.py:263
  118.3 1.5 collective-permute-start.37
  119.9 3.0 %collective-permute-start.38 = (bf16[96,2560]{1,0:T(8,128)(2,1)}, bf16[96,2560]{1,0:T(8,128)(2,1)S(1)}, u32[]{:S(2)}, u32[]{:S(2)}) collective-permute-start(bf16[96,2560]{1,0:T(8,128)(2,1)} %get-tuple-element.73), channel_id=1, source_target_pairs={{0,8},{4,12},{8,0},{12,4},{1,9},{5,13},{9,1},{13,5},{2,10},{6,14},... | collective-permute-start | bytes 1474568 | tf_op jit(solution)/shard_map/ppermute | solution.py:374
  122.9 0.9 collective-permute-start.39
  123.8 1.1 collective-permute-start.11
  124.9 0.9 collective-permute-done.10.refs_3_
  125.8 2.2 collective-permute-start.14
  128.0 5.5 %collective-permute-done.37 = bf16[96,2560]{1,0:T(8,128)(2,1)S(1)} collective-permute-done((bf16[96,2560]{1,0:T(8,128)(2,1)}, bf16[96,2560]{1,0:T(8,128)(2,1)S(1)}, u32[]{:S(2)}, u32[]{:S(2)}) %collective-permute-start.37) | collective-permute-done | bytes 491552 | tf_op jit(solution)/shard_map/ppermute | solution.py:374
  134.1 10.7 %collective-permute-done.38 = bf16[96,2560]{1,0:T(8,128)(2,1)S(1)} collective-permute-done((bf16[96,2560]{1,0:T(8,128)(2,1)}, bf16[96,2560]{1,0:T(8,128)(2,1)S(1)}, u32[]{:S(2)}, u32[]{:S(2)}) %collective-permute-start.38) | collective-permute-done | bytes 491552 | tf_op jit(solution)/shard_map/ppermute | solution.py:374
  144.8 1.3 add_convert_fusion.1
  146.1 0.8 fusion.1
  147.0 5.0 %collective-permute-start.40 = (bf16[24,2560]{1,0:T(8,128)(2,1)}, bf16[24,2560]{1,0:T(8,128)(2,1)S(1)}, u32[]{:S(2)}, u32[]{:S(2)}) collective-permute-start(bf16[24,2560]{1,0:T(8,128)(2,1)} %get-tuple-element.80), channel_id=1, source_target_pairs={{0,1},{1,2},{2,3},{3,0},{4,5},{5,6},{6,7},{7,4},{8,9},{9,10},{10,1... | collective-permute-start | bytes 368648 | tf_op jit(solution)/shard_map/ppermute | solution.py:374
  152.0 4.3 %collective-permute-start.41 = (bf16[24,2560]{1,0:T(8,128)(2,1)}, bf16[24,2560]{1,0:T(8,128)(2,1)S(1)}, u32[]{:S(2)}, u32[]{:S(2)}) collective-permute-start(bf16[24,2560]{1,0:T(8,128)(2,1)} %get-tuple-element.82), channel_id=1, source_target_pairs={{0,2},{1,3},{2,0},{3,1},{4,6},{5,7},{6,4},{7,5},{8,10},{9,11},{10,... | collective-permute-start | bytes 368648 | tf_op jit(solution)/shard_map/ppermute | solution.py:374
  156.3 7.5 %heads_grad.2.refs_8_ = f32[384,1024]{1,0:T(8,128)} custom-call(bf16[384,5120]{1,0:T(8,128)(2,1)} %bitcast.35, bf16[128,2560]{1,0:T(8,128)(2,1)} %gated.3.refs_0_, bf16[128,2560]{1,0:T(8,128)(2,1)} %collective-permute-done.16.refs_1_, bf16[128,2560]{1,0:T(8,128)(2,1)} %collective-permute-done.17.refs_2_, bf16[128,2560]{1,0:T(8,128)(2,1)} %collective-permute-done.18.refs_3_, ...), custom_call_target="tpu_custom_call" | custom-call | flops 2013265920 | bytes 7995392 | tf_op jit(solution)/shard_map/heads_grad/pallas_call | solution.py:303
  163.8 3.3 %collective-permute-start.42 = (bf16[24,2560]{1,0:T(8,128)(2,1)S(1)}, bf16[24,2560]{1,0:T(8,128)(2,1)S(1)}, u32[]{:S(2)}, u32[]{:S(2)}) collective-permute-start(bf16[24,2560]{1,0:T(8,128)(2,1)S(1)} %copy-done.24), channel_id=1, source_target_pairs={{0,3},{1,0},{2,1},{3,2},{4,7},{5,4},{6,5},{7,6},{8,11},{9,8},{10,9... | collective-permute-start | bytes 368648 | tf_op jit(solution)/shard_map/ppermute | solution.py:374
  167.2 0.8 copy-done.5
  168.0 7.7 %weight_grad.3 = (bf16[96,2560]{1,0:T(8,128)(2,1)}, bf16[96,2560]{1,0:T(8,128)(2,1)}, bf16[96,2560]{1,0:T(8,128)(2,1)}, bf16[96,2560]{1,0:T(8,128)(2,1)}) custom-call(s32[16]{0:T(128)} %stack.103.at_ref, bf16[384,1024]{1,0:T(8,128)(2,1)} %get-tuple-element.50.att_ref.refs_10_, bf16[128,2560]{1,0:T(8,128)(2,1)} %gated.2.refs_0_, bf16[128,2560]{1,0:T(8,128)(2,1)} %copy-done.1, ...), custom_call_target="tpu_custom_call" | custom-call | flops 2013265920 | bytes 7995392 | tf_op jit(solution)/shard_map/weight_grad/pallas_call | solution.py:263
  175.7 0.8 collective-permute-start.43
  176.5 2.7 %collective-permute-start.44 = (bf16[96,2560]{1,0:T(8,128)(2,1)}, bf16[96,2560]{1,0:T(8,128)(2,1)S(1)}, u32[]{:S(2)}, u32[]{:S(2)}) collective-permute-start(bf16[96,2560]{1,0:T(8,128)(2,1)} %get-tuple-element.76), channel_id=1, source_target_pairs={{0,8},{4,12},{8,0},{12,4},{1,9},{5,13},{9,1},{13,5},{2,10},{6,14},... | collective-permute-start | bytes 1474568 | tf_op jit(solution)/shard_map/ppermute | solution.py:374
  179.2 10.6 %collective-permute-start.45 = (bf16[96,2560]{1,0:T(8,128)(2,1)}, bf16[96,2560]{1,0:T(8,128)(2,1)S(1)}, u32[]{:S(2)}, u32[]{:S(2)}) collective-permute-start(bf16[96,2560]{1,0:T(8,128)(2,1)} %get-tuple-element.77), channel_id=1, source_target_pairs={{0,12},{4,0},{8,4},{12,8},{1,13},{5,1},{9,5},{13,9},{2,14},{6,2},{... | collective-permute-start | bytes 1474568 | tf_op jit(solution)/shard_map/ppermute | solution.py:374
  189.7 7.8 %heads_grad.3.refs_9_ = bf16[384,1024]{1,0:T(8,128)(2,1)} custom-call(bf16[384,5120]{1,0:T(8,128)(2,1)} %bitcast.36, bf16[128,2560]{1,0:T(8,128)(2,1)} %gated.2.refs_0_, bf16[128,2560]{1,0:T(8,128)(2,1)} %copy-done.1, bf16[128,2560]{1,0:T(8,128)(2,1)} %copy-done, bf16[128,2560]{1,0:T(8,128)(2,1)} %copy-done.3, bf16[128,2560]{1,0:T(8,128)(2,1)} %copy-done.4, ...), custom_call_target="tpu_custom_call" | custom-call | flops 2013265920 | bytes 7995392 | tf_op jit(solution)/shard_map/heads_grad/pallas_call | solution.py:303
  197.6 5.9 %backward.2 = (bf16[3,128,128]{2,1,0:T(8,128)(2,1)}, bf16[3,128,128]{2,1,0:T(8,128)(2,1)}, bf16[3,128,128]{2,1,0:T(8,128)(2,1)}, bf16[3,128,128]{2,1,0:T(8,128)(...) custom-call(bf16[3,128,384]{2,1,0:T(8,128)(2,1)} %get-tuple-element., ...), custom_call_target="tpu_custom_call" | custom-call | flops 1073741824 | bytes 4194304 | tf_op jit(solution)/shard_map/backward/pallas_call | solution.py:217
  203.5 2.9 %collective-permute-start.23 = (bf16[3,128,128]{2,1,0:T(8,128)(2,1)}, bf16[3,128,128]{2,1,0:T(8,128)(2,1)S(1)}, u32[]{:S(2)}, u32[]{:S(2)}) collective-permute-start(bf16[3,128,128]{2,1,0:T(8,128)(2,1)} %get-tuple-element.54), channel_id=1, source_target_pairs={{0,16},{16,0},{32,48},{48,32},{64,80},{80,64},{96,112},{112,96},{1... | collective-permute-start | bytes 294920 | tf_op jit(solution)/shard_map/ppermute | solution.py:369
  207.2 10.4 %backward.3 = (bf16[3,128,256]{2,1,0:T(8,128)(2,1)}, bf16[3,128,256]{2,1,0:T(8,128)(2,1)}, bf16[3,128,256]{2,1,0:T(8,128)(2,1)}, bf16[3,128,256]{2,1,0:T(8,128)(...) custom-call(bf16[3,128,384]{2,1,0:T(8,128)(2,1)} %get-tuple-element., ...), custom_call_target="tpu_custom_call" | custom-call | flops 2147483648 | bytes 8388608 | tf_op jit(solution)/shard_map/backward/pallas_call | solution.py:217
  217.7 1.0 collective-permute-start.25
  219.3 1.4 collective-permute-start.27
  220.8 2.5 collective-permute-start.28
  224.6 1.2 collective-permute-start.31
  225.8 1.0 collective-permute-start.32
  227.1 2.9 %collective-permute-start.33 = (bf16[3,128,256]{2,1,0:T(8,128)(2,1)S(1)}, bf16[3,128,256]{2,1,0:T(8,128)(2,1)S(1)}, u32[]{:S(2)}, u32[]{:S(2)}) collective-permute-start(bf16[3,128,256]{2,1,0:T(8,128)(2,1)S(1)} %copy-done.35), channel_id=1, source_target_pairs={{0,48},{16,96},{32,80},{48,0},{64,112},{80,32},{96,16},{112,64},{1... | collective-permute-start | bytes 589832 | tf_op jit(solution)/shard_map/ppermute | solution.py:369
  230.0 1.1 collective-permute-start.34
  231.2 0.8 collective-permute-start.35
  232.3 1.9 collective-permute-start.36
  234.2 1.3 collective-permute-done.32.refs_11_
  236.1 1.4 collective-permute-start.47
  237.5 7.7 %collective-permute-done.34.refs_13_ = bf16[3,128,256]{2,1,0:T(8,128)(2,1)S(1)} collective-permute-done((bf16[3,128,256]{2,1,0:T(8,128)(2,1)S(1)}, bf16[3,128,256]{2,1,0:T(8,128)(2,1)S(1)}, u32[]{:S(2)}, u32[]{:S(2)}) %collective-permute-start.34) | collective-permute-done | bytes 196640 | tf_op jit(solution)/shard_map/ppermute | solution.py:369
  245.2 1.0 convert_add_fusion.1
  247.5 4.2 %unpack.1 = (bf16[128,3072]{1,0:T(8,128)(2,1)}, bf16[128,3072]{1,0:T(8,128)(2,1)}, bf16[128,3072]{1,0:T(8,128)(2,1)}) custom-call(s32[8]{0:T(128)} %stack.86.col_ref, bf16[3,128,128]{2,1,0:T(8,128)(2,1)} %get-tuple-element.53.refs_11_.refs_0_, bf16[3,128,128]{2,1,0:T(8,128)(2,1)} %copy-done.25, bf16[3,128,128]{2,1,0:T(8,128)(2,1)} %copy-done.26, ...), custom_call_target="tpu_custom_call" | custom-call | bytes 4718592 | tf_op jit(solution)/shard_map/unpack/pallas_call | solution.py:88
  252.0 0.8 maximum_bitcast_fusion
  (146 shorter events, 11.0 us)
Async XLA Ops:
  7.2 149.1 %all-gather.3.cloned.1.call-start = ((), (), s32[]{:S(2)}) async-start(), calls=%async_computation | async-start | bytes 4177920 | tf_op jit(solution)/shard_map/all_gather | solution.py:394
  9.3 17.8 %collective-permute-start.15 = (bf16[128,2560]{1,0:T(8,128)(2,1)S(1)}, bf16[128,2560]{1,0:T(8,128)(2,1)S(1)}, u32[]{:S(2)}, u32[]{:S(2)}) collective-permute-start(bf16[128,2560]{1,0:T(8,128)(2,1)S(1)} %get-tuple-element.78), channel_id=1, source_target_pairs={{0,128},{1,129},{2,130},{3,131},{4,132},{5,133},{6,134},{7,135},{8... | collective-permute-start | bytes 1966088 | tf_op jit(solution)/shard_map/ppermute | solution.py:393
  31.8 13.9 %collective-permute-start.17 = (bf16[128,2560]{1,0:T(8,128)(2,1)}, bf16[128,2560]{1,0:T(8,128)(2,1)}, u32[]{:S(2)}, u32[]{:S(2)}) collective-permute-start(bf16[128,2560]{1,0:T(8,128)(2,1)} %gated.3.refs_0_), channel_id=1, source_target_pairs={{0,32},{16,112},{32,64},{48,16},{64,96},{80,48},{96,0},{112,80},{1... | collective-permute-start | bytes 1966088 | tf_op jit(solution)/shard_map/ppermute | solution.py:329
  34.3 12.8 %collective-permute-start.16 = (bf16[128,2560]{1,0:T(8,128)(2,1)}, bf16[128,2560]{1,0:T(8,128)(2,1)}, u32[]{:S(2)}, u32[]{:S(2)}) collective-permute-start(bf16[128,2560]{1,0:T(8,128)(2,1)} %gated.3.refs_0_), channel_id=1, source_target_pairs={{0,16},{16,0},{32,48},{48,32},{64,80},{80,64},{96,112},{112,96},{1... | collective-permute-start | bytes 1966088 | tf_op jit(solution)/shard_map/ppermute | solution.py:329
  35.3 41.9 %collective-permute-start.7 = (bf16[128,2560]{1,0:T(8,128)(2,1)S(1)}, bf16[128,2560]{1,0:T(8,128)(2,1)S(1)}, u32[]{:S(2)}, u32[]{:S(2)}) collective-permute-start(bf16[128,2560]{1,0:T(8,128)(2,1)S(1)} %get-tuple-element.79), channel_id=1, source_target_pairs={{0,128},{1,129},{2,130},{3,131},{4,132},{5,133},{6,134},{7,135},{8... | collective-permute-start | bytes 1966088 | tf_op jit(solution)/shard_map/ppermute | solution.py:393
  44.0 3.6 %collective-permute-start = (bf16[3,128,384]{2,1,0:T(8,128)(2,1)}, bf16[3,128,384]{2,1,0:T(8,128)(2,1)S(1)}, u32[]{:S(2)}, u32[]{:S(2)}) collective-permute-start(bf16[3,128,384]{2,1,0:T(8,128)(2,1)} %get-tuple-element.42), channel_id=1, source_target_pairs={{16,0},{0,16},{48,32},{32,48},{80,64},{64,80},{112,96},{96,112},{1... | collective-permute-start | bytes 884744 | tf_op jit(solution)/shard_map/ppermute | solution.py:369
  44.3 6.1 %collective-permute-start.1 = (bf16[3,128,384]{2,1,0:T(8,128)(2,1)}, bf16[3,128,384]{2,1,0:T(8,128)(2,1)S(1)}, u32[]{:S(2)}, u32[]{:S(2)}) collective-permute-start(bf16[3,128,384]{2,1,0:T(8,128)(2,1)} %get-tuple-element.43), channel_id=1, source_target_pairs={{96,0},{48,16},{0,32},{80,48},{32,64},{112,80},{64,96},{16,112},{9... | collective-permute-start | bytes 884744 | tf_op jit(solution)/shard_map/ppermute | solution.py:369
  45.8 47.7 %collective-permute-start.21 = (bf16[128,2560]{1,0:T(8,128)(2,1)}, bf16[128,2560]{1,0:T(8,128)(2,1)}, u32[]{:S(2)}, u32[]{:S(2)}) collective-permute-start(bf16[128,2560]{1,0:T(8,128)(2,1)} %collective-permute-done.17.refs_2_), channel_id=1, source_target_pairs={{0,32},{16,112},{32,64},{48,16},{64,96},{80,48},{96,0},{112,80},{1... | collective-permute-start | bytes 1966088 | tf_op jit(solution)/shard_map/ppermute | solution.py:329
  47.1 46.4 %collective-permute-start.18 = (bf16[128,2560]{1,0:T(8,128)(2,1)}, bf16[128,2560]{1,0:T(8,128)(2,1)}, u32[]{:S(2)}, u32[]{:S(2)}) collective-permute-start(bf16[128,2560]{1,0:T(8,128)(2,1)} %collective-permute-done.16.refs_1_), channel_id=1, source_target_pairs={{0,32},{16,112},{32,64},{48,16},{64,96},{80,48},{96,0},{112,80},{1... | collective-permute-start | bytes 1966088 | tf_op jit(solution)/shard_map/ppermute | solution.py:329
  47.6 47.2 %copy-start.8 = (bf16[3,128,384]{2,1,0:T(8,128)(2,1)}, bf16[3,128,384]{2,1,0:T(8,128)(2,1)S(1)}, u32[]{:S(2)}) copy-start(bf16[3,128,384]{2,1,0:T(8,128)(2,1)S(1)} %collective-permute-done.refs_1_) | copy-start | bytes 884740
  47.6 10.0 %collective-permute-start.2 = (bf16[3,128,384]{2,1,0:T(8,128)(2,1)}, bf16[3,128,384]{2,1,0:T(8,128)(2,1)S(1)}, u32[]{:S(2)}, u32[]{:S(2)}) collective-permute-start(bf16[3,128,384]{2,1,0:T(8,128)(2,1)} %get-tuple-element.44), channel_id=1, source_target_pairs={{112,0},{32,16},{16,32},{64,48},{48,64},{96,80},{80,96},{0,112},{1... | collective-permute-start | bytes 884744 | tf_op jit(solution)/shard_map/ppermute | solution.py:369
  50.4 44.4 %copy-start.9 = (bf16[3,128,384]{2,1,0:T(8,128)(2,1)}, bf16[3,128,384]{2,1,0:T(8,128)(2,1)S(1)}, u32[]{:S(2)}) copy-start(bf16[3,128,384]{2,1,0:T(8,128)(2,1)S(1)} %collective-permute-done.1.refs_2_) | copy-start | bytes 884740
  50.4 25.5 %collective-permute-start.3 = (bf16[3,128,384]{2,1,0:T(8,128)(2,1)}, bf16[3,128,384]{2,1,0:T(8,128)(2,1)S(1)}, u32[]{:S(2)}, u32[]{:S(2)}) collective-permute-start(bf16[3,128,384]{2,1,0:T(8,128)(2,1)} %get-tuple-element.45), channel_id=1, source_target_pairs={{48,0},{96,16},{80,32},{0,48},{112,64},{32,80},{16,96},{64,112},{4... | collective-permute-start | bytes 884744 | tf_op jit(solution)/shard_map/ppermute | solution.py:369
  57.6 37.2 %copy-start.10 = (bf16[3,128,384]{2,1,0:T(8,128)(2,1)}, bf16[3,128,384]{2,1,0:T(8,128)(2,1)S(1)}, u32[]{:S(2)}) copy-start(bf16[3,128,384]{2,1,0:T(8,128)(2,1)S(1)} %collective-permute-done.2.refs_3_) | copy-start | bytes 884740
  57.6 24.4 %collective-permute-start.4 = (bf16[3,128,384]{2,1,0:T(8,128)(2,1)}, bf16[3,128,384]{2,1,0:T(8,128)(2,1)S(1)}, u32[]{:S(2)}, u32[]{:S(2)}) collective-permute-start(bf16[3,128,384]{2,1,0:T(8,128)(2,1)} %get-tuple-element.46), channel_id=1, source_target_pairs={{32,0},{112,16},{64,32},{16,48},{96,64},{48,80},{0,96},{80,112},{3... | collective-permute-start | bytes 884744 | tf_op jit(solution)/shard_map/ppermute | solution.py:369
  75.9 19.0 %copy-start.11 = (bf16[3,128,384]{2,1,0:T(8,128)(2,1)}, bf16[3,128,384]{2,1,0:T(8,128)(2,1)S(1)}, u32[]{:S(2)}) copy-start(bf16[3,128,384]{2,1,0:T(8,128)(2,1)S(1)} %collective-permute-done.3.refs_4_) | copy-start | bytes 884740
  75.9 10.9 %collective-permute-start.5 = (bf16[3,128,384]{2,1,0:T(8,128)(2,1)}, bf16[3,128,384]{2,1,0:T(8,128)(2,1)S(1)}, u32[]{:S(2)}, u32[]{:S(2)}) collective-permute-start(bf16[3,128,384]{2,1,0:T(8,128)(2,1)} %get-tuple-element.47), channel_id=1, source_target_pairs={{64,0},{80,16},{96,32},{112,48},{0,64},{16,80},{32,96},{48,112},{6... | collective-permute-start | bytes 884744 | tf_op jit(solution)/shard_map/ppermute | solution.py:369
  77.2 13.6 %collective-permute-start.6 = (bf16[3,128,384]{2,1,0:T(8,128)(2,1)}, bf16[3,128,384]{2,1,0:T(8,128)(2,1)S(1)}, u32[]{:S(2)}, u32[]{:S(2)}) collective-permute-start(bf16[3,128,384]{2,1,0:T(8,128)(2,1)} %get-tuple-element.48), channel_id=1, source_target_pairs={{80,0},{64,16},{112,32},{96,48},{16,64},{0,80},{48,96},{32,112},{8... | collective-permute-start | bytes 884744 | tf_op jit(solution)/shard_map/ppermute | solution.py:369
  82.0 26.9 %collective-permute-start.9 = (bf16[128,2560]{1,0:T(8,128)(2,1)}, bf16[128,2560]{1,0:T(8,128)(2,1)S(1)}, u32[]{:S(2)}, u32[]{:S(2)}) collective-permute-start(bf16[128,2560]{1,0:T(8,128)(2,1)} %gated.2.refs_0_), channel_id=1, source_target_pairs={{0,32},{16,112},{32,64},{48,16},{64,96},{80,48},{96,0},{112,80},{1... | collective-permute-start | bytes 1966088 | tf_op jit(solution)/shard_map/ppermute | solution.py:329
  86.8 23.6 %collective-permute-start.8 = (bf16[128,2560]{1,0:T(8,128)(2,1)}, bf16[128,2560]{1,0:T(8,128)(2,1)S(1)}, u32[]{:S(2)}, u32[]{:S(2)}) collective-permute-start(bf16[128,2560]{1,0:T(8,128)(2,1)} %gated.2.refs_0_), channel_id=1, source_target_pairs={{0,16},{16,0},{32,48},{48,32},{64,80},{80,64},{96,112},{112,96},{1... | collective-permute-start | bytes 1966088 | tf_op jit(solution)/shard_map/ppermute | solution.py:329
  90.8 19.7 %collective-permute-start.19 = (bf16[128,2560]{1,0:T(8,128)(2,1)}, bf16[128,2560]{1,0:T(8,128)(2,1)}, u32[]{:S(2)}, u32[]{:S(2)}) collective-permute-start(bf16[128,2560]{1,0:T(8,128)(2,1)} %collective-permute-done.17.refs_2_), channel_id=1, source_target_pairs={{0,16},{16,0},{32,48},{48,32},{64,80},{80,64},{96,112},{112,96},{1... | collective-permute-start | bytes 1966088 | tf_op jit(solution)/shard_map/ppermute | solution.py:329
  93.4 17.2 %collective-permute-start.22 = (bf16[128,2560]{1,0:T(8,128)(2,1)}, bf16[128,2560]{1,0:T(8,128)(2,1)}, u32[]{:S(2)}, u32[]{:S(2)}) collective-permute-start(bf16[128,2560]{1,0:T(8,128)(2,1)} %collective-permute-done.21.refs_6_), channel_id=1, source_target_pairs={{0,16},{16,0},{32,48},{48,32},{64,80},{80,64},{96,112},{112,96},{1... | collective-permute-start | bytes 1966088 | tf_op jit(solution)/shard_map/ppermute | solution.py:329
  93.5 17.1 %collective-permute-start.20 = (bf16[128,2560]{1,0:T(8,128)(2,1)}, bf16[128,2560]{1,0:T(8,128)(2,1)}, u32[]{:S(2)}, u32[]{:S(2)}) collective-permute-start(bf16[128,2560]{1,0:T(8,128)(2,1)} %collective-permute-done.18.refs_3_), channel_id=1, source_target_pairs={{0,16},{16,0},{32,48},{48,32},{64,80},{80,64},{96,112},{112,96},{1... | collective-permute-start | bytes 1966088 | tf_op jit(solution)/shard_map/ppermute | solution.py:329
  109.0 14.8 %collective-permute-start.13 = (bf16[128,2560]{1,0:T(8,128)(2,1)S(1)}, bf16[128,2560]{1,0:T(8,128)(2,1)S(1)}, u32[]{:S(2)}, u32[]{:S(2)}) collective-permute-start(bf16[128,2560]{1,0:T(8,128)(2,1)S(1)} %collective-permute-done.9.refs_2_), channel_id=1, source_target_pairs={{0,32},{16,112},{32,64},{48,16},{64,96},{80,48},{96,0},{112,80},{1... | collective-permute-start | bytes 1966088 | tf_op jit(solution)/shard_map/ppermute | solution.py:329
  110.4 15.4 %collective-permute-start.10 = (bf16[128,2560]{1,0:T(8,128)(2,1)S(1)}, bf16[128,2560]{1,0:T(8,128)(2,1)S(1)}, u32[]{:S(2)}, u32[]{:S(2)}) collective-permute-start(bf16[128,2560]{1,0:T(8,128)(2,1)S(1)} %collective-permute-done.8.refs_1_), channel_id=1, source_target_pairs={{0,32},{16,112},{32,64},{48,16},{64,96},{80,48},{96,0},{112,80},{1... | collective-permute-start | bytes 1966088 | tf_op jit(solution)/shard_map/ppermute | solution.py:329
  118.3 15.1 %collective-permute-start.37 = (bf16[96,2560]{1,0:T(8,128)(2,1)}, bf16[96,2560]{1,0:T(8,128)(2,1)S(1)}, u32[]{:S(2)}, u32[]{:S(2)}) collective-permute-start(bf16[96,2560]{1,0:T(8,128)(2,1)} %get-tuple-element.72), channel_id=1, source_target_pairs={{0,4},{4,8},{8,12},{12,0},{1,5},{5,9},{9,13},{13,1},{2,6},{6,10},{... | collective-permute-start | bytes 1474568 | tf_op jit(solution)/shard_map/ppermute | solution.py:374
  119.9 25.0 %collective-permute-start.38 = (bf16[96,2560]{1,0:T(8,128)(2,1)}, bf16[96,2560]{1,0:T(8,128)(2,1)S(1)}, u32[]{:S(2)}, u32[]{:S(2)}) collective-permute-start(bf16[96,2560]{1,0:T(8,128)(2,1)} %get-tuple-element.73), channel_id=1, source_target_pairs={{0,8},{4,12},{8,0},{12,4},{1,9},{5,13},{9,1},{13,5},{2,10},{6,14},... | collective-permute-start | bytes 1474568 | tf_op jit(solution)/shard_map/ppermute | solution.py:374
  122.9 21.9 %collective-permute-start.39 = (bf16[96,2560]{1,0:T(8,128)(2,1)}, bf16[96,2560]{1,0:T(8,128)(2,1)S(1)}, u32[]{:S(2)}, u32[]{:S(2)}) collective-permute-start(bf16[96,2560]{1,0:T(8,128)(2,1)} %get-tuple-element.74), channel_id=1, source_target_pairs={{0,12},{4,0},{8,4},{12,8},{1,13},{5,1},{9,5},{13,9},{2,14},{6,2},{... | collective-permute-start | bytes 1474568 | tf_op jit(solution)/shard_map/ppermute | solution.py:374
  123.7 23.2 %copy-start.2 = (bf16[128,2560]{1,0:T(8,128)(2,1)}, bf16[128,2560]{1,0:T(8,128)(2,1)S(1)}, u32[]{:S(2)}) copy-start(bf16[128,2560]{1,0:T(8,128)(2,1)S(1)} %collective-permute-done.13.refs_6_) | copy-start | bytes 1966084
  123.8 40.1 %collective-permute-start.11 = (bf16[128,2560]{1,0:T(8,128)(2,1)S(1)}, bf16[128,2560]{1,0:T(8,128)(2,1)S(1)}, u32[]{:S(2)}, u32[]{:S(2)}) collective-permute-start(bf16[128,2560]{1,0:T(8,128)(2,1)S(1)} %collective-permute-done.9.refs_2_), channel_id=1, source_target_pairs={{0,16},{16,0},{32,48},{48,32},{64,80},{80,64},{96,112},{112,96},{1... | collective-permute-start | bytes 1966088 | tf_op jit(solution)/shard_map/ppermute | solution.py:329
  125.8 21.1 %copy-start.3 = (bf16[128,2560]{1,0:T(8,128)(2,1)}, bf16[128,2560]{1,0:T(8,128)(2,1)S(1)}, u32[]{:S(2)}) copy-start(bf16[128,2560]{1,0:T(8,128)(2,1)S(1)} %collective-permute-done.10.refs_3_) | copy-start | bytes 1966084
  125.8 41.4 %collective-permute-start.14 = (bf16[128,2560]{1,0:T(8,128)(2,1)S(1)}, bf16[128,2560]{1,0:T(8,128)(2,1)S(1)}, u32[]{:S(2)}, u32[]{:S(2)}) collective-permute-start(bf16[128,2560]{1,0:T(8,128)(2,1)S(1)} %collective-permute-done.13.refs_6_), channel_id=1, source_target_pairs={{0,16},{16,0},{32,48},{48,32},{64,80},{80,64},{96,112},{112,96},{1... | collective-permute-start | bytes 1966088 | tf_op jit(solution)/shard_map/ppermute | solution.py:329
  133.4 33.8 %collective-permute-start.12 = (bf16[128,2560]{1,0:T(8,128)(2,1)S(1)}, bf16[128,2560]{1,0:T(8,128)(2,1)}, u32[]{:S(2)}, u32[]{:S(2)}) collective-permute-start(bf16[128,2560]{1,0:T(8,128)(2,1)S(1)} %collective-permute-done.10.refs_3_), channel_id=1, source_target_pairs={{0,16},{16,0},{32,48},{48,32},{64,80},{80,64},{96,112},{112,96},{1... | collective-permute-start | bytes 1966088 | tf_op jit(solution)/shard_map/ppermute | solution.py:329
  147.0 32.1 %collective-permute-start.40 = (bf16[24,2560]{1,0:T(8,128)(2,1)}, bf16[24,2560]{1,0:T(8,128)(2,1)S(1)}, u32[]{:S(2)}, u32[]{:S(2)}) collective-permute-start(bf16[24,2560]{1,0:T(8,128)(2,1)} %get-tuple-element.80), channel_id=1, source_target_pairs={{0,1},{1,2},{2,3},{3,0},{4,5},{5,6},{6,7},{7,4},{8,9},{9,10},{10,1... | collective-permute-start | bytes 368648 | tf_op jit(solution)/shard_map/ppermute | solution.py:374
  152.0 51.4 %collective-permute-start.41 = (bf16[24,2560]{1,0:T(8,128)(2,1)}, bf16[24,2560]{1,0:T(8,128)(2,1)S(1)}, u32[]{:S(2)}, u32[]{:S(2)}) collective-permute-start(bf16[24,2560]{1,0:T(8,128)(2,1)} %get-tuple-element.82), channel_id=1, source_target_pairs={{0,2},{1,3},{2,0},{3,1},{4,6},{5,7},{6,4},{7,5},{8,10},{9,11},{10,... | collective-permute-start | bytes 368648 | tf_op jit(solution)/shard_map/ppermute | solution.py:374
  163.8 42.6 %collective-permute-start.42 = (bf16[24,2560]{1,0:T(8,128)(2,1)S(1)}, bf16[24,2560]{1,0:T(8,128)(2,1)S(1)}, u32[]{:S(2)}, u32[]{:S(2)}) collective-permute-start(bf16[24,2560]{1,0:T(8,128)(2,1)S(1)} %copy-done.24), channel_id=1, source_target_pairs={{0,3},{1,0},{2,1},{3,2},{4,7},{5,4},{6,5},{7,6},{8,11},{9,8},{10,9... | collective-permute-start | bytes 368648 | tf_op jit(solution)/shard_map/ppermute | solution.py:374
  175.7 43.6 %collective-permute-start.43 = (bf16[96,2560]{1,0:T(8,128)(2,1)}, bf16[96,2560]{1,0:T(8,128)(2,1)S(1)}, u32[]{:S(2)}, u32[]{:S(2)}) collective-permute-start(bf16[96,2560]{1,0:T(8,128)(2,1)} %get-tuple-element.75), channel_id=1, source_target_pairs={{0,4},{4,8},{8,12},{12,0},{1,5},{5,9},{9,13},{13,1},{2,6},{6,10},{... | collective-permute-start | bytes 1474568 | tf_op jit(solution)/shard_map/ppermute | solution.py:374
  176.5 44.3 %collective-permute-start.44 = (bf16[96,2560]{1,0:T(8,128)(2,1)}, bf16[96,2560]{1,0:T(8,128)(2,1)S(1)}, u32[]{:S(2)}, u32[]{:S(2)}) collective-permute-start(bf16[96,2560]{1,0:T(8,128)(2,1)} %get-tuple-element.76), channel_id=1, source_target_pairs={{0,8},{4,12},{8,0},{12,4},{1,9},{5,13},{9,1},{13,5},{2,10},{6,14},... | collective-permute-start | bytes 1474568 | tf_op jit(solution)/shard_map/ppermute | solution.py:374
  179.2 44.1 %collective-permute-start.45 = (bf16[96,2560]{1,0:T(8,128)(2,1)}, bf16[96,2560]{1,0:T(8,128)(2,1)S(1)}, u32[]{:S(2)}, u32[]{:S(2)}) collective-permute-start(bf16[96,2560]{1,0:T(8,128)(2,1)} %get-tuple-element.77), channel_id=1, source_target_pairs={{0,12},{4,0},{8,4},{12,8},{1,13},{5,1},{9,5},{13,9},{2,14},{6,2},{... | collective-permute-start | bytes 1474568 | tf_op jit(solution)/shard_map/ppermute | solution.py:374
  203.5 14.2 %collective-permute-start.23 = (bf16[3,128,128]{2,1,0:T(8,128)(2,1)}, bf16[3,128,128]{2,1,0:T(8,128)(2,1)S(1)}, u32[]{:S(2)}, u32[]{:S(2)}) collective-permute-start(bf16[3,128,128]{2,1,0:T(8,128)(2,1)} %get-tuple-element.54), channel_id=1, source_target_pairs={{0,16},{16,0},{32,48},{48,32},{64,80},{80,64},{96,112},{112,96},{1... | collective-permute-start | bytes 294920 | tf_op jit(solution)/shard_map/ppermute | solution.py:369
  206.4 12.3 %collective-permute-start.24 = (bf16[3,128,128]{2,1,0:T(8,128)(2,1)}, bf16[3,128,128]{2,1,0:T(8,128)(2,1)S(1)}, u32[]{:S(2)}, u32[]{:S(2)}) collective-permute-start(bf16[3,128,128]{2,1,0:T(8,128)(2,1)} %get-tuple-element.55), channel_id=1, source_target_pairs={{0,96},{16,48},{32,0},{48,80},{64,32},{80,112},{96,64},{112,16},{1... | collective-permute-start | bytes 294920 | tf_op jit(solution)/shard_map/ppermute | solution.py:369
  207.2 16.1 %copy-start.39 = (bf16[3,128,128]{2,1,0:T(8,128)(2,1)S(1)}, bf16[3,128,128]{2,1,0:T(8,128)(2,1)}, u32[]{:S(2)}) copy-start(bf16[3,128,128]{2,1,0:T(8,128)(2,1)} %get-tuple-element.60) | copy-start | bytes 294916
  207.2 16.8 %copy-start.7 = (bf16[96,2560]{1,0:T(8,128)(2,1)S(1)}, bf16[96,2560]{1,0:T(8,128)(2,1)}, u32[]{:S(2)}) copy-start(bf16[96,2560]{1,0:T(8,128)(2,1)} %get-tuple-element.52.refs_9_) | copy-start | bytes 1474564
  217.7 6.6 %collective-permute-start.25 = (bf16[3,128,128]{2,1,0:T(8,128)(2,1)S(1)}, bf16[3,128,128]{2,1,0:T(8,128)(2,1)S(1)}, u32[]{:S(2)}, u32[]{:S(2)}) collective-permute-start(bf16[3,128,128]{2,1,0:T(8,128)(2,1)S(1)} %copy-done.43), channel_id=1, source_target_pairs={{0,112},{16,32},{32,16},{48,64},{64,48},{80,96},{96,80},{112,0},{1... | collective-permute-start | bytes 294920 | tf_op jit(solution)/shard_map/ppermute | solution.py:369
  218.7 5.9 %collective-permute-start.26 = (bf16[3,128,128]{2,1,0:T(8,128)(2,1)S(1)}, bf16[3,128,128]{2,1,0:T(8,128)(2,1)S(1)}, u32[]{:S(2)}, u32[]{:S(2)}) collective-permute-start(bf16[3,128,128]{2,1,0:T(8,128)(2,1)S(1)} %copy-done.42), channel_id=1, source_target_pairs={{0,48},{16,96},{32,80},{48,0},{64,112},{80,32},{96,16},{112,64},{1... | collective-permute-start | bytes 294920 | tf_op jit(solution)/shard_map/ppermute | solution.py:369
  219.3 6.4 %collective-permute-start.27 = (bf16[3,128,128]{2,1,0:T(8,128)(2,1)S(1)}, bf16[3,128,128]{2,1,0:T(8,128)(2,1)S(1)}, u32[]{:S(2)}, u32[]{:S(2)}) collective-permute-start(bf16[3,128,128]{2,1,0:T(8,128)(2,1)S(1)} %copy-done.41), channel_id=1, source_target_pairs={{0,32},{16,112},{32,64},{48,16},{64,96},{80,48},{96,0},{112,80},{1... | collective-permute-start | bytes 294920 | tf_op jit(solution)/shard_map/ppermute | solution.py:369
  220.8 6.3 %collective-permute-start.28 = (bf16[3,128,128]{2,1,0:T(8,128)(2,1)S(1)}, bf16[3,128,128]{2,1,0:T(8,128)(2,1)S(1)}, u32[]{:S(2)}, u32[]{:S(2)}) collective-permute-start(bf16[3,128,128]{2,1,0:T(8,128)(2,1)S(1)} %copy-done.40), channel_id=1, source_target_pairs={{0,64},{16,80},{32,96},{48,112},{64,0},{80,16},{96,32},{112,48},{1... | collective-permute-start | bytes 294920 | tf_op jit(solution)/shard_map/ppermute | solution.py:369
  223.3 6.7 %collective-permute-start.29 = (bf16[3,128,128]{2,1,0:T(8,128)(2,1)S(1)}, bf16[3,128,128]{2,1,0:T(8,128)(2,1)S(1)}, u32[]{:S(2)}, u32[]{:S(2)}) collective-permute-start(bf16[3,128,128]{2,1,0:T(8,128)(2,1)S(1)} %copy-done.39), channel_id=1, source_target_pairs={{0,80},{16,64},{32,112},{48,96},{64,16},{80,0},{96,48},{112,32},{1... | collective-permute-start | bytes 294920 | tf_op jit(solution)/shard_map/ppermute | solution.py:369
  224.3 22.6 %copy-start.27 = (bf16[3,128,128]{2,1,0:T(8,128)(2,1)}, bf16[3,128,128]{2,1,0:T(8,128)(2,1)S(1)}, u32[]{:S(2)}) copy-start(bf16[3,128,128]{2,1,0:T(8,128)(2,1)S(1)} %collective-permute-done.25.refs_3_) | copy-start | bytes 294916
  224.3 6.9 %collective-permute-start.30 = (bf16[3,128,256]{2,1,0:T(8,128)(2,1)S(1)}, bf16[3,128,256]{2,1,0:T(8,128)(2,1)S(1)}, u32[]{:S(2)}, u32[]{:S(2)}) collective-permute-start(bf16[3,128,256]{2,1,0:T(8,128)(2,1)S(1)} %copy-done.38), channel_id=1, source_target_pairs={{0,16},{16,0},{32,48},{48,32},{64,80},{80,64},{96,112},{112,96},{1... | collective-permute-start | bytes 589832 | tf_op jit(solution)/shard_map/ppermute | solution.py:369
  224.6 22.3 %copy-start.28 = (bf16[3,128,128]{2,1,0:T(8,128)(2,1)}, bf16[3,128,128]{2,1,0:T(8,128)(2,1)S(1)}, u32[]{:S(2)}) copy-start(bf16[3,128,128]{2,1,0:T(8,128)(2,1)S(1)} %collective-permute-done.26.refs_4_) | copy-start | bytes 294916
  224.6 7.7 %collective-permute-start.31 = (bf16[3,128,256]{2,1,0:T(8,128)(2,1)S(1)}, bf16[3,128,256]{2,1,0:T(8,128)(2,1)S(1)}, u32[]{:S(2)}, u32[]{:S(2)}) collective-permute-start(bf16[3,128,256]{2,1,0:T(8,128)(2,1)S(1)} %copy-done.37), channel_id=1, source_target_pairs={{0,96},{16,48},{32,0},{48,80},{64,32},{80,112},{96,64},{112,16},{1... | collective-permute-start | bytes 589832 | tf_op jit(solution)/shard_map/ppermute | solution.py:369
  225.8 21.1 %copy-start.29 = (bf16[3,128,128]{2,1,0:T(8,128)(2,1)}, bf16[3,128,128]{2,1,0:T(8,128)(2,1)S(1)}, u32[]{:S(2)}) copy-start(bf16[3,128,128]{2,1,0:T(8,128)(2,1)S(1)} %collective-permute-done.27.refs_5_) | copy-start | bytes 294916
  225.8 9.7 %collective-permute-start.32 = (bf16[3,128,256]{2,1,0:T(8,128)(2,1)S(1)}, bf16[3,128,256]{2,1,0:T(8,128)(2,1)S(1)}, u32[]{:S(2)}, u32[]{:S(2)}) collective-permute-start(bf16[3,128,256]{2,1,0:T(8,128)(2,1)S(1)} %copy-done.36), channel_id=1, source_target_pairs={{0,112},{16,32},{32,16},{48,64},{64,48},{80,96},{96,80},{112,0},{1... | collective-permute-start | bytes 589832 | tf_op jit(solution)/shard_map/ppermute | solution.py:369
  227.1 19.8 %copy-start.30 = (bf16[3,128,128]{2,1,0:T(8,128)(2,1)}, bf16[3,128,128]{2,1,0:T(8,128)(2,1)S(1)}, u32[]{:S(2)}) copy-start(bf16[3,128,128]{2,1,0:T(8,128)(2,1)S(1)} %collective-permute-done.28.refs_6_) | copy-start | bytes 294916
  227.1 9.0 %collective-permute-start.33 = (bf16[3,128,256]{2,1,0:T(8,128)(2,1)S(1)}, bf16[3,128,256]{2,1,0:T(8,128)(2,1)S(1)}, u32[]{:S(2)}, u32[]{:S(2)}) collective-permute-start(bf16[3,128,256]{2,1,0:T(8,128)(2,1)S(1)} %copy-done.35), channel_id=1, source_target_pairs={{0,48},{16,96},{32,80},{48,0},{64,112},{80,32},{96,16},{112,64},{1... | collective-permute-start | bytes 589832 | tf_op jit(solution)/shard_map/ppermute | solution.py:369
  230.0 16.9 %copy-start.31 = (bf16[3,128,128]{2,1,0:T(8,128)(2,1)}, bf16[3,128,128]{2,1,0:T(8,128)(2,1)S(1)}, u32[]{:S(2)}) copy-start(bf16[3,128,128]{2,1,0:T(8,128)(2,1)S(1)} %collective-permute-done.29.refs_7_) | copy-start | bytes 294916
  230.0 15.2 %collective-permute-start.34 = (bf16[3,128,256]{2,1,0:T(8,128)(2,1)S(1)}, bf16[3,128,256]{2,1,0:T(8,128)(2,1)S(1)}, u32[]{:S(2)}, u32[]{:S(2)}) collective-permute-start(bf16[3,128,256]{2,1,0:T(8,128)(2,1)S(1)} %copy-done.34), channel_id=1, source_target_pairs={{0,32},{16,112},{32,64},{48,16},{64,96},{80,48},{96,0},{112,80},{1... | collective-permute-start | bytes 589832 | tf_op jit(solution)/shard_map/ppermute | solution.py:369
  231.2 15.7 %copy-start.17 = (bf16[3,128,256]{2,1,0:T(8,128)(2,1)}, bf16[3,128,256]{2,1,0:T(8,128)(2,1)S(1)}, u32[]{:S(2)}) copy-start(bf16[3,128,256]{2,1,0:T(8,128)(2,1)S(1)} %collective-permute-done.30.refs_9_) | copy-start | bytes 589828
  231.2 15.0 %collective-permute-start.35 = (bf16[3,128,256]{2,1,0:T(8,128)(2,1)S(1)}, bf16[3,128,256]{2,1,0:T(8,128)(2,1)S(1)}, u32[]{:S(2)}, u32[]{:S(2)}) collective-permute-start(bf16[3,128,256]{2,1,0:T(8,128)(2,1)S(1)} %copy-done.33), channel_id=1, source_target_pairs={{0,64},{16,80},{32,96},{48,112},{64,0},{80,16},{96,32},{112,48},{1... | collective-permute-start | bytes 589832 | tf_op jit(solution)/shard_map/ppermute | solution.py:369
  232.3 14.6 %collective-permute-start.36 = (bf16[3,128,256]{2,1,0:T(8,128)(2,1)S(1)}, bf16[3,128,256]{2,1,0:T(8,128)(2,1)S(1)}, u32[]{:S(2)}, u32[]{:S(2)}) collective-permute-start(bf16[3,128,256]{2,1,0:T(8,128)(2,1)S(1)} %copy-done.32), channel_id=1, source_target_pairs={{0,80},{16,64},{32,112},{48,96},{64,16},{80,0},{96,48},{112,32},{1... | collective-permute-start | bytes 589832 | tf_op jit(solution)/shard_map/ppermute | solution.py:369
  235.5 16.2 %collective-permute-start.46 = (bf16[24,2560]{1,0:T(8,128)(2,1)S(1)}, bf16[24,2560]{1,0:T(8,128)(2,1)S(1)}, u32[]{:S(2)}, u32[]{:S(2)}) collective-permute-start(bf16[24,2560]{1,0:T(8,128)(2,1)S(1)} %get-tuple-element.83), channel_id=1, source_target_pairs={{0,1},{1,2},{2,3},{3,0},{4,5},{5,6},{6,7},{7,4},{8,9},{9,10},{10,1... | collective-permute-start | bytes 368648 | tf_op jit(solution)/shard_map/ppermute | solution.py:374
  236.1 15.6 %collective-permute-start.47 = (bf16[24,2560]{1,0:T(8,128)(2,1)S(1)}, bf16[24,2560]{1,0:T(8,128)(2,1)S(1)}, u32[]{:S(2)}, u32[]{:S(2)}) collective-permute-start(bf16[24,2560]{1,0:T(8,128)(2,1)S(1)} %get-tuple-element.85), channel_id=1, source_target_pairs={{0,2},{1,3},{2,0},{3,1},{4,6},{5,7},{6,4},{7,5},{8,10},{9,11},{10,... | collective-permute-start | bytes 368648 | tf_op jit(solution)/shard_map/ppermute | solution.py:374
  245.2 6.7 %collective-permute-start.48 = (bf16[24,2560]{1,0:T(8,128)(2,1)S(1)}, bf16[24,2560]{1,0:T(8,128)(2,1)S(1)}, u32[]{:S(2)}, u32[]{:S(2)}) collective-permute-start(bf16[24,2560]{1,0:T(8,128)(2,1)S(1)} %get-tuple-element.84), channel_id=1, source_target_pairs={{0,3},{1,0},{2,1},{3,2},{4,7},{5,4},{6,5},{7,6},{8,11},{9,8},{10,9... | collective-permute-start | bytes 368648 | tf_op jit(solution)/shard_map/ppermute | solution.py:374
  (30 other events, 236.4 us)
Sparse Core Ops, SparseCore 0:
  10.5 83.5 all-gather.2

commit v2 on v0

v2 whole, which is shorter than its diff:
```python
import functools

import jax
import jax.numpy as jnp
from jax import lax
from jax.experimental import pallas as pl
from jax.experimental.pallas import tpu as pltpu
from jax.sharding import Mesh, PartitionSpec as P

HD = 128
XS, CS, YS, ZS = 4, 2, 4, 4
RANKS = XS * CS
TOK = 128
SEQ = RANKS * TOK
NH = 3
WIDTH = NH * HD
D = 5120
TILE = 1024
SCALE = HD**-0.5
LOG2E = 1.4426950408889634
F32 = jnp.float32
BF16 = jnp.bfloat16
NT = (((1,), (1,)), ((), ()))
NN = (((1,), (0,)), ((), ()))
CHUNKS = (3072, 2048)
STARTS = tuple(sum(CHUNKS[:i]) for i in range(len(CHUNKS)))
ROW = WIDTH // (YS * ZS)
VMEM_LIMIT = 56 * 1024 * 1024


def dot(a, b, dims=NN):
    return lax.dot_general(a, b, dims, preferred_element_type=F32)


def params(**more):
    return pltpu.CompilerParams(vmem_limit_bytes=VMEM_LIMIT, **more)


def cost(flops, nbytes, trans=0):
    return pl.CostEstimate(flops=flops, bytes_accessed=nbytes, transcendentals=trans)


def hbm(count):
    return [pl.BlockSpec(memory_space=pl.ANY)] * count


def pack_body(q_ref, k_ref, v_ref, out_ref):
    for r in range(RANKS):
        for i, ref in enumerate((q_ref, k_ref, v_ref)):
            out_ref[r, i] = ref[:, r * WIDTH : (r + 1) * WIDTH]


def pack(q, k, v):
    whole = pl.BlockSpec((TOK, RANKS * WIDTH), lambda j: (0, 0))
    return pl.pallas_call(
        pack_body,
        grid=(1,),
        in_specs=[whole] * 3,
        out_specs=pl.BlockSpec((RANKS, 3, TOK, WIDTH), lambda j: (0, 0, 0, 0)),
        out_shape=jax.ShapeDtypeStruct((RANKS, 3, TOK, WIDTH), BF16),
        compiler_params=params(),
        cost_estimate=cost(0, 2 * 3 * 2 * SEQ * WIDTH),
        name="pack",
    )(q, k, v)


def unpack_body(home_ref, *outs):
    for r in range(RANKS):
        for i, out in enumerate(outs):
            out[:, r * WIDTH : (r + 1) * WIDTH] = home_ref[r, i]


def unpack(home):
    whole = pl.BlockSpec((TOK, RANKS * WIDTH), lambda j: (0, 0))
    return pl.pallas_call(
        unpack_body,
        grid=(1,),
        in_specs=[pl.BlockSpec(home.shape, lambda j: (0, 0, 0, 0))],
        out_specs=[whole] * 3,
        out_shape=[jax.ShapeDtypeStruct((TOK, RANKS * WIDTH), BF16)] * 3,
        compiler_params=params(),
        cost_estimate=cost(0, 2 * 3 * 2 * SEQ * WIDTH),
        name="unpack",
    )(home)


def gate_body(gate_ref, mine_ref, other_ref, *refs):
    out_ref = refs[-1]
    total = mine_ref[...].astype(F32) + other_ref[...].astype(F32)
    out_ref[...] = (gate_ref[...] * total).astype(BF16)


def gated(gate, cot, other, start, after=()):
    wide = other.shape[1]
    at = start // TILE
    return pl.pallas_call(
        gate_body,
        grid=(wide // TILE,),
        in_specs=[
            pl.BlockSpec((1, TILE), lambda j: (0, j + at)),
            pl.BlockSpec((TOK, TILE), lambda j: (0, j + at)),
            pl.BlockSpec((TOK, TILE), lambda j: (0, j)),
        ]
        + hbm(len(after)),
        out_specs=pl.BlockSpec((TOK, TILE), lambda j: (0, j)),
        out_shape=jax.ShapeDtypeStruct((TOK, wide), BF16),
        compiler_params=params(),
        cost_estimate=cost(2 * TOK * wide, 6 * TOK * wide),
        name="gated",
    )(gate, cot, other, *after)


def forward_body(slot_ref, qkv_ref, *refs):
    prob_ref, att_ref, q_s, k_s, vt_s = refs[-5:]
    for s in range(RANKS):
        rows = pl.ds(s * TOK, TOK)
        piece = slot_ref[s]
        q_s[rows, :] = qkv_ref[piece, 0]
        k_s[rows, :] = qkv_ref[piece, 1]
        vt_s[:, rows] = qkv_ref[piece, 2].astype(F32).T.astype(BF16)
    scores = dot(k_s[...], q_s[...], NT)
    top = jnp.max(scores, axis=0, keepdims=True)
    e = jnp.exp2((scores - top) * (SCALE * LOG2E))
    norm = 1.0 / jnp.sum(e, axis=0, keepdims=True)
    prob = (e * norm).astype(BF16)
    prob_ref[0] = prob
    att_ref[...] = dot(vt_s[...], prob).astype(BF16)


def forward(slots, qkv, after=()):
    return pl.pallas_call(
        forward_body,
        grid_spec=pltpu.PrefetchScalarGridSpec(
            num_scalar_prefetch=1,
            grid=(NH,),
            in_specs=[pl.BlockSpec((RANKS, 3, TOK, HD), lambda h, s: (0, 0, 0, h))] + hbm(len(after)),
            out_specs=[
                pl.BlockSpec((1, SEQ, SEQ), lambda h, s: (h, 0, 0)),
                pl.BlockSpec((HD, SEQ), lambda h, s: (h, 0)),
            ],
            scratch_shapes=[
                pltpu.VMEM((SEQ, HD), BF16),
                pltpu.VMEM((SEQ, HD), BF16),
                pltpu.VMEM((HD, SEQ), BF16),
            ],
        ),
        out_shape=[
            jax.ShapeDtypeStruct((NH, SEQ, SEQ), BF16),
            jax.ShapeDtypeStruct((WIDTH, SEQ), BF16),
        ],
        compiler_params=params(),
        cost_estimate=cost(4 * NH * SEQ * SEQ * HD, 2 * NH * SEQ * SEQ + 8 * SEQ * WIDTH, NH * SEQ * SEQ),
        name="forward",
    )(slots, qkv, *after)


def backward_body(slot_ref, qkv_ref, prob_ref, gt_ref, att_ref, *refs):
    out_ref, q_s, v_s, kt_s = refs[-4:]
    for s in range(RANKS):
        rows = pl.ds(s * TOK, TOK)
        piece = slot_ref[s]
        q_s[rows, :] = qkv_ref[piece, 0]
        kt_s[:, rows] = qkv_ref[piece, 1].astype(F32).T.astype(BF16)
        v_s[rows, :] = qkv_ref[piece, 2]
    gt = gt_ref[...]
    prob = prob_ref[0]
    delta = jnp.sum(gt.astype(F32) * att_ref[...].astype(F32), axis=0, keepdims=True)
    dprob = dot(v_s[...], gt)
    dscore = (prob.astype(F32) * ((dprob - delta) * SCALE)).astype(BF16)
    grads = (
        dot(kt_s[...], dscore).T.astype(BF16),
        dot(dscore, q_s[...]).astype(BF16),
        dot(prob, gt, NT).astype(BF16),
    )
    for s in range(RANKS):
        for i, grad in enumerate(grads):
            out_ref[slot_ref[s], i] = grad[s * TOK : (s + 1) * TOK]


def backward(slots, qkv, prob, gt, att):
    return pl.pallas_call(
        backward_body,
        grid_spec=pltpu.PrefetchScalarGridSpec(
            num_scalar_prefetch=1,
            grid=(NH,),
            in_specs=[
                pl.BlockSpec((RANKS, 3, TOK, HD), lambda h, s: (0, 0, 0, h)),
                pl.BlockSpec((1, SEQ, SEQ), lambda h, s: (h, 0, 0)),
                pl.BlockSpec((HD, SEQ), lambda h, s: (h, 0)),
                pl.BlockSpec((HD, SEQ), lambda h, s: (h, 0)),
            ],
            out_specs=pl.BlockSpec((RANKS, 3, TOK, HD), lambda h, s: (0, 0, 0, h)),
            scratch_shapes=[
                pltpu.VMEM((SEQ, HD), BF16),
                pltpu.VMEM((SEQ, HD), BF16),
                pltpu.VMEM((HD, SEQ), BF16),
            ],
        ),
        out_shape=jax.ShapeDtypeStruct((RANKS, 3, TOK, WIDTH), BF16),
        compiler_params=params(),
        cost_estimate=cost(8 * NH * SEQ * SEQ * HD, 2 * NH * SEQ * (SEQ + 8 * HD)),
        name="backward",
    )(slots, qkv, prob, gt, att)


def row_specs(pieces, index):
    return [pl.BlockSpec((p.shape[0], TILE), index) for p in pieces]


def weight_body(parts, at_ref, att_ref, *refs):
    outs, wide_s, att_s = refs[-2 - YS : -2], refs[-2], refs[-1]
    block, row = WIDTH // YS, WIDTH // (YS * ZS)

    @pl.when(pl.program_id(0) == 0)
    def _():
        wide_s[...] = att_ref[...].astype(F32)
        for i in range(YS * ZS):
            start = pl.multiple_of(at_ref[i] * row, 8)
            att_s[pl.ds(i * row, row), :] = wide_s[pl.ds(start, row), :]

    rows = jnp.concatenate([ref[...] for ref in refs[:parts]], axis=0)
    term = dot(att_s[...].astype(BF16), rows).astype(BF16)
    for i, out in enumerate(outs):
        out[...] = term[i * block : (i + 1) * block]


def weight_grad(order, att, pieces, after=()):
    wide = pieces[0].shape[1]
    block = WIDTH // YS
    return pl.pallas_call(
        functools.partial(weight_body, len(pieces)),
        grid_spec=pltpu.PrefetchScalarGridSpec(
            num_scalar_prefetch=1,
            grid=(wide // TILE,),
            in_specs=[pl.BlockSpec((WIDTH, SEQ), lambda j, o: (0, 0))] + row_specs(pieces, lambda j, o: (0, j)) + hbm(len(after)),
            out_specs=[pl.BlockSpec((block, TILE), lambda j, o: (0, j))] * YS,
            scratch_shapes=[pltpu.VMEM((WIDTH, SEQ), F32), pltpu.VMEM((WIDTH, SEQ), F32)],
        ),
        out_shape=[jax.ShapeDtypeStruct((block, wide), BF16)] * YS,
        compiler_params=params(),
        cost_estimate=cost(2 * WIDTH * SEQ * wide, 2 * (WIDTH * SEQ + SEQ * wide + WIDTH * wide)),
        name="weight_grad",
    )(order, att, *pieces, *after)


def heads_body(count, parts, carry, from_ref, w_ref, *refs):
    acc_s, out_s = refs[-2:]
    out_ref = refs[-3]
    step = pl.program_id(0)

    @pl.when(step == 0)
    def _():
        acc_s[...] = refs[parts][...] if carry else jnp.zeros_like(acc_s)

    rows = jnp.concatenate([ref[...] for ref in refs[:parts]], axis=0)
    acc_s[...] += dot(w_ref[...], rows, NT)

    @pl.when(step == count - 1)
    def _():
        if carry:
            for i in range(YS * ZS):
                start = pl.multiple_of(from_ref[i] * ROW, 8)
                out_s[pl.ds(start, ROW), :] = acc_s[pl.ds(i * ROW, ROW), :]
            out_ref[...] = out_s[...].astype(BF16)
        else:
            out_ref[...] = acc_s[...]


def heads_grad(come, weights, offset, pieces, carry=None, after=()):
    wide = pieces[0].shape[1]
    count = wide // TILE
    first = offset // TILE
    whole = pl.BlockSpec((WIDTH, SEQ), lambda j, o: (0, 0))
    extra = [] if carry is None else [carry]
    return pl.pallas_call(
        functools.partial(heads_body, count, len(pieces), carry is not None),
        grid_spec=pltpu.PrefetchScalarGridSpec(
            num_scalar_prefetch=1,
            grid=(count,),
            in_specs=[pl.BlockSpec((WIDTH, TILE), lambda j, o: (0, j + first))]
            + row_specs(pieces, lambda j, o: (0, j))
            + [whole] * len(extra)
            + hbm(len(after)),
            out_specs=whole,
            scratch_shapes=[pltpu.VMEM((WIDTH, SEQ), F32), pltpu.VMEM((WIDTH, SEQ), F32)],
        ),
        out_shape=jax.ShapeDtypeStruct((WIDTH, SEQ), F32 if carry is None else BF16),
        compiler_params=params(),
        cost_estimate=cost(2 * WIDTH * SEQ * wide, 2 * (WIDTH * SEQ + SEQ * wide + WIDTH * wide)),
        name="heads_grad",
    )(come, weights, *pieces, *extra, *after)


def rank(x, c):
    return (x % XS) * CS + c


ONWARD = [(rank(x, c), rank(x + 1 - 2 * c, c)) for x in range(XS) for c in range(CS)]
SIBLING = [(rank(x, c), rank(x, 1 - c)) for x in range(XS) for c in range(CS)]


def send(value, perm):
    return lax.ppermute(value, ("x", "c"), perm)


def hold_body(*refs):
    pass


def hold(value, *after):
    return pl.pallas_call(
        hold_body,
        in_specs=hbm(1 + len(after)),
        out_specs=hbm(1)[0],
        out_shape=jax.ShapeDtypeStruct(value.shape, value.dtype),
        input_output_aliases={0: 0},
        compiler_params=params(),
        cost_estimate=cost(0, 0),
        name="hold",
    )(value, *after)


def slot_table():
    x, c = lax.axis_index("x"), lax.axis_index("c")
    step = 1 - 2 * c
    at = lambda xx, cc: lax.rem(xx + 2 * XS, XS) * CS + cc
    return jnp.stack(
        [
            at(x, c),
            at(x, 1 - c),
            at(x - step, c),
            at(x - step, 1 - c),
            at(x + step, 1 - c),
            at(x + step, c),
            at(x + 2, c),
            at(x + 2, 1 - c),
        ]
    ).astype(jnp.int32)


def exchange(value, axis):
    return lax.all_to_all(value, axis, split_axis=0, concat_axis=0, tiled=True)


def clip_order():
    y, z = lax.axis_index("y"), lax.axis_index("z")
    return jnp.stack([(y + i) % YS * ZS + (z + j) % ZS for i in range(YS) for j in range(ZS)]).astype(jnp.int32)


def come_order():
    z = lax.axis_index("z")
    return jnp.stack([i * ZS + (z - j + ZS) % ZS for i in range(YS) for j in range(ZS)]).astype(jnp.int32)


def around(parts, axis, size):
    return [parts[0]] + [
        lax.ppermute(parts[i], axis, [(a, (a + i) % size) for a in range(size)]) for i in range(1, size)
    ]


def total(parts):
    return functools.reduce(jnp.add, [p.astype(F32) for p in parts])


def scatter_sum(parts, *after):
    got = around(parts, "y", YS)
    if after:
        got[1] = hold(got[1], *after)
    part = total(got).astype(BF16)
    return total(around([part[i * ROW : (i + 1) * ROW] for i in range(ZS)], "z", ZS))


def local(queries, keys, values, cotangent, gate, w_out):
    slots = slot_table()
    order, come = clip_order(), come_order()
    cot = cotangent[0, 0]
    to_context = lambda value: lax.ppermute(value, "b", [(0, 1)])

    other0 = to_context(cot[:, : CHUNKS[0]])
    packed = pack(queries[0, 0], keys[0, 0], values[0, 0])
    qkv = exchange(packed, ("x", "c"))
    along_z = around([w_out[0]] * ZS, "z", ZS)
    along_z[1] = hold(along_z[1], other0, qkv)
    along_z = jnp.concatenate(along_z, axis=0)
    weights = lax.all_gather(along_z, "y", axis=0, tiled=True)
    own0 = gated(gate[0], cot, other0, STARTS[0], after=[along_z])
    near0 = send(own0, ONWARD)
    sib0 = send(own0, SIBLING)
    near_sib0 = send(sib0, ONWARD)
    other1 = to_context(hold(cot[:, STARTS[1] :], other0))
    prob, att = forward(slots, qkv, after=[sib0])
    own1 = gated(gate[0], cot, other1, STARTS[1], after=[att])
    near1 = send(own1, ONWARD)
    sib1 = send(own1, SIBLING)
    near_sib1 = send(sib1, ONWARD)
    near0 = hold(near0, sib1)
    far0 = hold(send(near0, ONWARD), near1)
    pieces0 = [own0, sib0, near0, near_sib0, send(near0, SIBLING), send(near_sib0, SIBLING), far0, send(far0, SIBLING)]
    far1 = send(near1, ONWARD)
    first_term = weight_grad(order, att, pieces0)
    acc = heads_grad(come, weights, 0, pieces0, after=[first_term[0]])
    far1 = hold(far1, acc)
    pieces1 = [own1, sib1, near1, near_sib1, send(near1, SIBLING), send(near_sib1, SIBLING), far1, send(far1, SIBLING)]
    gt = heads_grad(come, weights, STARTS[1], pieces1, acc)
    home = backward(slots, qkv, prob, gt, att)
    last_term = weight_grad(order, att, pieces1, after=[home])
    first_sum = scatter_sum(first_term, last_term[0])
    last_sum = scatter_sum(last_term)
    dq, dk, dv = unpack(exchange(home, ("x", "c")))
    return (
        dq[None, None],
        dk[None, None],
        dv[None, None],
        jnp.concatenate([first_sum, last_sum], axis=1)[None],
    )


def solution(mesh):
    fine = Mesh(mesh.devices.reshape(2, XS, CS, YS, ZS), ("b", "x", "c", "y", "z"))
    tokens = P("b", ("y", "z"), ("x", "c"), None)
    weight = P("b", ("x", "c", "y", "z"), None)
    return jax.shard_map(
        local,
        mesh=fine,
        in_specs=(tokens, tokens, tokens, tokens, P("b", ("y", "z"), None), weight),
        out_specs=(tokens, tokens, tokens, weight),
        check_vma=False,
    )
```

time: 276 us -> 233 us (0.84)
  waiting for transfers between devices: 102 us -> 66.4 us
  Pallas kernels: 72.5 us -> 58.6 us
  local copies, waits for them, and re-layouts: 8.2 us -> 17 us
    all_to_all x7 -> x2, waiting for transfers between devices: 60.6 us -> 0.01 us  [exchange(): return lax.all_to_all(value, axis, split_axis=0, concat_axis=0, tiled=True)]
    all_to_all x7 -> x2, starting transfers between devices: 40.2 us -> 11.2 us  [exchange(): return lax.all_to_all(value, axis, split_axis=0, concat_axis=0, tiled=True)]
    ppermute x16 -> x31, starting transfers between devices: 29.3 us -> 57.5 us  [the longest x15 37.5 us: around(): lax.ppermute(parts[i], axis, [(a, (a + i) % size) for a in range(size)])]
    ppermute x16 -> x31, waiting for transfers between devices: 41.7 us -> 66.3 us  [the longest x15 42.4 us: around(): lax.ppermute(parts[i], axis, [(a, (a + i) % size) for a in range(size)])]
    unnamed x18 -> x48, local copies, waits for them, and re-layouts: 5.29 us -> 11.9 us
    pallas_call x2 -> x1, Pallas kernels: 17 us -> 10.5 us  [backward(): pl.pallas_call(backward_body, grid_spec=pltpu.PrefetchScalarGridSpec(num_...]
    pallas_call x1, Pallas kernels: 14.4 us -> 8.97 us  [forward(): pl.pallas_call(forward_body, grid_spec=pltpu.PrefetchScalarGridSpec(num_s...]
    reduce_sum x4 -> x0, other arithmetic: 4.08 us -> none  [the longest x2 3.94 us: scatter_sum(): part = jnp.sum(got.astype(F32), axis=0).astype(BF16)]
  transfers between devices with their start and end apart: 24 -> 34, of which waited for: 13 -> 9; matrix products, arithmetic and copies ran while one was open for 3% -> 4% of each run, Pallas kernels for 24% -> 23%
where the time goes in v2:
time: 233 us; the launch traced here: 230 us
  starting transfers between devices  68.6 us (29%)
  waiting for transfers between devices  66.4 us (28%)
  Pallas kernels  58.6 us (25%)
  local copies, waits for them, and re-layouts  17 us (7%)
  between operations  14.2 us (6%)
  other arithmetic  5.18 us (2%)
    ppermute x15, waiting for transfers between devices, around(): lax.ppermute(parts[i], axis, [(a, (a + i) % size) for a in range(size)])  42.4 us
    ppermute x15, starting transfers between devices, around(): lax.ppermute(parts[i], axis, [(a, (a + i) % size) for a in range(size)])  37.5 us
    ppermute x14, waiting for transfers between devices, send(): return lax.ppermute(value, ('x', 'c'), perm)  24 us
    ppermute x14, starting transfers between devices, send(): return lax.ppermute(value, ('x', 'c'), perm)  16 us
    pallas_call x2, Pallas kernels, heads_grad(): pl.pallas_call(functools.partial(heads_body, count, len(pieces), carry is...  14.1 us
    pallas_call x2, Pallas kernels, weight_grad(): pl.pallas_call(functools.partial(weight_body, len(pieces)), grid_spec=plt...  13.4 us
    unnamed x48, local copies, waits for them, and re-layouts  11.9 us
    all_to_all x2, starting transfers between devices, exchange(): return lax.all_to_all(value, axis, split_axis=0, concat_axis=0, tiled=True)  11.2 us
  transfers between devices with their start and end apart: 34, of which 9 were waited for; matrix products, arithmetic and copies ran while one was open for 4% of the time, Pallas kernels for 23%

profile of v2, /device:TPU:1, one launch (start us, length us, event | category | flops | bytes accessed | tf_op | source)
XLA Modules:
  0.0 230.1 jit_solution(5477140841058087969)
XLA Ops:
  7.2 3.2 %pack.1 = bf16[8,3,128,384]{3,2,1,0:T(8,128)(2,1)} custom-call(bf16[128,3072]{1,0:T(8,128)(2,1)} %bitcast.55, bf16[128,3072]{1,0:T(8,128)(2,1)} %bitcast.56, bf16[128,3072]{1,0:T(8,128)(2,1)} %bitcast.57), custom_call_target="tpu_custom_call" | custom-call | bytes 4718592 | tf_op jit(solution)/shard_map/pack/pallas_call | solution.py:55
  10.4 6.8 %all-to-all-start = ((bf16[8,3,128,384]{3,2,1,0:T(8,128)(2,1)}), bf16[8,3,128,384]{3,2,1,0:T(8,128)(2,1)S(1)}, u32[]{:S(2)}, u32[]{:S(2)}) async-start(bf16[8,3,128,384]{3,2,1,0:T(8,128)(2,1)} %pack.1), calls=%async_computation | async-start | bytes 4718592 | tf_op jit(solution)/shard_map/all_to_all | solution.py:342
  17.1 1.2 slice.40
  18.3 2.6 %collective-permute-start = (bf16[128,3072]{1,0:T(8,128)(2,1)S(1)}, bf16[128,3072]{1,0:T(8,128)(2,1)S(1)}, u32[]{:S(2)}, u32[]{:S(2)}) collective-permute-start(bf16[128,3072]{1,0:T(8,128)(2,1)S(1)} %slice.40), channel_id=1, source_target_pairs={{0,128},{1,129},{2,130},{3,131},{4,132},{5,133},{6,134},{7,135},{8... | collective-permute-start | bytes 2359304 | tf_op jit(solution)/shard_map/ppermute | solution.py:377
  21.0 3.1 %collective-permute-start.1 = (bf16[24,5120]{1,0:T(8,128)(2,1)}, bf16[24,5120]{1,0:T(8,128)(2,1)S(1)}, u32[]{:S(2)}, u32[]{:S(2)}) collective-permute-start(bf16[24,5120]{1,0:T(8,128)(2,1)} %bitcast.58), channel_id=1, source_target_pairs={{0,1},{1,2},{2,3},{3,0},{4,5},{5,6},{6,7},{7,4},{8,9},{9,10},{10,1... | collective-permute-start | bytes 737288 | tf_op jit(solution)/shard_map/ppermute | solution.py:357
  24.0 4.2 %collective-permute-start.2 = (bf16[24,5120]{1,0:T(8,128)(2,1)}, bf16[24,5120]{1,0:T(8,128)(2,1)}, u32[]{:S(2)}, u32[]{:S(2)}) collective-permute-start(bf16[24,5120]{1,0:T(8,128)(2,1)} %bitcast.59), channel_id=1, source_target_pairs={{0,2},{1,3},{2,0},{3,1},{4,6},{5,7},{6,4},{7,5},{8,10},{9,11},{10,... | collective-permute-start | bytes 737288 | tf_op jit(solution)/shard_map/ppermute | solution.py:357
  28.3 2.4 %collective-permute-start.3 = (bf16[24,5120]{1,0:T(8,128)(2,1)}, bf16[24,5120]{1,0:T(8,128)(2,1)}, u32[]{:S(2)}, u32[]{:S(2)}) collective-permute-start(bf16[24,5120]{1,0:T(8,128)(2,1)} %bitcast.60), channel_id=1, source_target_pairs={{0,3},{1,0},{2,1},{3,2},{4,7},{5,4},{6,5},{7,6},{8,11},{9,8},{10,9... | collective-permute-start | bytes 737288 | tf_op jit(solution)/shard_map/ppermute | solution.py:357
  30.6 23.6 %collective-permute-done.1.refs_0_ = bf16[24,5120]{1,0:T(8,128)(2,1)S(1)} collective-permute-done((bf16[24,5120]{1,0:T(8,128)(2,1)}, bf16[24,5120]{1,0:T(8,128)(2,1)S(1)}, u32[]{:S(2)}, u32[]{:S(2)}) %collective-permute-start.1) | collective-permute-done | bytes 245792 | tf_op jit(solution)/shard_map/ppermute | solution.py:357
  54.2 0.7 copy-done.18
  55.2 1.5 copy-done
  56.7 3.9 %collective-permute-done.2 = bf16[24,5120]{1,0:T(8,128)(2,1)} collective-permute-done((bf16[24,5120]{1,0:T(8,128)(2,1)}, bf16[24,5120]{1,0:T(8,128)(2,1)}, u32[]{:S(2)}, u32[]{:S(2)}) %collective-permute-start.2) | collective-permute-done | bytes 245792 | tf_op jit(solution)/shard_map/ppermute | solution.py:357
  60.6 2.2 pad_maximum_fusion.refs_0_
  62.9 3.2 %gated.2.refs_0_ = bf16[128,3072]{1,0:T(8,128)(2,1)} custom-call(f32[1,5120]{1,0:T(1,128)} %bitcast.62, bf16[128,5120]{1,0:T(8,128)(2,1)} %bitcast.52, bf16[128,3072]{1,0:T(8,128)(2,1)} %copy-done.2, bf16[96,5120]{1,0:T(8,128)(2,1)} %pad_maximum_fusion.refs_0_), custom_call_target="tpu_custom_call" | custom-call | flops 786432 | bytes 2359296 | tf_op jit(solution)/shard_map/gated/pallas_call | solution.py:96
  66.1 1.2 collective-permute-start.4
  67.2 1.9 slice.41.refs_0_
  69.1 1.3 collective-permute-start.5
  70.5 2.9 %collective-permute-start.12 = (bf16[128,3072]{1,0:T(8,128)(2,1)S(1)}, bf16[128,3072]{1,0:T(8,128)(2,1)S(1)}, u32[]{:S(2)}, u32[]{:S(2)}) collective-permute-start(bf16[128,3072]{1,0:T(8,128)(2,1)S(1)} %copy-done.8), channel_id=1, source_target_pairs={{0,32},{16,112},{32,64},{48,16},{64,96},{80,48},{96,0},{112,80},{1... | collective-permute-start | bytes 2359304 | tf_op jit(solution)/shard_map/ppermute | solution.py:303
  73.4 0.6 stack.137.slot_ref
  74.0 0.9 copy-done.19
  74.9 9.0 %forward.1 = (bf16[3,1024,1024]{2,1,0:T(8,128)(2,1)}, bf16[384,1024]{1,0:T(8,128)(2,1)}) custom-call(s32[8]{0:T(128)} %stack.137.slot_ref, bf16[8,3,128,384]{3,2,1,0:T(8,128)(2,1)} %copy-done, bf16[128,3072]{1,0:T(8,128)(2,1)} %copy-done.19), custom_call_target="tpu_custom_call" | custom-call | flops 1610612736 | bytes 9437184 | tf_op jit(solution)/shard_map/forward/pallas_call | solution.py:131
  83.9 0.8 copy-done.22
  84.7 2.0 gated.3.refs_0_
  86.7 1.8 collective-permute-start.13
  88.8 0.6 copy-done.9
  89.4 0.8 copy-done.5
  90.2 0.8 collective-permute-start.16
  92.0 6.0 %collective-permute-done.13.refs_3_ = bf16[128,3072]{1,0:T(8,128)(2,1)} collective-permute-done((bf16[128,3072]{1,0:T(8,128)(2,1)S(1)}, bf16[128,3072]{1,0:T(8,128)(2,1)}, u32[]{:S(2)}, u32[]{:S(2)}) %collective-permute-start.13) | collective-permute-done | bytes 786464 | tf_op jit(solution)/shard_map/ppermute | solution.py:303
  98.0 2.5 %collective-permute-start.15 = (bf16[128,3072]{1,0:T(8,128)(2,1)}, bf16[128,3072]{1,0:T(8,128)(2,1)}, u32[]{:S(2)}, u32[]{:S(2)}) collective-permute-start(bf16[128,3072]{1,0:T(8,128)(2,1)} %collective-permute-done.13.refs_3_), channel_id=1, source_target_pairs={{0,16},{16,0},{32,48},{48,32},{64,80},{80,64},{96,112},{112,96},{1... | collective-permute-start | bytes 2359304 | tf_op jit(solution)/shard_map/ppermute | solution.py:303
  100.5 11.6 %collective-permute-done.7.refs_1_.refs_2_ = bf16[128,2048]{1,0:T(8,128)(2,1)S(1)} collective-permute-done((bf16[128,2048]{1,0:T(8,128)(2,1)S(1)}, bf16[128,2048]{1,0:T(8,128)(2,1)S(1)}, u32[]{:S(2)}, u32[]{:S(2)}) %collective-permute-start.7) | collective-permute-done | bytes 524320 | tf_op jit(solution)/shard_map/ppermute | solution.py:303
  112.1 0.8 copy-done.7
  112.8 0.9 copy-done.10
  113.7 2.4 %collective-permute-start.17 = (bf16[128,3072]{1,0:T(8,128)(2,1)}, bf16[128,3072]{1,0:T(8,128)(2,1)S(1)}, u32[]{:S(2)}, u32[]{:S(2)}) collective-permute-start(bf16[128,3072]{1,0:T(8,128)(2,1)} %hold.9.refs_6_), channel_id=1, source_target_pairs={{0,16},{16,0},{32,48},{48,32},{64,80},{80,64},{96,112},{112,96},{1... | collective-permute-start | bytes 2359304 | tf_op jit(solution)/shard_map/ppermute | solution.py:303
  117.0 0.7 stack.171.at_ref
  117.6 0.7 stack.154.from_ref
  118.3 6.1 %collective-permute-done.8.refs_3_ = bf16[128,2048]{1,0:T(8,128)(2,1)S(1)} collective-permute-done((bf16[128,2048]{1,0:T(8,128)(2,1)S(1)}, bf16[128,2048]{1,0:T(8,128)(2,1)S(1)}, u32[]{:S(2)}, u32[]{:S(2)}) %collective-permute-start.8) | collective-permute-done | bytes 524320 | tf_op jit(solution)/shard_map/ppermute | solution.py:303
  124.5 2.1 collective-permute-start.9
  126.6 0.9 copy-done.21
  127.5 7.6 %weight_grad.2 = (bf16[96,3072]{1,0:T(8,128)(2,1)}, bf16[96,3072]{1,0:T(8,128)(2,1)}, bf16[96,3072]{1,0:T(8,128)(2,1)}, bf16[96,3072]{1,0:T(8,128)(2,1)}) custom-call(s32[16]{0:T(128)} %stack.171.at_ref, bf16[384,1024]{1,0:T(8,128)(2,1)} %get-tuple-element.18.refs_0_.att_ref, bf16[128,3072]{1,0:T(8,128)(2,1)} %gated.2.refs_0_, bf16[128,3072]{1,0:T(8,128)(2,1)} %copy-done.19, ...), custom_call_target="tpu_custom_call" | custom-call | flops 2415919104 | bytes 9437184 | tf_op jit(solution)/shard_map/weight_grad/pallas_call | solution.py:230
  135.2 7.6 %heads_grad.2.refs_1_.refs_8_ = f32[384,1024]{1,0:T(8,128)} custom-call(s32[16]{0:T(128)} %stack.154.from_ref, bf16[384,5120]{1,0:T(8,128)(2,1)} %all-gather.2.cloned.1.call-done.w_ref, bf16[128,3072]{1,0:T(8,128)(2,1)} %gated.2.refs_0_, bf16[128,3072]{1,0:T(8,128)(2,1)} %copy-done.19, bf16[128,3072]{1,0:T(8,128)(2,1)} %hold.8.refs_2_, ...), custom_call_target="tpu_custom_call" | custom-call | flops 2415919104 | bytes 9437184 | tf_op jit(solution)/shard_map/heads_grad/pallas_call | solution.py:275
  142.8 0.8 copy-done.3
  144.0 1.3 collective-permute-start.19
  145.3 2.6 %collective-permute-start.20 = (bf16[96,3072]{1,0:T(8,128)(2,1)}, bf16[96,3072]{1,0:T(8,128)(2,1)}, u32[]{:S(2)}, u32[]{:S(2)}) collective-permute-start(bf16[96,3072]{1,0:T(8,128)(2,1)} %get-tuple-element.25), channel_id=1, source_target_pairs={{0,8},{4,12},{8,0},{12,4},{1,9},{5,13},{9,1},{13,5},{2,10},{6,14},... | collective-permute-start | bytes 1769480 | tf_op jit(solution)/shard_map/ppermute | solution.py:357
  147.9 1.1 collective-permute-start.21
  149.0 0.8 copy-done.15
  149.8 0.8 copy-done.16
  150.6 6.5 %heads_grad.3.gt_ref = bf16[384,1024]{1,0:T(8,128)(2,1)} custom-call(s32[16]{0:T(128)} %stack.154.from_ref, bf16[384,5120]{1,0:T(8,128)(2,1)} %all-gather.2.cloned.1.call-done.w_ref, bf16[128,2048]{1,0:T(8,128)(2,1)} %gated.3.refs_0_, bf16[128,2048]{1,0:T(8,128)(2,1)} %copy-done.5, bf16[128,2048]{1,0:T(8,128)(2,1)} %copy-done.7, ...), custom_call_target="tpu_custom_call" | custom-call | flops 1610612736 | bytes 6553600 | tf_op jit(solution)/shard_map/heads_grad/pallas_call | solution.py:275
  157.1 10.5 %backward.1.refs_8_ = bf16[8,3,128,384]{3,2,1,0:T(8,128)(2,1)} custom-call(s32[8]{0:T(128)} %stack.137.slot_ref, bf16[8,3,128,384]{3,2,1,0:T(8,128)(2,1)} %copy-done, bf16[3,1024,1024]{2,1,0:T(8,128)(2,1)} %get-tuple-element.17.prob_ref, bf16[384,1024]{1,0:T(8,128)(2,1)} %heads_grad.3.gt_ref, bf16[384,1024]{1,0:T(8,128)(2,1)} %get-tuple-element.18.refs_0_.att_ref), custom_call_target="tpu_custom_call" | custom-call | flops 3221225472 | bytes 12582912 | tf_op jit(solution)/shard_map/backward/pallas_call | solution.py:181
  167.6 4.4 %all-to-all-start.1 = ((bf16[8,3,128,384]{3,2,1,0:T(8,128)(2,1)}), bf16[8,3,128,384]{3,2,1,0:T(8,128)(2,1)S(1)}, u32[]{:S(2)}, u32[]{:S(2)}) async-start(bf16[8,3,128,384]{3,2,1,0:T(8,128)(2,1)} %backward.1.refs_8_), calls=%async_computation.1 | async-start | bytes 4718592 | tf_op jit(solution)/shard_map/all_to_all | solution.py:342
  172.0 5.8 %weight_grad.3 = (bf16[96,2048]{1,0:T(8,128)(2,1)}, bf16[96,2048]{1,0:T(8,128)(2,1)}, bf16[96,2048]{1,0:T(8,128)(2,1)}, bf16[96,2048]{1,0:T(8,128)(2,1)}) custom-call(s32[16]{0:T(128)} %stack.171.at_ref, bf16[384,1024]{1,0:T(8,128)(2,1)} %get-tuple-element.18.refs_0_.att_ref, bf16[128,2048]{1,0:T(8,128)(2,1)} %gated.3.refs_0_, bf16[128,2048]{1,0:T(8,128)(2,1)} %copy-done.5, ...), custom_call_target="tpu_custom_call" | custom-call | flops 1610612736 | bytes 6553600 | tf_op jit(solution)/shard_map/weight_grad/pallas_call | solution.py:230
  178.3 0.7 collective-permute-start.26
  179.0 1.9 collective-permute-start.27
  181.0 1.8 add_convert_fusion
  182.8 5.8 %collective-permute-start.22 = (bf16[24,3072]{1,0:T(8,128)(2,1)S(1)}, bf16[24,3072]{1,0:T(8,128)(2,1)S(1)}, u32[]{:S(2)}, u32[]{:S(2)}) collective-permute-start(bf16[24,3072]{1,0:T(8,128)(2,1)S(1)} %get-tuple-element.30), channel_id=1, source_target_pairs={{0,1},{1,2},{2,3},{3,0},{4,5},{5,6},{6,7},{7,4},{8,9},{9,10},{10,1... | collective-permute-start | bytes 442376 | tf_op jit(solution)/shard_map/ppermute | solution.py:357
  188.7 1.3 collective-permute-start.23
  189.9 8.5 %collective-permute-done.25 = bf16[96,2048]{1,0:T(8,128)(2,1)S(1)} collective-permute-done((bf16[96,2048]{1,0:T(8,128)(2,1)}, bf16[96,2048]{1,0:T(8,128)(2,1)S(1)}, u32[]{:S(2)}, u32[]{:S(2)}) %collective-permute-start.25) | collective-permute-done | bytes 393248 | tf_op jit(solution)/shard_map/ppermute | solution.py:357
  198.4 4.9 %collective-permute-start.24 = (bf16[24,3072]{1,0:T(8,128)(2,1)S(1)}, bf16[24,3072]{1,0:T(8,128)(2,1)S(1)}, u32[]{:S(2)}, u32[]{:S(2)}) collective-permute-start(bf16[24,3072]{1,0:T(8,128)(2,1)S(1)} %get-tuple-element.31), channel_id=1, source_target_pairs={{0,3},{1,0},{2,1},{3,2},{4,7},{5,4},{6,5},{7,6},{8,11},{9,8},{10,9... | collective-permute-start | bytes 442376 | tf_op jit(solution)/shard_map/ppermute | solution.py:357
  203.6 1.2 collective-permute-start.28
  204.8 3.1 %collective-permute-start.29 = (bf16[24,2048]{1,0:T(8,128)(2,1)S(1)}, bf16[24,2048]{1,0:T(8,128)(2,1)S(1)}, u32[]{:S(2)}, u32[]{:S(2)}) collective-permute-start(bf16[24,2048]{1,0:T(8,128)(2,1)S(1)} %get-tuple-element.35), channel_id=1, source_target_pairs={{0,2},{1,3},{2,0},{3,1},{4,6},{5,7},{6,4},{7,5},{8,10},{9,11},{10,... | collective-permute-start | bytes 294920 | tf_op jit(solution)/shard_map/ppermute | solution.py:357
  207.9 3.5 %collective-permute-start.30 = (bf16[24,2048]{1,0:T(8,128)(2,1)S(1)}, bf16[24,2048]{1,0:T(8,128)(2,1)S(1)}, u32[]{:S(2)}, u32[]{:S(2)}) collective-permute-start(bf16[24,2048]{1,0:T(8,128)(2,1)S(1)} %get-tuple-element.34), channel_id=1, source_target_pairs={{0,3},{1,0},{2,1},{3,2},{4,7},{5,4},{6,5},{7,6},{8,11},{9,8},{10,9... | collective-permute-start | bytes 294920 | tf_op jit(solution)/shard_map/ppermute | solution.py:357
  211.5 2.3 collective-permute-done.29
  213.7 4.1 %collective-permute-done.30 = bf16[24,2048]{1,0:T(8,128)(2,1)S(1)} collective-permute-done((bf16[24,2048]{1,0:T(8,128)(2,1)S(1)}, bf16[24,2048]{1,0:T(8,128)(2,1)S(1)}, u32[]{:S(2)}, u32[]{:S(2)}) %collective-permute-start.30) | collective-permute-done | bytes 98336 | tf_op jit(solution)/shard_map/ppermute | solution.py:357
  217.9 0.8 maximum_bitcast_fusion
  218.7 1.4 copy-done.1
  220.1 3.2 %unpack.1 = (bf16[128,3072]{1,0:T(8,128)(2,1)}, bf16[128,3072]{1,0:T(8,128)(2,1)}, bf16[128,3072]{1,0:T(8,128)(2,1)}) custom-call(bf16[8,3,128,384]{3,2,1,0:T(8,128)(2,1)} %copy-done.1), custom_call_target="tpu_custom_call" | custom-call | bytes 4718592 | tf_op jit(solution)/shard_map/unpack/pallas_call | solution.py:75
  (82 shorter events, 3.9 us)
Async XLA Ops:
  10.4 43.8 %all-to-all-start = ((bf16[8,3,128,384]{3,2,1,0:T(8,128)(2,1)}), bf16[8,3,128,384]{3,2,1,0:T(8,128)(2,1)S(1)}, u32[]{:S(2)}, u32[]{:S(2)}) async-start(bf16[8,3,128,384]{3,2,1,0:T(8,128)(2,1)} %pack.1), calls=%async_computation | async-start | bytes 4718592 | tf_op jit(solution)/shard_map/all_to_all | solution.py:342
  17.1 118.0 %all-gather.2.cloned.1.call-start = ((), (), s32[]{:S(2)}) async-start(), calls=%async_computation.2 | async-start | bytes 4915200 | tf_op jit(solution)/shard_map/all_gather | solution.py:385
  18.3 35.9 %collective-permute-start = (bf16[128,3072]{1,0:T(8,128)(2,1)S(1)}, bf16[128,3072]{1,0:T(8,128)(2,1)S(1)}, u32[]{:S(2)}, u32[]{:S(2)}) collective-permute-start(bf16[128,3072]{1,0:T(8,128)(2,1)S(1)} %slice.40), channel_id=1, source_target_pairs={{0,128},{1,129},{2,130},{3,131},{4,132},{5,133},{6,134},{7,135},{8... | collective-permute-start | bytes 2359304 | tf_op jit(solution)/shard_map/ppermute | solution.py:377
  21.0 33.2 %collective-permute-start.1 = (bf16[24,5120]{1,0:T(8,128)(2,1)}, bf16[24,5120]{1,0:T(8,128)(2,1)S(1)}, u32[]{:S(2)}, u32[]{:S(2)}) collective-permute-start(bf16[24,5120]{1,0:T(8,128)(2,1)} %bitcast.58), channel_id=1, source_target_pairs={{0,1},{1,2},{2,3},{3,0},{4,5},{5,6},{6,7},{7,4},{8,9},{9,10},{10,1... | collective-permute-start | bytes 737288 | tf_op jit(solution)/shard_map/ppermute | solution.py:357
  24.0 36.6 %collective-permute-start.2 = (bf16[24,5120]{1,0:T(8,128)(2,1)}, bf16[24,5120]{1,0:T(8,128)(2,1)}, u32[]{:S(2)}, u32[]{:S(2)}) collective-permute-start(bf16[24,5120]{1,0:T(8,128)(2,1)} %bitcast.59), channel_id=1, source_target_pairs={{0,2},{1,3},{2,0},{3,1},{4,6},{5,7},{6,4},{7,5},{8,10},{9,11},{10,... | collective-permute-start | bytes 737288 | tf_op jit(solution)/shard_map/ppermute | solution.py:357
  28.3 32.4 %collective-permute-start.3 = (bf16[24,5120]{1,0:T(8,128)(2,1)}, bf16[24,5120]{1,0:T(8,128)(2,1)}, u32[]{:S(2)}, u32[]{:S(2)}) collective-permute-start(bf16[24,5120]{1,0:T(8,128)(2,1)} %bitcast.60), channel_id=1, source_target_pairs={{0,3},{1,0},{2,1},{3,2},{4,7},{5,4},{6,5},{7,6},{8,11},{9,8},{10,9... | collective-permute-start | bytes 737288 | tf_op jit(solution)/shard_map/ppermute | solution.py:357
  54.2 0.7 copy-start.18
  54.2 1.0 copy-start.2
  55.2 1.5 copy-start
  56.7 4.0 %copy-start.23 = (bf16[1,24,5120]{2,1,0:T(8,128)(2,1)S(1)}, bf16[1,24,5120]{2,1,0:T(8,128)(2,1)}, u32[]{:S(2)}) copy-start(bf16[1,24,5120]{2,1,0:T(8,128)(2,1)} %param.11) | copy-start | bytes 737284
  66.1 4.4 %copy-start.8 = (bf16[128,3072]{1,0:T(8,128)(2,1)S(1)}, bf16[128,3072]{1,0:T(8,128)(2,1)}, u32[]{:S(2)}) copy-start(bf16[128,3072]{1,0:T(8,128)(2,1)} %gated.2.refs_0_) | copy-start | bytes 2359300
  66.1 7.9 %collective-permute-start.4 = (bf16[128,3072]{1,0:T(8,128)(2,1)}, bf16[128,3072]{1,0:T(8,128)(2,1)S(1)}, u32[]{:S(2)}, u32[]{:S(2)}) collective-permute-start(bf16[128,3072]{1,0:T(8,128)(2,1)} %gated.2.refs_0_), channel_id=1, source_target_pairs={{0,16},{16,0},{32,48},{48,32},{64,80},{80,64},{96,112},{112,96},{1... | collective-permute-start | bytes 2359304 | tf_op jit(solution)/shard_map/ppermute | solution.py:303
  69.1 14.7 %collective-permute-start.5 = (bf16[128,2048]{1,0:T(8,128)(2,1)}, bf16[128,2048]{1,0:T(8,128)(2,1)S(1)}, u32[]{:S(2)}, u32[]{:S(2)}) collective-permute-start(bf16[128,2048]{1,0:T(8,128)(2,1)} %hold.7), channel_id=1, source_target_pairs={{0,128},{1,129},{2,130},{3,131},{4,132},{5,133},{6,134},{7,135},{8... | collective-permute-start | bytes 1572872 | tf_op jit(solution)/shard_map/ppermute | solution.py:377
  70.5 18.1 %collective-permute-start.12 = (bf16[128,3072]{1,0:T(8,128)(2,1)S(1)}, bf16[128,3072]{1,0:T(8,128)(2,1)S(1)}, u32[]{:S(2)}, u32[]{:S(2)}) collective-permute-start(bf16[128,3072]{1,0:T(8,128)(2,1)S(1)} %copy-done.8), channel_id=1, source_target_pairs={{0,32},{16,112},{32,64},{48,16},{64,96},{80,48},{96,0},{112,80},{1... | collective-permute-start | bytes 2359304 | tf_op jit(solution)/shard_map/ppermute | solution.py:303
  74.0 0.9 copy-start.19
  83.8 2.8 %copy-start.20 = (bf16[128,3072]{1,0:T(8,128)(2,1)S(1)}, bf16[128,3072]{1,0:T(8,128)(2,1)}, u32[]{:S(2)}) copy-start(bf16[128,3072]{1,0:T(8,128)(2,1)} %copy-done.19) | copy-start | bytes 2359300
  83.8 0.8 copy-start.22
  86.7 4.4 %copy-start.4 = (bf16[128,2048]{1,0:T(8,128)(2,1)S(1)}, bf16[128,2048]{1,0:T(8,128)(2,1)}, u32[]{:S(2)}) copy-start(bf16[128,2048]{1,0:T(8,128)(2,1)} %gated.3.refs_0_) | copy-start | bytes 1572868
  86.7 2.1 collective-permute-start.6
  86.7 11.3 %collective-permute-start.13 = (bf16[128,3072]{1,0:T(8,128)(2,1)S(1)}, bf16[128,3072]{1,0:T(8,128)(2,1)}, u32[]{:S(2)}, u32[]{:S(2)}) collective-permute-start(bf16[128,3072]{1,0:T(8,128)(2,1)S(1)} %copy-done.20), channel_id=1, source_target_pairs={{0,32},{16,112},{32,64},{48,16},{64,96},{80,48},{96,0},{112,80},{1... | collective-permute-start | bytes 2359304 | tf_op jit(solution)/shard_map/ppermute | solution.py:303
  88.5 0.9 copy-start.9
  89.4 0.8 copy-start.5
  90.2 25.9 %copy-start.6 = (bf16[128,2048]{1,0:T(8,128)(2,1)S(1)}, bf16[128,2048]{1,0:T(8,128)(2,1)}, u32[]{:S(2)}) copy-start(bf16[128,2048]{1,0:T(8,128)(2,1)} %copy-done.5) | copy-start | bytes 1572868
  90.2 21.8 %collective-permute-start.16 = (bf16[128,3072]{1,0:T(8,128)(2,1)}, bf16[128,3072]{1,0:T(8,128)(2,1)S(1)}, u32[]{:S(2)}, u32[]{:S(2)}) collective-permute-start(bf16[128,3072]{1,0:T(8,128)(2,1)} %hold.8.refs_2_), channel_id=1, source_target_pairs={{0,32},{16,112},{32,64},{48,16},{64,96},{80,48},{96,0},{112,80},{1... | collective-permute-start | bytes 2359304 | tf_op jit(solution)/shard_map/ppermute | solution.py:303
  91.1 21.0 %collective-permute-start.7 = (bf16[128,2048]{1,0:T(8,128)(2,1)S(1)}, bf16[128,2048]{1,0:T(8,128)(2,1)S(1)}, u32[]{:S(2)}, u32[]{:S(2)}) collective-permute-start(bf16[128,2048]{1,0:T(8,128)(2,1)S(1)} %copy-done.4), channel_id=1, source_target_pairs={{0,32},{16,112},{32,64},{48,16},{64,96},{80,48},{96,0},{112,80},{1... | collective-permute-start | bytes 1572872 | tf_op jit(solution)/shard_map/ppermute | solution.py:303
  91.7 34.9 %collective-permute-start.14 = (bf16[128,3072]{1,0:T(8,128)(2,1)}, bf16[128,3072]{1,0:T(8,128)(2,1)}, u32[]{:S(2)}, u32[]{:S(2)}) collective-permute-start(bf16[128,3072]{1,0:T(8,128)(2,1)} %hold.8.refs_2_), channel_id=1, source_target_pairs={{0,16},{16,0},{32,48},{48,32},{64,80},{80,64},{96,112},{112,96},{1... | collective-permute-start | bytes 2359304 | tf_op jit(solution)/shard_map/ppermute | solution.py:303
  98.0 28.6 %collective-permute-start.15 = (bf16[128,3072]{1,0:T(8,128)(2,1)}, bf16[128,3072]{1,0:T(8,128)(2,1)}, u32[]{:S(2)}, u32[]{:S(2)}) collective-permute-start(bf16[128,3072]{1,0:T(8,128)(2,1)} %collective-permute-done.13.refs_3_), channel_id=1, source_target_pairs={{0,16},{16,0},{32,48},{48,32},{64,80},{80,64},{96,112},{112,96},{1... | collective-permute-start | bytes 2359304 | tf_op jit(solution)/shard_map/ppermute | solution.py:303
  112.1 0.8 copy-start.7
  112.8 0.9 copy-start.10
  113.7 12.9 %collective-permute-start.17 = (bf16[128,3072]{1,0:T(8,128)(2,1)}, bf16[128,3072]{1,0:T(8,128)(2,1)S(1)}, u32[]{:S(2)}, u32[]{:S(2)}) collective-permute-start(bf16[128,3072]{1,0:T(8,128)(2,1)} %hold.9.refs_6_), channel_id=1, source_target_pairs={{0,16},{16,0},{32,48},{48,32},{64,80},{80,64},{96,112},{112,96},{1... | collective-permute-start | bytes 2359304 | tf_op jit(solution)/shard_map/ppermute | solution.py:303
  116.1 8.3 %collective-permute-start.8 = (bf16[128,2048]{1,0:T(8,128)(2,1)S(1)}, bf16[128,2048]{1,0:T(8,128)(2,1)S(1)}, u32[]{:S(2)}, u32[]{:S(2)}) collective-permute-start(bf16[128,2048]{1,0:T(8,128)(2,1)S(1)} %copy-done.6), channel_id=1, source_target_pairs={{0,32},{16,112},{32,64},{48,16},{64,96},{80,48},{96,0},{112,80},{1... | collective-permute-start | bytes 1572872 | tf_op jit(solution)/shard_map/ppermute | solution.py:303
  116.7 26.1 %collective-permute-start.11 = (bf16[128,2048]{1,0:T(8,128)(2,1)}, bf16[128,2048]{1,0:T(8,128)(2,1)S(1)}, u32[]{:S(2)}, u32[]{:S(2)}) collective-permute-start(bf16[128,2048]{1,0:T(8,128)(2,1)} %copy-done.7), channel_id=1, source_target_pairs={{0,32},{16,112},{32,64},{48,16},{64,96},{80,48},{96,0},{112,80},{1... | collective-permute-start | bytes 1572872 | tf_op jit(solution)/shard_map/ppermute | solution.py:303
  124.5 10.7 %copy-start.13 = (bf16[128,2048]{1,0:T(8,128)(2,1)}, bf16[128,2048]{1,0:T(8,128)(2,1)S(1)}, u32[]{:S(2)}) copy-start(bf16[128,2048]{1,0:T(8,128)(2,1)S(1)} %collective-permute-done.8.refs_3_) | copy-start | bytes 1572868
  124.5 23.4 %collective-permute-start.9 = (bf16[128,2048]{1,0:T(8,128)(2,1)}, bf16[128,2048]{1,0:T(8,128)(2,1)S(1)}, u32[]{:S(2)}, u32[]{:S(2)}) collective-permute-start(bf16[128,2048]{1,0:T(8,128)(2,1)} %copy-done.7), channel_id=1, source_target_pairs={{0,16},{16,0},{32,48},{48,32},{64,80},{80,64},{96,112},{112,96},{1... | collective-permute-start | bytes 1572872 | tf_op jit(solution)/shard_map/ppermute | solution.py:303
  126.5 22.4 %collective-permute-start.10 = (bf16[128,2048]{1,0:T(8,128)(2,1)S(1)}, bf16[128,2048]{1,0:T(8,128)(2,1)S(1)}, u32[]{:S(2)}, u32[]{:S(2)}) collective-permute-start(bf16[128,2048]{1,0:T(8,128)(2,1)S(1)} %collective-permute-done.8.refs_3_), channel_id=1, source_target_pairs={{0,16},{16,0},{32,48},{48,32},{64,80},{80,64},{96,112},{112,96},{1... | collective-permute-start | bytes 1572872 | tf_op jit(solution)/shard_map/ppermute | solution.py:303
  126.6 0.9 copy-start.21
  142.8 0.8 copy-start.3
  143.5 5.4 %collective-permute-start.18 = (bf16[128,2048]{1,0:T(8,128)(2,1)}, bf16[128,2048]{1,0:T(8,128)(2,1)S(1)}, u32[]{:S(2)}, u32[]{:S(2)}) collective-permute-start(bf16[128,2048]{1,0:T(8,128)(2,1)} %hold.10.refs_6_), channel_id=1, source_target_pairs={{0,16},{16,0},{32,48},{48,32},{64,80},{80,64},{96,112},{112,96},{1... | collective-permute-start | bytes 1572872 | tf_op jit(solution)/shard_map/ppermute | solution.py:303
  144.0 35.1 %collective-permute-start.19 = (bf16[96,3072]{1,0:T(8,128)(2,1)}, bf16[96,3072]{1,0:T(8,128)(2,1)S(1)}, u32[]{:S(2)}, u32[]{:S(2)}) collective-permute-start(bf16[96,3072]{1,0:T(8,128)(2,1)} %get-tuple-element.23), channel_id=1, source_target_pairs={{0,4},{4,8},{8,12},{12,0},{1,5},{5,9},{9,13},{13,1},{2,6},{6,10},{... | collective-permute-start | bytes 1769480 | tf_op jit(solution)/shard_map/ppermute | solution.py:357
  145.3 35.7 %collective-permute-start.20 = (bf16[96,3072]{1,0:T(8,128)(2,1)}, bf16[96,3072]{1,0:T(8,128)(2,1)}, u32[]{:S(2)}, u32[]{:S(2)}) collective-permute-start(bf16[96,3072]{1,0:T(8,128)(2,1)} %get-tuple-element.25), channel_id=1, source_target_pairs={{0,8},{4,12},{8,0},{12,4},{1,9},{5,13},{9,1},{13,5},{2,10},{6,14},... | collective-permute-start | bytes 1769480 | tf_op jit(solution)/shard_map/ppermute | solution.py:357
  147.9 1.1 copy-start.14
  147.9 33.0 %collective-permute-start.21 = (bf16[96,3072]{1,0:T(8,128)(2,1)}, bf16[96,3072]{1,0:T(8,128)(2,1)}, u32[]{:S(2)}, u32[]{:S(2)}) collective-permute-start(bf16[96,3072]{1,0:T(8,128)(2,1)} %get-tuple-element.26), channel_id=1, source_target_pairs={{0,12},{4,0},{8,4},{12,8},{1,13},{5,1},{9,5},{13,9},{2,14},{6,2},{... | collective-permute-start | bytes 1769480 | tf_op jit(solution)/shard_map/ppermute | solution.py:357
  149.0 0.8 copy-start.15
  149.8 0.8 copy-start.16
  167.6 51.1 %all-to-all-start.1 = ((bf16[8,3,128,384]{3,2,1,0:T(8,128)(2,1)}), bf16[8,3,128,384]{3,2,1,0:T(8,128)(2,1)S(1)}, u32[]{:S(2)}, u32[]{:S(2)}) async-start(bf16[8,3,128,384]{3,2,1,0:T(8,128)(2,1)} %backward.1.refs_8_), calls=%async_computation.1 | async-start | bytes 4718592 | tf_op jit(solution)/shard_map/all_to_all | solution.py:342
  177.9 3.1 %copy-start.11 = (bf16[96,3072]{1,0:T(8,128)(2,1)S(1)}, bf16[96,3072]{1,0:T(8,128)(2,1)}, u32[]{:S(2)}) copy-start(bf16[96,3072]{1,0:T(8,128)(2,1)} %get-tuple-element.19.refs_8_) | copy-start | bytes 1769476
  177.9 20.5 %collective-permute-start.25 = (bf16[96,2048]{1,0:T(8,128)(2,1)}, bf16[96,2048]{1,0:T(8,128)(2,1)S(1)}, u32[]{:S(2)}, u32[]{:S(2)}) collective-permute-start(bf16[96,2048]{1,0:T(8,128)(2,1)} %get-tuple-element.27), channel_id=1, source_target_pairs={{0,4},{4,8},{8,12},{12,0},{1,5},{5,9},{9,13},{13,1},{2,6},{6,10},{... | collective-permute-start | bytes 1179656 | tf_op jit(solution)/shard_map/ppermute | solution.py:357
  178.3 25.0 %collective-permute-start.26 = (bf16[96,2048]{1,0:T(8,128)(2,1)}, bf16[96,2048]{1,0:T(8,128)(2,1)S(1)}, u32[]{:S(2)}, u32[]{:S(2)}) collective-permute-start(bf16[96,2048]{1,0:T(8,128)(2,1)} %get-tuple-element.28), channel_id=1, source_target_pairs={{0,8},{4,12},{8,0},{12,4},{1,9},{5,13},{9,1},{13,5},{2,10},{6,14},... | collective-permute-start | bytes 1179656 | tf_op jit(solution)/shard_map/ppermute | solution.py:357
  179.0 1.9 copy-start.12
  179.0 24.3 %collective-permute-start.27 = (bf16[96,2048]{1,0:T(8,128)(2,1)}, bf16[96,2048]{1,0:T(8,128)(2,1)S(1)}, u32[]{:S(2)}, u32[]{:S(2)}) collective-permute-start(bf16[96,2048]{1,0:T(8,128)(2,1)} %get-tuple-element.29), channel_id=1, source_target_pairs={{0,12},{4,0},{8,4},{12,8},{1,13},{5,1},{9,5},{13,9},{2,14},{6,2},{... | collective-permute-start | bytes 1179656 | tf_op jit(solution)/shard_map/ppermute | solution.py:357
  180.9 22.4 %copy-start.17 = (bf16[96,2048]{1,0:T(8,128)(2,1)S(1)}, bf16[96,2048]{1,0:T(8,128)(2,1)}, u32[]{:S(2)}) copy-start(bf16[96,2048]{1,0:T(8,128)(2,1)} %get-tuple-element.24.refs_1_) | copy-start | bytes 1179652
  182.8 25.1 %collective-permute-start.22 = (bf16[24,3072]{1,0:T(8,128)(2,1)S(1)}, bf16[24,3072]{1,0:T(8,128)(2,1)S(1)}, u32[]{:S(2)}, u32[]{:S(2)}) collective-permute-start(bf16[24,3072]{1,0:T(8,128)(2,1)S(1)} %get-tuple-element.30), channel_id=1, source_target_pairs={{0,1},{1,2},{2,3},{3,0},{4,5},{5,6},{6,7},{7,4},{8,9},{9,10},{10,1... | collective-permute-start | bytes 442376 | tf_op jit(solution)/shard_map/ppermute | solution.py:357
  188.7 22.7 %collective-permute-start.23 = (bf16[24,3072]{1,0:T(8,128)(2,1)S(1)}, bf16[24,3072]{1,0:T(8,128)(2,1)S(1)}, u32[]{:S(2)}, u32[]{:S(2)}) collective-permute-start(bf16[24,3072]{1,0:T(8,128)(2,1)S(1)} %get-tuple-element.32), channel_id=1, source_target_pairs={{0,2},{1,3},{2,0},{3,1},{4,6},{5,7},{6,4},{7,5},{8,10},{9,11},{10,... | collective-permute-start | bytes 442376 | tf_op jit(solution)/shard_map/ppermute | solution.py:357
  198.4 13.0 %collective-permute-start.24 = (bf16[24,3072]{1,0:T(8,128)(2,1)S(1)}, bf16[24,3072]{1,0:T(8,128)(2,1)S(1)}, u32[]{:S(2)}, u32[]{:S(2)}) collective-permute-start(bf16[24,3072]{1,0:T(8,128)(2,1)S(1)} %get-tuple-element.31), channel_id=1, source_target_pairs={{0,3},{1,0},{2,1},{3,2},{4,7},{5,4},{6,5},{7,6},{8,11},{9,8},{10,9... | collective-permute-start | bytes 442376 | tf_op jit(solution)/shard_map/ppermute | solution.py:357
  203.6 7.9 %collective-permute-start.28 = (bf16[24,2048]{1,0:T(8,128)(2,1)S(1)}, bf16[24,2048]{1,0:T(8,128)(2,1)S(1)}, u32[]{:S(2)}, u32[]{:S(2)}) collective-permute-start(bf16[24,2048]{1,0:T(8,128)(2,1)S(1)} %get-tuple-element.33), channel_id=1, source_target_pairs={{0,1},{1,2},{2,3},{3,0},{4,5},{5,6},{6,7},{7,4},{8,9},{9,10},{10,1... | collective-permute-start | bytes 294920 | tf_op jit(solution)/shard_map/ppermute | solution.py:357
  204.8 8.9 %collective-permute-start.29 = (bf16[24,2048]{1,0:T(8,128)(2,1)S(1)}, bf16[24,2048]{1,0:T(8,128)(2,1)S(1)}, u32[]{:S(2)}, u32[]{:S(2)}) collective-permute-start(bf16[24,2048]{1,0:T(8,128)(2,1)S(1)} %get-tuple-element.35), channel_id=1, source_target_pairs={{0,2},{1,3},{2,0},{3,1},{4,6},{5,7},{6,4},{7,5},{8,10},{9,11},{10,... | collective-permute-start | bytes 294920 | tf_op jit(solution)/shard_map/ppermute | solution.py:357
  207.9 9.9 %collective-permute-start.30 = (bf16[24,2048]{1,0:T(8,128)(2,1)S(1)}, bf16[24,2048]{1,0:T(8,128)(2,1)S(1)}, u32[]{:S(2)}, u32[]{:S(2)}) collective-permute-start(bf16[24,2048]{1,0:T(8,128)(2,1)S(1)} %get-tuple-element.34), channel_id=1, source_target_pairs={{0,3},{1,0},{2,1},{3,2},{4,7},{5,4},{6,5},{7,6},{8,11},{9,8},{10,9... | collective-permute-start | bytes 294920 | tf_op jit(solution)/shard_map/ppermute | solution.py:357
  218.7 1.4 copy-start.1
Sparse Core Ops, SparseCore 0:
  63.0 51.3 all-gather.1

commit v3 on v2

--- a/solution.py
+++ b/solution.py
@@ -16,6 +16,7 @@
 WIDTH = NH * HD
 D = 5120
 TILE = 1024
+GATE_TILE = 2560
 SCALE = HD**-0.5
 LOG2E = 1.4426950408889634
 F32 = jnp.float32
@@ -25,6 +26,7 @@
 CHUNKS = (3072, 2048)
 STARTS = tuple(sum(CHUNKS[:i]) for i in range(len(CHUNKS)))
 ROW = WIDTH // (YS * ZS)
+BLOCK = WIDTH // YS
 VMEM_LIMIT = 56 * 1024 * 1024
 
 
@@ -90,19 +92,18 @@
     out_ref[...] = (gate_ref[...] * total).astype(BF16)
 
 
-def gated(gate, cot, other, start, after=()):
-    wide = other.shape[1]
-    at = start // TILE
+def gated(gate, cot, other, start, wide, after=()):
+    at = start // GATE_TILE
     return pl.pallas_call(
         gate_body,
-        grid=(wide // TILE,),
+        grid=(wide // GATE_TILE,),
         in_specs=[
-            pl.BlockSpec((1, TILE), lambda j: (0, j + at)),
-            pl.BlockSpec((TOK, TILE), lambda j: (0, j + at)),
-            pl.BlockSpec((TOK, TILE), lambda j: (0, j)),
+            pl.BlockSpec((1, GATE_TILE), lambda j: (0, j + at)),
+            pl.BlockSpec((TOK, GATE_TILE), lambda j: (0, j + at)),
+            pl.BlockSpec((TOK, GATE_TILE), lambda j: (0, j + at)),
         ]
         + hbm(len(after)),
-        out_specs=pl.BlockSpec((TOK, TILE), lambda j: (0, j)),
+        out_specs=pl.BlockSpec((TOK, GATE_TILE), lambda j: (0, j)),
         out_shape=jax.ShapeDtypeStruct((TOK, wide), BF16),
         compiler_params=params(),
         cost_estimate=cost(2 * TOK * wide, 6 * TOK * wide),
@@ -208,8 +209,8 @@
 
 
 def weight_body(parts, at_ref, att_ref, *refs):
-    outs, wide_s, att_s = refs[-2 - YS : -2], refs[-2], refs[-1]
-    block, row = WIDTH // YS, WIDTH // (YS * ZS)
+    out_ref, wide_s, att_s = refs[-3:]
+    row = ROW
 
     @pl.when(pl.program_id(0) == 0)
     def _():
@@ -220,75 +221,71 @@
 
     rows = jnp.concatenate([ref[...] for ref in refs[:parts]], axis=0)
     term = dot(att_s[...].astype(BF16), rows).astype(BF16)
-    for i, out in enumerate(outs):
-        out[...] = term[i * block : (i + 1) * block]
+    for i in range(YS):
+        out_ref[i] = term[i * BLOCK : (i + 1) * BLOCK]
 
 
 def weight_grad(order, att, pieces, after=()):
     wide = pieces[0].shape[1]
-    block = WIDTH // YS
     return pl.pallas_call(
         functools.partial(weight_body, len(pieces)),
         grid_spec=pltpu.PrefetchScalarGridSpec(
             num_scalar_prefetch=1,
             grid=(wide // TILE,),
             in_specs=[pl.BlockSpec((WIDTH, SEQ), lambda j, o: (0, 0))] + row_specs(pieces, lambda j, o: (0, j)) + hbm(len(after)),
-            out_specs=[pl.BlockSpec((block, TILE), lambda j, o: (0, j))] * YS,
+            out_specs=pl.BlockSpec((YS, BLOCK, TILE), lambda j, o: (0, 0, j)),
             scratch_shapes=[pltpu.VMEM((WIDTH, SEQ), F32), pltpu.VMEM((WIDTH, SEQ), F32)],
         ),
-        out_shape=[jax.ShapeDtypeStruct((block, wide), BF16)] * YS,
+        out_shape=jax.ShapeDtypeStruct((YS, BLOCK, wide), BF16),
         compiler_params=params(),
         cost_estimate=cost(2 * WIDTH * SEQ * wide, 2 * (WIDTH * SEQ + SEQ * wide + WIDTH * wide)),
         name="weight_grad",
     )(order, att, *pieces, *after)
 
 
-def heads_body(count, parts, carry, from_ref, w_ref, *refs):
-    acc_s, out_s = refs[-2:]
-    out_ref = refs[-3]
+def heads_body(counts, parts, w_ref, *refs):
+    out_ref, acc_s = refs[-2:]
     step = pl.program_id(0)
 
     @pl.when(step == 0)
     def _():
-        acc_s[...] = refs[parts][...] if carry else jnp.zeros_like(acc_s)
-
-    rows = jnp.concatenate([ref[...] for ref in refs[:parts]], axis=0)
-    acc_s[...] += dot(w_ref[...], rows, NT)
-
-    @pl.when(step == count - 1)
+        acc_s[...] = jnp.zeros_like(acc_s)
+
+    begin = 0
+    for i, count in enumerate(counts):
+        pieces = refs[i * parts : (i + 1) * parts]
+
+        @pl.when((step >= begin) & (step < begin + count))
+        def _():
+            rows = jnp.concatenate([ref[...] for ref in pieces], axis=0)
+            acc_s[...] += dot(w_ref[...], rows, NT)
+
+        begin += count
+
+    @pl.when(step == begin - 1)
     def _():
-        if carry:
-            for i in range(YS * ZS):
-                start = pl.multiple_of(from_ref[i] * ROW, 8)
-                out_s[pl.ds(start, ROW), :] = acc_s[pl.ds(i * ROW, ROW), :]
-            out_ref[...] = out_s[...].astype(BF16)
-        else:
-            out_ref[...] = acc_s[...]
-
-
-def heads_grad(come, weights, offset, pieces, carry=None, after=()):
-    wide = pieces[0].shape[1]
-    count = wide // TILE
-    first = offset // TILE
-    whole = pl.BlockSpec((WIDTH, SEQ), lambda j, o: (0, 0))
-    extra = [] if carry is None else [carry]
-    return pl.pallas_call(
-        functools.partial(heads_body, count, len(pieces), carry is not None),
-        grid_spec=pltpu.PrefetchScalarGridSpec(
-            num_scalar_prefetch=1,
-            grid=(count,),
-            in_specs=[pl.BlockSpec((WIDTH, TILE), lambda j, o: (0, j + first))]
-            + row_specs(pieces, lambda j, o: (0, j))
-            + [whole] * len(extra)
-            + hbm(len(after)),
-            out_specs=whole,
-            scratch_shapes=[pltpu.VMEM((WIDTH, SEQ), F32), pltpu.VMEM((WIDTH, SEQ), F32)],
-        ),
-        out_shape=jax.ShapeDtypeStruct((WIDTH, SEQ), F32 if carry is None else BF16),
-        compiler_params=params(),
-        cost_estimate=cost(2 * WIDTH * SEQ * wide, 2 * (WIDTH * SEQ + SEQ * wide + WIDTH * wide)),
+        out_ref[...] = acc_s[...].astype(BF16)
+
+
+def heads_grad(weights, groups, after=()):
+    counts = [g[0].shape[1] // TILE for g in groups]
+    first, last = counts
+    near = lambda j: (0, jnp.minimum(j, first - 1))
+    far = lambda j: (0, jnp.maximum(j - first, 0))
+    return pl.pallas_call(
+        functools.partial(heads_body, counts, len(groups[0])),
+        grid=(first + last,),
+        in_specs=[pl.BlockSpec((WIDTH, TILE), lambda j: (0, j))]
+        + row_specs(groups[0], near)
+        + row_specs(groups[1], far)
+        + hbm(len(after)),
+        out_specs=pl.BlockSpec((WIDTH, SEQ), lambda j: (0, 0)),
+        scratch_shapes=[pltpu.VMEM((WIDTH, SEQ), F32)],
+        out_shape=jax.ShapeDtypeStruct((WIDTH, SEQ), BF16),
+        compiler_params=params(),
+        cost_estimate=cost(2 * WIDTH * SEQ * D, 2 * (WIDTH * SEQ + SEQ * D + WIDTH * D)),
         name="heads_grad",
-    )(come, weights, *pieces, *extra, *after)
+    )(weights, *groups[0], *groups[1], *after)
 
 
 def rank(x, c):
@@ -318,6 +315,27 @@
         cost_estimate=cost(0, 0),
         name="hold",
     )(value, *after)
+
+
+def pair_body(own_ref, sib_ref, *refs):
+    out_ref = refs[-1]
+    out_ref[:TOK] = own_ref[...]
+    out_ref[TOK:] = sib_ref[...]
+
+
+def pair_up(own, sib, start, wide, after):
+    at = start // TILE
+    spec = pl.BlockSpec((TOK, TILE), lambda j: (0, j + at))
+    return pl.pallas_call(
+        pair_body,
+        grid=(wide // TILE,),
+        in_specs=[spec] * 2 + hbm(len(after)),
+        out_specs=pl.BlockSpec((2 * TOK, TILE), lambda j: (0, j)),
+        out_shape=jax.ShapeDtypeStruct((2 * TOK, wide), BF16),
+        compiler_params=params(),
+        cost_estimate=cost(0, 8 * TOK * wide),
+        name="pair_up",
+    )(own, sib, *after)
 
 
 def slot_table():
@@ -342,14 +360,9 @@
     return lax.all_to_all(value, axis, split_axis=0, concat_axis=0, tiled=True)
 
 
-def clip_order():
-    y, z = lax.axis_index("y"), lax.axis_index("z")
+def clip_order(seen):
+    y, z = seen * lax.axis_index("y"), lax.axis_index("z")
     return jnp.stack([(y + i) % YS * ZS + (z + j) % ZS for i in range(YS) for j in range(ZS)]).astype(jnp.int32)
-
-
-def come_order():
-    z = lax.axis_index("z")
-    return jnp.stack([i * ZS + (z - j + ZS) % ZS for i in range(YS) for j in range(ZS)]).astype(jnp.int32)
 
 
 def around(parts, axis, size):
@@ -362,50 +375,42 @@
     return functools.reduce(jnp.add, [p.astype(F32) for p in parts])
 
 
-def scatter_sum(parts, *after):
-    got = around(parts, "y", YS)
-    if after:
-        got[1] = hold(got[1], *after)
-    part = total(got).astype(BF16)
+def scatter_sum(part):
+    part = part.astype(BF16)
     return total(around([part[i * ROW : (i + 1) * ROW] for i in range(ZS)], "z", ZS))
 
 
 def local(queries, keys, values, cotangent, gate, w_out):
     slots = slot_table()
-    order, come = clip_order(), come_order()
     cot = cotangent[0, 0]
     to_context = lambda value: lax.ppermute(value, "b", [(0, 1)])
 
-    other0 = to_context(cot[:, : CHUNKS[0]])
+    other = to_context(cot)
     packed = pack(queries[0, 0], keys[0, 0], values[0, 0])
     qkv = exchange(packed, ("x", "c"))
-    along_z = around([w_out[0]] * ZS, "z", ZS)
-    along_z[1] = hold(along_z[1], other0, qkv)
-    along_z = jnp.concatenate(along_z, axis=0)
-    weights = lax.all_gather(along_z, "y", axis=0, tiled=True)
-    own0 = gated(gate[0], cot, other0, STARTS[0], after=[along_z])
-    near0 = send(own0, ONWARD)
-    sib0 = send(own0, SIBLING)
-    near_sib0 = send(sib0, ONWARD)
-    other1 = to_context(hold(cot[:, STARTS[1] :], other0))
-    prob, att = forward(slots, qkv, after=[sib0])
-    own1 = gated(gate[0], cot, other1, STARTS[1], after=[att])
-    near1 = send(own1, ONWARD)
-    sib1 = send(own1, SIBLING)
-    near_sib1 = send(sib1, ONWARD)
-    near0 = hold(near0, sib1)
-    far0 = hold(send(near0, ONWARD), near1)
-    pieces0 = [own0, sib0, near0, near_sib0, send(near0, SIBLING), send(near_sib0, SIBLING), far0, send(far0, SIBLING)]
-    far1 = send(near1, ONWARD)
-    first_term = weight_grad(order, att, pieces0)
-    acc = heads_grad(come, weights, 0, pieces0, after=[first_term[0]])
-    far1 = hold(far1, acc)
-    pieces1 = [own1, sib1, near1, near_sib1, send(near1, SIBLING), send(near_sib1, SIBLING), far1, send(far1, SIBLING)]
-    gt = heads_grad(come, weights, STARTS[1], pieces1, acc)
+    own = gated(gate[0], cot, other, 0, D, after=[packed])
+    sib = send(own, SIBLING)
+    weights = lax.all_gather(hold(w_out[0], sib, qkv), ("y", "z"), axis=0, tiled=True)
+    pair0 = pair_up(own, sib, STARTS[0], CHUNKS[0], [])
+    near0 = send(pair0, ONWARD)
+    prob, att = forward(slots, qkv, after=[pair0])
+    pair1 = pair_up(own, sib, STARTS[1], CHUNKS[1], [att])
+    near1 = send(pair1, ONWARD)
+    near0 = hold(near0, pair1)
+    far0 = hold(send(near0[:TOK], ONWARD), near1)
+    pieces0 = [pair0, near0, send(near0, SIBLING), far0, send(far0, SIBLING)]
+    first_term = weight_grad(clip_order(0), att, pieces0)
+    far1 = send(near1[:TOK], ONWARD)
+    far1 = hold(far1, first_term)
+    pieces1 = [pair1, near1, send(near1, SIBLING), far1, send(far1, SIBLING)]
+    last_term = weight_grad(clip_order(1), att, pieces1)
+    gt = heads_grad(weights, (pieces0, pieces1), after=[last_term])
     home = backward(slots, qkv, prob, gt, att)
-    last_term = weight_grad(order, att, pieces1, after=[home])
-    first_sum = scatter_sum(first_term, last_term[0])
-    last_sum = scatter_sum(last_term)
+    got = hold(exchange(first_term, "y"), home)
+    last = around([last_term[i] for i in range(YS)], "y", YS)
+    last[0] = hold(last[0], got)
+    first_sum = scatter_sum(jnp.sum(got.astype(F32), axis=0))
+    last_sum = scatter_sum(total(last))
     dq, dk, dv = unpack(exchange(home, ("x", "c")))
     return (
         dq[None, None],

time: 233 us -> 207 us (0.89)
  the two profiles are of different devices: /device:TPU:1 before, /device:TPU:42 now
where the time goes in v3:
time: 207 us; the launch traced here: 206 us
  waiting for transfers between devices  59.6 us (29%)
  Pallas kernels  58 us (28%)
  starting transfers between devices  55 us (27%)
  local copies, waits for them, and re-layouts  16.6 us (8%)
  between operations  14.1 us (7%)
  other arithmetic  2.84 us (1%)
    ppermute x9, starting transfers between devices, around(): lax.ppermute(parts[i], axis, [(a, (a + i) % size) for a in range(size)])  32.5 us
    ppermute x9, waiting for transfers between devices, send(): return lax.ppermute(value, ('x', 'c'), perm)  23.9 us
    ppermute x1, waiting for transfers between devices, local(): to_context = lambda value: lax.ppermute(value, 'b', [(0, 1)])  23.4 us
    all_to_all x3, starting transfers between devices, exchange(): return lax.all_to_all(value, axis, split_axis=0, concat_axis=0, tiled=True)  15 us
    pallas_call x2, Pallas kernels, weight_grad(): pl.pallas_call(functools.partial(weight_body, len(pieces)), grid_spec=plt...  13.7 us
    pallas_call x1, Pallas kernels, backward(): pl.pallas_call(backward_body, grid_spec=pltpu.PrefetchScalarGridSpec(num_...  10.5 us
    pallas_call x1, Pallas kernels, heads_grad(): pl.pallas_call(functools.partial(heads_body, counts, len(groups[0])), gri...  10.1 us
    unnamed x23, local copies, waits for them, and re-layouts  9.85 us
  transfers between devices with their start and end apart: 23, of which 9 were waited for; matrix products, arithmetic and copies ran while one was open for 5% of the time, Pallas kernels for 27%

profile of v3, /device:TPU:42, one launch (start us, length us, event | category | flops | bytes accessed | tf_op | source)
XLA Modules:
  0.0 206.2 jit_solution(9624097082177792595)
XLA Ops:
  7.2 1.7 copy.23
  8.9 1.3 collective-permute-start
  10.2 3.2 %pack.1.refs_0_ = bf16[8,3,128,384]{3,2,1,0:T(8,128)(2,1)} custom-call(bf16[128,3072]{1,0:T(8,128)(2,1)} %bitcast.62, bf16[128,3072]{1,0:T(8,128)(2,1)} %bitcast.63, bf16[128,3072]{1,0:T(8,128)(2,1)} %bitcast.64), custom_call_target="tpu_custom_call" | custom-call | bytes 4718592 | tf_op jit(solution)/shard_map/pack/pallas_call | solution.py:57
  13.4 4.8 %all-to-all-start = ((bf16[8,3,128,384]{3,2,1,0:T(8,128)(2,1)}), bf16[8,3,128,384]{3,2,1,0:T(8,128)(2,1)S(1)}, u32[]{:S(2)}, u32[]{:S(2)}) async-start(bf16[8,3,128,384]{3,2,1,0:T(8,128)(2,1)} %pack.1.refs_0_), calls=%async_computation | async-start | bytes 4718592 | tf_op jit(solution)/shard_map/all_to_all | solution.py:360
  18.2 23.4 %collective-permute-done.other_ref = bf16[128,5120]{1,0:T(8,128)(2,1)} collective-permute-done((bf16[128,5120]{1,0:T(8,128)(2,1)}, bf16[128,5120]{1,0:T(8,128)(2,1)}, u32[]{:S(2)}, u32[]{:S(2)}) %collective-permute-start) | collective-permute-done | bytes 1310752 | tf_op jit(solution)/shard_map/ppermute | solution.py:386
  41.6 2.8 %gated.1.own_ref = bf16[128,5120]{1,0:T(8,128)(2,1)} custom-call(f32[1,5120]{1,0:T(1,128)} %bitcast.65, bf16[128,5120]{1,0:T(8,128)(2,1)} %bitcast.61, bf16[128,5120]{1,0:T(8,128)(2,1)} %collective-permute-done.other_ref, bf16[8,3,128,384]{3,2,1,0:T(8,128)(2,1)} %pack.1.refs_0_), custom_call_target="tpu_custom_call" | custom-call | flops 1310720 | bytes 3932160 | tf_op jit(solution)/shard_map/gated/pallas_call | solution.py:97
  44.3 0.0 collective-permute-start.1
  44.3 2.4 %all-to-all-done.qkv_ref.refs_2_ = bf16[8,3,128,384]{3,2,1,0:T(8,128)(2,1)S(1)} async-done(((bf16[8,3,128,384]{3,2,1,0:T(8,128)(2,1)}), bf16[8,3,128,384]{3,2,1,0:T(8,128)(2,1)S(1)}, u32[]{:S(2)}, u32[]{:S(2)}) %all-to-all-start) | async-done | bytes 2359328 | tf_op jit(solution)/shard_map/all_to_all | solution.py:360
  46.8 0.9 collective-permute-done.1.sib_ref.refs_1_
  47.7 0.5 copy-done.2
  48.2 0.0 all-gather.2.cloned.1.call-update
  48.3 3.4 %pair_up.2.refs_0_ = bf16[256,3072]{1,0:T(8,128)(2,1)} custom-call(bf16[128,5120]{1,0:T(8,128)(2,1)} %gated.1.own_ref, bf16[128,5120]{1,0:T(8,128)(2,1)} %collective-permute-done.1.sib_ref.refs_1_), custom_call_target="tpu_custom_call" | custom-call | bytes 3145728 | tf_op jit(solution)/shard_map/pair_up/pallas_call | solution.py:329
  51.7 1.0 collective-permute-start.2
  52.7 0.6 stack.137.slot_ref
  53.2 9.0 %forward.1 = (bf16[3,1024,1024]{2,1,0:T(8,128)(2,1)}, bf16[384,1024]{1,0:T(8,128)(2,1)}) custom-call(s32[8]{0:T(128)} %stack.137.slot_ref, bf16[8,3,128,384]{3,2,1,0:T(8,128)(2,1)} %copy-done.2, bf16[256,3072]{1,0:T(8,128)(2,1)} %pair_up.2.refs_0_), custom_call_target="tpu_custom_call" | custom-call | flops 1610612736 | bytes 9437184 | tf_op jit(solution)/shard_map/forward/pallas_call | solution.py:132
  62.2 2.1 pair_up.3.refs_1_.refs_0_.refs_5_
  64.3 1.2 collective-permute-start.5
  65.4 6.9 %collective-permute-done.2.refs_0_ = bf16[256,3072]{1,0:T(8,128)(2,1)S(1)} collective-permute-done((bf16[256,3072]{1,0:T(8,128)(2,1)}, bf16[256,3072]{1,0:T(8,128)(2,1)S(1)}, u32[]{:S(2)}, u32[]{:S(2)}) %collective-permute-start.2) | collective-permute-done | bytes 1572896 | tf_op jit(solution)/shard_map/ppermute | solution.py:300
  72.3 1.2 copy-done.3
  73.5 1.3 slice.56
  74.8 1.1 collective-permute-start.4
  75.8 7.7 %collective-permute-done.5.refs_1_.refs_6_ = bf16[256,2048]{1,0:T(8,128)(2,1)S(1)} collective-permute-done((bf16[256,2048]{1,0:T(8,128)(2,1)}, bf16[256,2048]{1,0:T(8,128)(2,1)S(1)}, u32[]{:S(2)}, u32[]{:S(2)}) %collective-permute-start.5) | collective-permute-done | bytes 1048608 | tf_op jit(solution)/shard_map/ppermute | solution.py:300
  83.5 8.4 %collective-permute-done.4.refs_0_ = bf16[128,3072]{1,0:T(8,128)(2,1)S(1)} collective-permute-done((bf16[128,3072]{1,0:T(8,128)(2,1)S(1)}, bf16[128,3072]{1,0:T(8,128)(2,1)S(1)}, u32[]{:S(2)}, u32[]{:S(2)}) %collective-permute-start.4) | collective-permute-done | bytes 786464 | tf_op jit(solution)/shard_map/ppermute | solution.py:300
  92.0 0.9 copy-done.6
  92.8 1.1 slice.57
  93.9 1.1 collective-permute-start.8
  95.0 1.9 collective-permute-start.7
  96.9 0.6 stack.154.at_ref
  97.6 0.9 copy-done.9
  98.4 7.7 %weight_grad.2.refs_1_ = bf16[4,96,3072]{2,1,0:T(8,128)(2,1)} custom-call(s32[16]{0:T(128)} %stack.154.at_ref, bf16[384,1024]{1,0:T(8,128)(2,1)} %get-tuple-element.10.refs_0_.att_ref, bf16[256,3072]{1,0:T(8,128)(2,1)} %pair_up.2.refs_0_, bf16[256,3072]{1,0:T(8,128)(2,1)} %hold.7.refs_1_, bf16[256,3072]{1,0:T(8,128)(2,1)} %collective-permute-done.3.refs_2_, ...), custom_call_target="tpu_custom_call" | custom-call | flops 2415919104 | bytes 9437184 | tf_op jit(solution)/shard_map/weight_grad/pallas_call | solution.py:230
  106.2 0.0 collective-permute-done.8.refs_0_
  106.2 0.8 copy-done.7
  107.0 4.9 %all-to-all-start.2 = ((bf16[4,96,3072]{2,1,0:T(8,128)(2,1)}), bf16[4,96,3072]{2,1,0:T(8,128)(2,1)S(1)}, u32[]{:S(2)}, u32[]{:S(2)}) async-start(bf16[4,96,3072]{2,1,0:T(8,128)(2,1)} %weight_grad.2.refs_1_), calls=%async_computation.2 | async-start | bytes 4718592 | tf_op jit(solution)/shard_map/all_to_all | solution.py:360
  111.9 0.6 stack.171.at_ref
  112.5 0.0 collective-permute-done.7.refs_2_.refs_7_
  112.5 0.0 collective-permute-done.9.refs_4_.refs_9_
  112.5 0.8 copy-done.10
  113.3 6.0 %weight_grad.3.refs_10_ = bf16[4,96,2048]{2,1,0:T(8,128)(2,1)} custom-call(s32[16]{0:T(128)} %stack.171.at_ref, bf16[384,1024]{1,0:T(8,128)(2,1)} %get-tuple-element.10.refs_0_.att_ref, bf16[256,2048]{1,0:T(8,128)(2,1)} %pair_up.3.refs_1_.refs_0_.refs_5_, bf16[256,2048]{1,0:T(8,128)(2,1)} %copy-done.5, ...), custom_call_target="tpu_custom_call" | custom-call | flops 1610612736 | bytes 6553600 | tf_op jit(solution)/shard_map/weight_grad/pallas_call | solution.py:230
  119.3 2.5 %slice_bitcast_fusion.3 = (bf16[96,2048]{1,0:T(8,128)(2,1)}, bf16[96,2048]{1,0:T(8,128)(2,1)}, bf16[96,2048]{1,0:T(8,128)(2,1)}, bf16[96,2048]{1,0:T(8,128)(2,1)}) fusion(bf16[4,96,2048]{2,1,0:T(8,128)(2,1)} %weight_grad.3.refs_10_), kind=kLoop, calls=%fused_computation.5 | loop fusion | bytes 3145728 | tf_op jit(solution)/shard_map/squeeze | solution.py:410
  121.9 0.0 collective-permute-start.15
  121.9 2.9 %collective-permute-start.14 = (bf16[96,2048]{1,0:T(8,128)(2,1)}, bf16[96,2048]{1,0:T(8,128)(2,1)}, u32[]{:S(2)}, u32[]{:S(2)}) collective-permute-start(bf16[96,2048]{1,0:T(8,128)(2,1)} %get-tuple-element.16), channel_id=1, source_target_pairs={{0,8},{4,12},{8,0},{12,4},{1,9},{5,13},{9,1},{13,5},{2,10},{6,14},... | collective-permute-start | bytes 1179656 | tf_op jit(solution)/shard_map/ppermute | solution.py:370
  124.8 1.8 collective-permute-start.13
  126.6 10.1 %heads_grad.1.gt_ref = bf16[384,1024]{1,0:T(8,128)(2,1)} custom-call(bf16[384,5120]{1,0:T(8,128)(2,1)} %all-gather.2.cloned.1.call-done.w_ref, bf16[256,3072]{1,0:T(8,128)(2,1)} %pair_up.2.refs_0_, bf16[256,3072]{1,0:T(8,128)(2,1)} %hold.7.refs_1_, bf16[256,3072]{1,0:T(8,128)(2,1)} %collective-permute-done.3.refs_2_, bf16[128,3072]{1,0:T(8,128)(2,1)} %hold.8.refs_3_, ...), custom_call_target="tpu_custom_call" | custom-call | flops 4026531840 | bytes 15204352 | tf_op jit(solution)/shard_map/heads_grad/pallas_call | solution.py:275
  136.7 10.5 %backward.1.refs_1_ = bf16[8,3,128,384]{3,2,1,0:T(8,128)(2,1)} custom-call(s32[8]{0:T(128)} %stack.137.slot_ref, bf16[8,3,128,384]{3,2,1,0:T(8,128)(2,1)} %copy-done.2, bf16[3,1024,1024]{2,1,0:T(8,128)(2,1)} %get-tuple-element.9.prob_ref, bf16[384,1024]{1,0:T(8,128)(2,1)} %heads_grad.1.gt_ref, bf16[384,1024]{1,0:T(8,128)(2,1)} %get-tuple-element.10.refs_0_.att_ref), custom_call_target="tpu_custom_call" | custom-call | flops 3221225472 | bytes 12582912 | tf_op jit(solution)/shard_map/backward/pallas_call | solution.py:182
  147.2 3.1 %all-to-all-done.2.refs_0_ = bf16[4,96,3072]{2,1,0:T(8,128)(2,1)S(1)} async-done(((bf16[4,96,3072]{2,1,0:T(8,128)(2,1)}), bf16[4,96,3072]{2,1,0:T(8,128)(2,1)S(1)}, u32[]{:S(2)}, u32[]{:S(2)}) %all-to-all-start.2) | async-done | bytes 2359328 | tf_op jit(solution)/shard_map/all_to_all | solution.py:360
  150.2 1.4 copy-done
  151.7 5.2 %all-to-all-start.1 = ((bf16[8,3,128,384]{3,2,1,0:T(8,128)(2,1)}), bf16[8,3,128,384]{3,2,1,0:T(8,128)(2,1)}, u32[]{:S(2)}, u32[]{:S(2)}) async-start(bf16[8,3,128,384]{3,2,1,0:T(8,128)(2,1)} %backward.1.refs_1_), calls=%async_computation.1 | async-start | bytes 4718592 | tf_op jit(solution)/shard_map/all_to_all | solution.py:360
  156.9 1.7 copy-done.1
  158.6 0.4 reduce_sum.12
  159.0 0.0 collective-permute-done.15
  159.0 2.2 %collective-permute-done.14 = bf16[96,2048]{1,0:T(8,128)(2,1)} collective-permute-done((bf16[96,2048]{1,0:T(8,128)(2,1)}, bf16[96,2048]{1,0:T(8,128)(2,1)}, u32[]{:S(2)}, u32[]{:S(2)}) %collective-permute-start.14) | collective-permute-done | bytes 393248 | tf_op jit(solution)/shard_map/ppermute | solution.py:370
  161.2 0.0 collective-permute-done.13
  161.2 1.5 add_convert_fusion
  162.7 2.6 %collective-permute-start.16 = (bf16[24,2048]{1,0:T(8,128)(2,1)S(1)}, bf16[24,2048]{1,0:T(8,128)(2,1)S(1)}, u32[]{:S(2)}, u32[]{:S(2)}) collective-permute-start(bf16[24,2048]{1,0:T(8,128)(2,1)S(1)} %get-tuple-element.21), channel_id=1, source_target_pairs={{0,1},{1,2},{2,3},{3,0},{4,5},{5,6},{6,7},{7,4},{8,9},{9,10},{10,1... | collective-permute-start | bytes 294920 | tf_op jit(solution)/shard_map/ppermute | solution.py:370
  165.3 1.6 collective-permute-start.18
  166.9 5.1 %collective-permute-start.17 = (bf16[24,2048]{1,0:T(8,128)(2,1)S(1)}, bf16[24,2048]{1,0:T(8,128)(2,1)S(1)}, u32[]{:S(2)}, u32[]{:S(2)}) collective-permute-start(bf16[24,2048]{1,0:T(8,128)(2,1)S(1)} %get-tuple-element.23), channel_id=1, source_target_pairs={{0,2},{1,3},{2,0},{3,1},{4,6},{5,7},{6,4},{7,5},{8,10},{9,11},{10,... | collective-permute-start | bytes 294920 | tf_op jit(solution)/shard_map/ppermute | solution.py:370
  172.0 0.1 collective-permute-start.10
  172.1 4.1 %collective-permute-start.12 = (bf16[24,3072]{1,0:T(8,128)(2,1)S(1)}, bf16[24,3072]{1,0:T(8,128)(2,1)S(1)}, u32[]{:S(2)}, u32[]{:S(2)}) collective-permute-start(bf16[24,3072]{1,0:T(8,128)(2,1)S(1)} %get-tuple-element.19), channel_id=1, source_target_pairs={{0,3},{1,0},{2,1},{3,2},{4,7},{5,4},{6,5},{7,6},{8,11},{9,8},{10,9... | collective-permute-start | bytes 442376 | tf_op jit(solution)/shard_map/ppermute | solution.py:370
  176.2 14.4 %collective-permute-start.11 = (bf16[24,3072]{1,0:T(8,128)(2,1)S(1)}, bf16[24,3072]{1,0:T(8,128)(2,1)S(1)}, u32[]{:S(2)}, u32[]{:S(2)}) collective-permute-start(bf16[24,3072]{1,0:T(8,128)(2,1)S(1)} %get-tuple-element.20), channel_id=1, source_target_pairs={{0,2},{1,3},{2,0},{3,1},{4,6},{5,7},{6,4},{7,5},{8,10},{9,11},{10,... | collective-permute-start | bytes 442376 | tf_op jit(solution)/shard_map/ppermute | solution.py:370
  190.6 0.1 convert_add_fusion.1
  190.6 4.6 %collective-permute-done.11 = bf16[24,3072]{1,0:T(8,128)(2,1)S(1)} collective-permute-done((bf16[24,3072]{1,0:T(8,128)(2,1)S(1)}, bf16[24,3072]{1,0:T(8,128)(2,1)S(1)}, u32[]{:S(2)}, u32[]{:S(2)}) %collective-permute-start.11) | collective-permute-done | bytes 147488 | tf_op jit(solution)/shard_map/ppermute | solution.py:370
  195.3 0.1 convert_add_fusion
  195.3 0.8 maximum_bitcast_fusion
  196.2 3.2 %unpack.1 = (bf16[128,3072]{1,0:T(8,128)(2,1)}, bf16[128,3072]{1,0:T(8,128)(2,1)}, bf16[128,3072]{1,0:T(8,128)(2,1)}) custom-call(bf16[8,3,128,384]{3,2,1,0:T(8,128)(2,1)} %all-to-all-done.1.home_ref), custom_call_target="tpu_custom_call" | custom-call | bytes 4718592 | tf_op jit(solution)/shard_map/unpack/pallas_call | solution.py:77
  (35 shorter events, 0.1 us)
Async XLA Ops:
  8.9 32.7 %collective-permute-start = (bf16[128,5120]{1,0:T(8,128)(2,1)}, bf16[128,5120]{1,0:T(8,128)(2,1)}, u32[]{:S(2)}, u32[]{:S(2)}) collective-permute-start(bf16[128,5120]{1,0:T(8,128)(2,1)} %bitcast.60), channel_id=1, source_target_pairs={{0,128},{1,129},{2,130},{3,131},{4,132},{5,133},{6,134},{7,135},{8... | collective-permute-start | bytes 3932168 | tf_op jit(solution)/shard_map/ppermute | solution.py:386
  13.4 33.4 %all-to-all-start = ((bf16[8,3,128,384]{3,2,1,0:T(8,128)(2,1)}), bf16[8,3,128,384]{3,2,1,0:T(8,128)(2,1)S(1)}, u32[]{:S(2)}, u32[]{:S(2)}) async-start(bf16[8,3,128,384]{3,2,1,0:T(8,128)(2,1)} %pack.1.refs_0_), calls=%async_computation | async-start | bytes 4718592 | tf_op jit(solution)/shard_map/all_to_all | solution.py:360
  18.2 108.3 %all-gather.2.cloned.1.call-start = ((), (), s32[]{:S(2)}) async-start(), calls=%async_computation.3 | async-start | bytes 4177920 | tf_op jit(solution)/shard_map/all_gather | solution.py:393
  44.3 3.4 %collective-permute-start.1 = (bf16[128,5120]{1,0:T(8,128)(2,1)}, bf16[128,5120]{1,0:T(8,128)(2,1)}, u32[]{:S(2)}, u32[]{:S(2)}) collective-permute-start(bf16[128,5120]{1,0:T(8,128)(2,1)} %gated.1.own_ref), channel_id=1, source_target_pairs={{0,16},{16,0},{32,48},{48,32},{64,80},{80,64},{96,112},{112,96},{1... | collective-permute-start | bytes 3932168 | tf_op jit(solution)/shard_map/ppermute | solution.py:300
  46.8 1.5 copy-start.2
  51.7 20.6 %collective-permute-start.2 = (bf16[256,3072]{1,0:T(8,128)(2,1)}, bf16[256,3072]{1,0:T(8,128)(2,1)S(1)}, u32[]{:S(2)}, u32[]{:S(2)}) collective-permute-start(bf16[256,3072]{1,0:T(8,128)(2,1)} %pair_up.2.refs_0_), channel_id=1, source_target_pairs={{0,32},{16,112},{32,64},{48,16},{64,96},{80,48},{96,0},{112,80},{1... | collective-permute-start | bytes 4718600 | tf_op jit(solution)/shard_map/ppermute | solution.py:300
  64.3 19.3 %collective-permute-start.5 = (bf16[256,2048]{1,0:T(8,128)(2,1)}, bf16[256,2048]{1,0:T(8,128)(2,1)S(1)}, u32[]{:S(2)}, u32[]{:S(2)}) collective-permute-start(bf16[256,2048]{1,0:T(8,128)(2,1)} %pair_up.3.refs_1_.refs_0_.refs_5_), channel_id=1, source_target_pairs={{0,32},{16,112},{32,64},{48,16},{64,96},{80,48},{96,0},{112,80},{1... | collective-permute-start | bytes 3145736 | tf_op jit(solution)/shard_map/ppermute | solution.py:300
  72.3 1.2 copy-start.3
  73.5 2.4 %copy-start.4 = (bf16[256,3072]{1,0:T(8,128)(2,1)S(1)}, bf16[256,3072]{1,0:T(8,128)(2,1)}, u32[]{:S(2)}) copy-start(bf16[256,3072]{1,0:T(8,128)(2,1)} %hold.7.refs_1_) | copy-start | bytes 4718596
  74.8 17.2 %collective-permute-start.4 = (bf16[128,3072]{1,0:T(8,128)(2,1)S(1)}, bf16[128,3072]{1,0:T(8,128)(2,1)S(1)}, u32[]{:S(2)}, u32[]{:S(2)}) collective-permute-start(bf16[128,3072]{1,0:T(8,128)(2,1)S(1)} %slice.56), channel_id=1, source_target_pairs={{0,32},{16,112},{32,64},{48,16},{64,96},{80,48},{96,0},{112,80},{1... | collective-permute-start | bytes 2359304 | tf_op jit(solution)/shard_map/ppermute | solution.py:300
  75.8 21.7 %collective-permute-start.3 = (bf16[256,3072]{1,0:T(8,128)(2,1)S(1)}, bf16[256,3072]{1,0:T(8,128)(2,1)}, u32[]{:S(2)}, u32[]{:S(2)}) collective-permute-start(bf16[256,3072]{1,0:T(8,128)(2,1)S(1)} %copy-done.4), channel_id=1, source_target_pairs={{0,16},{16,0},{32,48},{48,32},{64,80},{80,64},{96,112},{112,96},{1... | collective-permute-start | bytes 4718600 | tf_op jit(solution)/shard_map/ppermute | solution.py:300
  83.5 8.4 %copy-start.5 = (bf16[256,2048]{1,0:T(8,128)(2,1)}, bf16[256,2048]{1,0:T(8,128)(2,1)S(1)}, u32[]{:S(2)}) copy-start(bf16[256,2048]{1,0:T(8,128)(2,1)S(1)} %collective-permute-done.5.refs_1_.refs_6_) | copy-start | bytes 3145732
  92.0 0.9 copy-start.6
  92.8 4.7 %collective-permute-start.6 = (bf16[128,3072]{1,0:T(8,128)(2,1)}, bf16[128,3072]{1,0:T(8,128)(2,1)S(1)}, u32[]{:S(2)}, u32[]{:S(2)}) collective-permute-start(bf16[128,3072]{1,0:T(8,128)(2,1)} %hold.8.refs_3_), channel_id=1, source_target_pairs={{0,16},{16,0},{32,48},{48,32},{64,80},{80,64},{96,112},{112,96},{1... | collective-permute-start | bytes 2359304 | tf_op jit(solution)/shard_map/ppermute | solution.py:300
  93.9 12.2 %collective-permute-start.8 = (bf16[128,2048]{1,0:T(8,128)(2,1)S(1)}, bf16[128,2048]{1,0:T(8,128)(2,1)S(1)}, u32[]{:S(2)}, u32[]{:S(2)}) collective-permute-start(bf16[128,2048]{1,0:T(8,128)(2,1)S(1)} %slice.57), channel_id=1, source_target_pairs={{0,32},{16,112},{32,64},{48,16},{64,96},{80,48},{96,0},{112,80},{1... | collective-permute-start | bytes 1572872 | tf_op jit(solution)/shard_map/ppermute | solution.py:300
  95.0 17.5 %collective-permute-start.7 = (bf16[256,2048]{1,0:T(8,128)(2,1)}, bf16[256,2048]{1,0:T(8,128)(2,1)}, u32[]{:S(2)}, u32[]{:S(2)}) collective-permute-start(bf16[256,2048]{1,0:T(8,128)(2,1)} %copy-done.5), channel_id=1, source_target_pairs={{0,16},{16,0},{32,48},{48,32},{64,80},{80,64},{96,112},{112,96},{1... | collective-permute-start | bytes 3145736 | tf_op jit(solution)/shard_map/ppermute | solution.py:300
  97.6 0.9 copy-start.9
  106.2 0.8 copy-start.7
  107.0 5.5 %collective-permute-start.9 = (bf16[128,2048]{1,0:T(8,128)(2,1)}, bf16[128,2048]{1,0:T(8,128)(2,1)S(1)}, u32[]{:S(2)}, u32[]{:S(2)}) collective-permute-start(bf16[128,2048]{1,0:T(8,128)(2,1)} %hold.9.refs_3_.refs_8_), channel_id=1, source_target_pairs={{0,16},{16,0},{32,48},{48,32},{64,80},{80,64},{96,112},{112,96},{1... | collective-permute-start | bytes 1572872 | tf_op jit(solution)/shard_map/ppermute | solution.py:300
  107.0 43.3 %all-to-all-start.2 = ((bf16[4,96,3072]{2,1,0:T(8,128)(2,1)}), bf16[4,96,3072]{2,1,0:T(8,128)(2,1)S(1)}, u32[]{:S(2)}, u32[]{:S(2)}) async-start(bf16[4,96,3072]{2,1,0:T(8,128)(2,1)} %weight_grad.2.refs_1_), calls=%async_computation.2 | async-start | bytes 4718592 | tf_op jit(solution)/shard_map/all_to_all | solution.py:360
  112.5 0.8 copy-start.10
  121.9 37.2 %collective-permute-start.15 = (bf16[96,2048]{1,0:T(8,128)(2,1)}, bf16[96,2048]{1,0:T(8,128)(2,1)}, u32[]{:S(2)}, u32[]{:S(2)}) collective-permute-start(bf16[96,2048]{1,0:T(8,128)(2,1)} %get-tuple-element.15), channel_id=1, source_target_pairs={{0,12},{4,0},{8,4},{12,8},{1,13},{5,1},{9,5},{13,9},{2,14},{6,2},{... | collective-permute-start | bytes 1179656 | tf_op jit(solution)/shard_map/ppermute | solution.py:370
  121.9 39.3 %collective-permute-start.14 = (bf16[96,2048]{1,0:T(8,128)(2,1)}, bf16[96,2048]{1,0:T(8,128)(2,1)}, u32[]{:S(2)}, u32[]{:S(2)}) collective-permute-start(bf16[96,2048]{1,0:T(8,128)(2,1)} %get-tuple-element.16), channel_id=1, source_target_pairs={{0,8},{4,12},{8,0},{12,4},{1,9},{5,13},{9,1},{13,5},{2,10},{6,14},... | collective-permute-start | bytes 1179656 | tf_op jit(solution)/shard_map/ppermute | solution.py:370
  124.8 36.4 %collective-permute-start.13 = (bf16[96,2048]{1,0:T(8,128)(2,1)}, bf16[96,2048]{1,0:T(8,128)(2,1)}, u32[]{:S(2)}, u32[]{:S(2)}) collective-permute-start(bf16[96,2048]{1,0:T(8,128)(2,1)} %get-tuple-element.17), channel_id=1, source_target_pairs={{0,4},{4,8},{8,12},{12,0},{1,5},{5,9},{9,13},{13,1},{2,6},{6,10},{... | collective-permute-start | bytes 1179656 | tf_op jit(solution)/shard_map/ppermute | solution.py:370
  150.2 1.4 copy-start
  151.7 44.5 %all-to-all-start.1 = ((bf16[8,3,128,384]{3,2,1,0:T(8,128)(2,1)}), bf16[8,3,128,384]{3,2,1,0:T(8,128)(2,1)}, u32[]{:S(2)}, u32[]{:S(2)}) async-start(bf16[8,3,128,384]{3,2,1,0:T(8,128)(2,1)} %backward.1.refs_1_), calls=%async_computation.1 | async-start | bytes 4718592 | tf_op jit(solution)/shard_map/all_to_all | solution.py:360
  156.9 1.7 copy-start.1
  158.6 2.6 %copy-start.8 = (bf16[96,2048]{1,0:T(8,128)(2,1)S(1)}, bf16[96,2048]{1,0:T(8,128)(2,1)}, u32[]{:S(2)}) copy-start(bf16[96,2048]{1,0:T(8,128)(2,1)} %hold.11) | copy-start | bytes 1179652
  162.7 13.5 %collective-permute-start.16 = (bf16[24,2048]{1,0:T(8,128)(2,1)S(1)}, bf16[24,2048]{1,0:T(8,128)(2,1)S(1)}, u32[]{:S(2)}, u32[]{:S(2)}) collective-permute-start(bf16[24,2048]{1,0:T(8,128)(2,1)S(1)} %get-tuple-element.21), channel_id=1, source_target_pairs={{0,1},{1,2},{2,3},{3,0},{4,5},{5,6},{6,7},{7,4},{8,9},{9,10},{10,1... | collective-permute-start | bytes 294920 | tf_op jit(solution)/shard_map/ppermute | solution.py:370
  165.3 25.3 %collective-permute-start.18 = (bf16[24,2048]{1,0:T(8,128)(2,1)S(1)}, bf16[24,2048]{1,0:T(8,128)(2,1)S(1)}, u32[]{:S(2)}, u32[]{:S(2)}) collective-permute-start(bf16[24,2048]{1,0:T(8,128)(2,1)S(1)} %get-tuple-element.22), channel_id=1, source_target_pairs={{0,3},{1,0},{2,1},{3,2},{4,7},{5,4},{6,5},{7,6},{8,11},{9,8},{10,9... | collective-permute-start | bytes 294920 | tf_op jit(solution)/shard_map/ppermute | solution.py:370
  166.9 23.7 %collective-permute-start.17 = (bf16[24,2048]{1,0:T(8,128)(2,1)S(1)}, bf16[24,2048]{1,0:T(8,128)(2,1)S(1)}, u32[]{:S(2)}, u32[]{:S(2)}) collective-permute-start(bf16[24,2048]{1,0:T(8,128)(2,1)S(1)} %get-tuple-element.23), channel_id=1, source_target_pairs={{0,2},{1,3},{2,0},{3,1},{4,6},{5,7},{6,4},{7,5},{8,10},{9,11},{10,... | collective-permute-start | bytes 294920 | tf_op jit(solution)/shard_map/ppermute | solution.py:370
  172.0 18.6 %collective-permute-start.10 = (bf16[24,3072]{1,0:T(8,128)(2,1)S(1)}, bf16[24,3072]{1,0:T(8,128)(2,1)S(1)}, u32[]{:S(2)}, u32[]{:S(2)}) collective-permute-start(bf16[24,3072]{1,0:T(8,128)(2,1)S(1)} %get-tuple-element.18), channel_id=1, source_target_pairs={{0,1},{1,2},{2,3},{3,0},{4,5},{5,6},{6,7},{7,4},{8,9},{9,10},{10,1... | collective-permute-start | bytes 442376 | tf_op jit(solution)/shard_map/ppermute | solution.py:370
  172.1 18.6 %collective-permute-start.12 = (bf16[24,3072]{1,0:T(8,128)(2,1)S(1)}, bf16[24,3072]{1,0:T(8,128)(2,1)S(1)}, u32[]{:S(2)}, u32[]{:S(2)}) collective-permute-start(bf16[24,3072]{1,0:T(8,128)(2,1)S(1)} %get-tuple-element.19), channel_id=1, source_target_pairs={{0,3},{1,0},{2,1},{3,2},{4,7},{5,4},{6,5},{7,6},{8,11},{9,8},{10,9... | collective-permute-start | bytes 442376 | tf_op jit(solution)/shard_map/ppermute | solution.py:370
  176.2 19.1 %collective-permute-start.11 = (bf16[24,3072]{1,0:T(8,128)(2,1)S(1)}, bf16[24,3072]{1,0:T(8,128)(2,1)S(1)}, u32[]{:S(2)}, u32[]{:S(2)}) collective-permute-start(bf16[24,3072]{1,0:T(8,128)(2,1)S(1)} %get-tuple-element.20), channel_id=1, source_target_pairs={{0,2},{1,3},{2,0},{3,1},{4,6},{5,7},{6,4},{7,5},{8,10},{9,11},{10,... | collective-permute-start | bytes 442376 | tf_op jit(solution)/shard_map/ppermute | solution.py:370
Sparse Core Ops, SparseCore 0:
  48.4 78.0 all-gather.1

commit v4 on v3

--- a/solution.py
+++ b/solution.py
@@ -23,7 +23,7 @@
 BF16 = jnp.bfloat16
 NT = (((1,), (1,)), ((), ()))
 NN = (((1,), (0,)), ((), ()))
-CHUNKS = (3072, 2048)
+CHUNKS = (2048, 3072)
 STARTS = tuple(sum(CHUNKS[:i]) for i in range(len(CHUNKS)))
 ROW = WIDTH // (YS * ZS)
 BLOCK = WIDTH // YS
@@ -167,10 +167,10 @@
     prob = prob_ref[0]
     delta = jnp.sum(gt.astype(F32) * att_ref[...].astype(F32), axis=0, keepdims=True)
     dprob = dot(v_s[...], gt)
-    dscore = (prob.astype(F32) * ((dprob - delta) * SCALE)).astype(BF16)
+    dscore = (prob.astype(F32) * (dprob - delta)).astype(BF16)
     grads = (
-        dot(kt_s[...], dscore).T.astype(BF16),
-        dot(dscore, q_s[...]).astype(BF16),
+        (dot(kt_s[...], dscore) * SCALE).T.astype(BF16),
+        (dot(dscore, q_s[...]) * SCALE).astype(BF16),
         dot(prob, gt, NT).astype(BF16),
     )
     for s in range(RANKS):
@@ -208,8 +208,8 @@
     return [pl.BlockSpec((p.shape[0], TILE), index) for p in pieces]
 
 
-def weight_body(parts, at_ref, att_ref, *refs):
-    out_ref, wide_s, att_s = refs[-3:]
+def weight_body(parts, count, at_ref, att_ref, *refs):
+    outs, wide_s, att_s = refs[parts + count : -2], refs[-2], refs[-1]
     row = ROW
 
     @pl.when(pl.program_id(0) == 0)
@@ -222,21 +222,29 @@
     rows = jnp.concatenate([ref[...] for ref in refs[:parts]], axis=0)
     term = dot(att_s[...].astype(BF16), rows).astype(BF16)
     for i in range(YS):
-        out_ref[i] = term[i * BLOCK : (i + 1) * BLOCK]
-
-
-def weight_grad(order, att, pieces, after=()):
+        block = term[i * BLOCK : (i + 1) * BLOCK]
+        if len(outs) == 1:
+            outs[0][i] = block
+        else:
+            outs[i][...] = block
+
+
+def weight_grad(order, att, pieces, split, after=()):
     wide = pieces[0].shape[1]
     return pl.pallas_call(
-        functools.partial(weight_body, len(pieces)),
+        functools.partial(weight_body, len(pieces), len(after)),
         grid_spec=pltpu.PrefetchScalarGridSpec(
             num_scalar_prefetch=1,
             grid=(wide // TILE,),
             in_specs=[pl.BlockSpec((WIDTH, SEQ), lambda j, o: (0, 0))] + row_specs(pieces, lambda j, o: (0, j)) + hbm(len(after)),
-            out_specs=pl.BlockSpec((YS, BLOCK, TILE), lambda j, o: (0, 0, j)),
+            out_specs=[pl.BlockSpec((BLOCK, TILE), lambda j, o: (0, j))] * YS
+            if split
+            else [pl.BlockSpec((YS, BLOCK, TILE), lambda j, o: (0, 0, j))],
             scratch_shapes=[pltpu.VMEM((WIDTH, SEQ), F32), pltpu.VMEM((WIDTH, SEQ), F32)],
         ),
-        out_shape=jax.ShapeDtypeStruct((YS, BLOCK, wide), BF16),
+        out_shape=[jax.ShapeDtypeStruct((BLOCK, wide), BF16)] * YS
+        if split
+        else [jax.ShapeDtypeStruct((YS, BLOCK, wide), BF16)],
         compiler_params=params(),
         cost_estimate=cost(2 * WIDTH * SEQ * wide, 2 * (WIDTH * SEQ + SEQ * wide + WIDTH * wide)),
         name="weight_grad",
@@ -394,20 +402,20 @@
     pair0 = pair_up(own, sib, STARTS[0], CHUNKS[0], [])
     near0 = send(pair0, ONWARD)
     prob, att = forward(slots, qkv, after=[pair0])
-    pair1 = pair_up(own, sib, STARTS[1], CHUNKS[1], [att])
+    pair1 = pair_up(own, sib, STARTS[1], CHUNKS[1], [att, near0])
     near1 = send(pair1, ONWARD)
     near0 = hold(near0, pair1)
     far0 = hold(send(near0[:TOK], ONWARD), near1)
     pieces0 = [pair0, near0, send(near0, SIBLING), far0, send(far0, SIBLING)]
-    first_term = weight_grad(clip_order(0), att, pieces0)
+    (first_term,) = weight_grad(clip_order(0), att, pieces0, False)
     far1 = send(near1[:TOK], ONWARD)
     far1 = hold(far1, first_term)
     pieces1 = [pair1, near1, send(near1, SIBLING), far1, send(far1, SIBLING)]
-    last_term = weight_grad(clip_order(1), att, pieces1)
-    gt = heads_grad(weights, (pieces0, pieces1), after=[last_term])
+    last_term = weight_grad(clip_order(1), att, pieces1, True)
+    gt = heads_grad(weights, (pieces0, pieces1), after=last_term[:1])
     home = backward(slots, qkv, prob, gt, att)
     got = hold(exchange(first_term, "y"), home)
-    last = around([last_term[i] for i in range(YS)], "y", YS)
+    last = around(last_term, "y", YS)
     last[0] = hold(last[0], got)
     first_sum = scatter_sum(jnp.sum(got.astype(F32), axis=0))
     last_sum = scatter_sum(total(last))

time: 207 us -> 200 us (0.966)
  the two profiles are of different devices: /device:TPU:42 before, /device:TPU:1 now
where the time goes in v4:
time: 200 us; the launch traced here: 199 us
  waiting for transfers between devices  57.4 us (29%)
  Pallas kernels  56.8 us (28%)
  starting transfers between devices  55.6 us (28%)
  between operations  14.1 us (7%)
  local copies, waits for them, and re-layouts  12.4 us (6%)
  other arithmetic  2.81 us (1%)
    ppermute x9, waiting for transfers between devices, send(): return lax.ppermute(value, ('x', 'c'), perm)  20.3 us
    ppermute x9, starting transfers between devices, around(): lax.ppermute(parts[i], axis, [(a, (a + i) % size) for a in range(size)])  19.3 us
    ppermute x1, waiting for transfers between devices, local(): to_context = lambda value: lax.ppermute(value, 'b', [(0, 1)])  18.2 us
    ppermute x9, starting transfers between devices, send(): return lax.ppermute(value, ('x', 'c'), perm)  15.6 us
    all_to_all x3, starting transfers between devices, exchange(): return lax.all_to_all(value, axis, split_axis=0, concat_axis=0, tiled=True)  15.3 us
    pallas_call x2, Pallas kernels, weight_grad(): pl.pallas_call(functools.partial(weight_body, len(pieces), len(after)), g...  13.6 us
    ppermute x9, waiting for transfers between devices, around(): lax.ppermute(parts[i], axis, [(a, (a + i) % size) for a in range(size)])  12.2 us
    pallas_call x1, Pallas kernels, backward(): pl.pallas_call(backward_body, grid_spec=pltpu.PrefetchScalarGridSpec(num_...  9.92 us
  transfers between devices with their start and end apart: 23, of which 7 were waited for; matrix products, arithmetic and copies ran while one was open for 3% of the time, Pallas kernels for 27%

profile of v4, /device:TPU:1, one launch (start us, length us, event | category | flops | bytes accessed | tf_op | source)
XLA Modules:
  0.0 199.1 jit_solution(7589574307128618670)
XLA Ops:
  7.2 1.7 copy.23
  8.8 5.4 %collective-permute-start = (bf16[128,5120]{1,0:T(8,128)(2,1)}, bf16[128,5120]{1,0:T(8,128)(2,1)}, u32[]{:S(2)}, u32[]{:S(2)}) collective-permute-start(bf16[128,5120]{1,0:T(8,128)(2,1)} %bitcast.52), channel_id=1, source_target_pairs={{0,128},{1,129},{2,130},{3,131},{4,132},{5,133},{6,134},{7,135},{8... | collective-permute-start | bytes 3932168 | tf_op jit(solution)/shard_map/ppermute | solution.py:394
  14.3 3.2 %pack.1.refs_0_ = bf16[8,3,128,384]{3,2,1,0:T(8,128)(2,1)} custom-call(bf16[128,3072]{1,0:T(8,128)(2,1)} %bitcast.54, bf16[128,3072]{1,0:T(8,128)(2,1)} %bitcast.55, bf16[128,3072]{1,0:T(8,128)(2,1)} %bitcast.56), custom_call_target="tpu_custom_call" | custom-call | bytes 4718592 | tf_op jit(solution)/shard_map/pack/pallas_call | solution.py:57
  17.5 5.3 %all-to-all-start = ((bf16[8,3,128,384]{3,2,1,0:T(8,128)(2,1)}), bf16[8,3,128,384]{3,2,1,0:T(8,128)(2,1)S(1)}, u32[]{:S(2)}, u32[]{:S(2)}) async-start(bf16[8,3,128,384]{3,2,1,0:T(8,128)(2,1)} %pack.1.refs_0_), calls=%async_computation | async-start | bytes 4718592 | tf_op jit(solution)/shard_map/all_to_all | solution.py:368
  22.7 18.2 %collective-permute-done.other_ref = bf16[128,5120]{1,0:T(8,128)(2,1)} collective-permute-done((bf16[128,5120]{1,0:T(8,128)(2,1)}, bf16[128,5120]{1,0:T(8,128)(2,1)}, u32[]{:S(2)}, u32[]{:S(2)}) %collective-permute-start) | collective-permute-done | bytes 1310752 | tf_op jit(solution)/shard_map/ppermute | solution.py:394
  40.9 2.8 %gated.1.own_ref = bf16[128,5120]{1,0:T(8,128)(2,1)} custom-call(f32[1,5120]{1,0:T(1,128)} %bitcast.57, bf16[128,5120]{1,0:T(8,128)(2,1)} %bitcast.53, bf16[128,5120]{1,0:T(8,128)(2,1)} %collective-permute-done.other_ref, bf16[8,3,128,384]{3,2,1,0:T(8,128)(2,1)} %pack.1.refs_0_), custom_call_target="tpu_custom_call" | custom-call | flops 1310720 | bytes 3932160 | tf_op jit(solution)/shard_map/gated/pallas_call | solution.py:97
  43.7 1.5 collective-permute-start.1
  45.3 6.6 %all-to-all-done.qkv_ref.refs_2_ = bf16[8,3,128,384]{3,2,1,0:T(8,128)(2,1)S(1)} async-done(((bf16[8,3,128,384]{3,2,1,0:T(8,128)(2,1)}), bf16[8,3,128,384]{3,2,1,0:T(8,128)(2,1)S(1)}, u32[]{:S(2)}, u32[]{:S(2)}) %all-to-all-start) | async-done | bytes 2359328 | tf_op jit(solution)/shard_map/all_to_all | solution.py:368
  51.9 0.0 collective-permute-done.1.sib_ref.refs_1_
  51.9 1.4 copy-done.2
  53.3 0.0 all-gather.2.cloned.1.call-update
  53.4 2.1 %pair_up.2.refs_0_ = bf16[256,2048]{1,0:T(8,128)(2,1)} custom-call(bf16[128,5120]{1,0:T(8,128)(2,1)} %gated.1.own_ref, bf16[128,5120]{1,0:T(8,128)(2,1)} %collective-permute-done.1.sib_ref.refs_1_), custom_call_target="tpu_custom_call" | custom-call | bytes 2097152 | tf_op jit(solution)/shard_map/pair_up/pallas_call | solution.py:337
  55.4 0.9 collective-permute-start.2
  56.3 0.7 stack.137.slot_ref
  57.0 9.0 %forward.1 = (bf16[3,1024,1024]{2,1,0:T(8,128)(2,1)}, bf16[384,1024]{1,0:T(8,128)(2,1)}) custom-call(s32[8]{0:T(128)} %stack.137.slot_ref, bf16[8,3,128,384]{3,2,1,0:T(8,128)(2,1)} %copy-done.2, bf16[256,2048]{1,0:T(8,128)(2,1)} %pair_up.2.refs_0_), custom_call_target="tpu_custom_call" | custom-call | flops 1610612736 | bytes 9437184 | tf_op jit(solution)/shard_map/forward/pallas_call | solution.py:132
  66.0 3.6 %collective-permute-done.2.refs_1_.refs_0_ = bf16[256,2048]{1,0:T(8,128)(2,1)S(1)} collective-permute-done((bf16[256,2048]{1,0:T(8,128)(2,1)}, bf16[256,2048]{1,0:T(8,128)(2,1)S(1)}, u32[]{:S(2)}, u32[]{:S(2)}) %collective-permute-start.2) | collective-permute-done | bytes 1048608 | tf_op jit(solution)/shard_map/ppermute | solution.py:308
  69.6 1.0 copy-done.3
  70.6 3.4 %pair_up.3.refs_1_.refs_0_.refs_5_ = bf16[256,3072]{1,0:T(8,128)(2,1)} custom-call(bf16[128,5120]{1,0:T(8,128)(2,1)} %gated.1.own_ref, bf16[128,5120]{1,0:T(8,128)(2,1)} %collective-permute-done.1.sib_ref.refs_1_, bf16[384,1024]{1,0:T(8,128)(2,1)} %get-tuple-element.14.refs_0_.att_ref, bf16[256,2048]{1,0:T(8,128)(2,1)} %copy-done.3), custom_call_target="tpu_custom_call" | custom-call | bytes 3145728 | tf_op jit(solution)/shard_map/pair_up/pallas_call | solution.py:337
  74.0 1.8 collective-permute-start.5
  75.8 1.1 slice.40
  76.9 0.1 collective-permute-start.4
  77.0 1.2 collective-permute-start.3
  78.2 15.5 %collective-permute-done.5.refs_1_.refs_6_ = bf16[256,3072]{1,0:T(8,128)(2,1)S(1)} collective-permute-done((bf16[256,3072]{1,0:T(8,128)(2,1)}, bf16[256,3072]{1,0:T(8,128)(2,1)S(1)}, u32[]{:S(2)}, u32[]{:S(2)}) %collective-permute-start.5) | collective-permute-done | bytes 1572896 | tf_op jit(solution)/shard_map/ppermute | solution.py:308
  93.8 1.0 slice.41
  94.8 2.7 %collective-permute-start.8 = (bf16[128,3072]{1,0:T(8,128)(2,1)}, bf16[128,3072]{1,0:T(8,128)(2,1)}, u32[]{:S(2)}, u32[]{:S(2)}) collective-permute-start(bf16[128,3072]{1,0:T(8,128)(2,1)} %slice.41), channel_id=1, source_target_pairs={{0,32},{16,112},{32,64},{48,16},{64,96},{80,48},{96,0},{112,80},{1... | collective-permute-start | bytes 2359304 | tf_op jit(solution)/shard_map/ppermute | solution.py:308
  97.5 2.3 %collective-permute-start.7 = (bf16[256,3072]{1,0:T(8,128)(2,1)S(1)}, bf16[256,3072]{1,0:T(8,128)(2,1)}, u32[]{:S(2)}, u32[]{:S(2)}) collective-permute-start(bf16[256,3072]{1,0:T(8,128)(2,1)S(1)} %collective-permute-done.5.refs_1_.refs_6_), channel_id=1, source_target_pairs={{0,16},{16,0},{32,48},{48,32},{64,80},{80,64},{96,112},{112,96},{1... | collective-permute-start | bytes 4718600 | tf_op jit(solution)/shard_map/ppermute | solution.py:308
  99.8 0.0 collective-permute-done.4.refs_0_
  99.8 0.8 copy-done.6
  100.6 4.6 %collective-permute-start.6 = (bf16[128,2048]{1,0:T(8,128)(2,1)}, bf16[128,2048]{1,0:T(8,128)(2,1)S(1)}, u32[]{:S(2)}, u32[]{:S(2)}) collective-permute-start(bf16[128,2048]{1,0:T(8,128)(2,1)} %hold.8.refs_3_), channel_id=1, source_target_pairs={{0,16},{16,0},{32,48},{48,32},{64,80},{80,64},{96,112},{112,96},{1... | collective-permute-start | bytes 1572872 | tf_op jit(solution)/shard_map/ppermute | solution.py:308
  105.2 0.6 stack.154.at_ref
  105.9 0.0 collective-permute-done.3.refs_2_
  105.9 1.1 collective-permute-done.6.refs_4_
  107.0 0.8 copy-done.8
  107.8 6.0 %weight_grad.2.refs_1_ = bf16[4,96,2048]{2,1,0:T(8,128)(2,1)} custom-call(s32[16]{0:T(128)} %stack.154.at_ref, bf16[384,1024]{1,0:T(8,128)(2,1)} %get-tuple-element.14.refs_0_.att_ref, bf16[256,2048]{1,0:T(8,128)(2,1)} %pair_up.2.refs_0_, bf16[256,2048]{1,0:T(8,128)(2,1)} %hold.7.refs_1_, bf16[256,2048]{1,0:T(8,128)(2,1)} %copy-done.7, ...), custom_call_target="tpu_custom_call" | custom-call | flops 1610612736 | bytes 6553600 | tf_op jit(solution)/shard_map/weight_grad/pallas_call | solution.py:234
  113.9 0.0 collective-permute-done.8.refs_0_
  113.9 0.4 collective-permute-start.9
  114.2 4.2 %all-to-all-start.2 = ((bf16[4,96,2048]{2,1,0:T(8,128)(2,1)}), bf16[4,96,2048]{2,1,0:T(8,128)(2,1)S(1)}, u32[]{:S(2)}, u32[]{:S(2)}) async-start(bf16[4,96,2048]{2,1,0:T(8,128)(2,1)} %weight_grad.2.refs_1_), calls=%async_computation.2 | async-start | bytes 3145728 | tf_op jit(solution)/shard_map/all_to_all | solution.py:368
  118.5 0.6 stack.171.at_ref
  119.1 7.6 %weight_grad.3 = (bf16[96,3072]{1,0:T(8,128)(2,1)}, bf16[96,3072]{1,0:T(8,128)(2,1)}, bf16[96,3072]{1,0:T(8,128)(2,1)}, bf16[96,3072]{1,0:T(8,128)(2,1)}) custom-call(s32[16]{0:T(128)} %stack.171.at_ref, bf16[384,1024]{1,0:T(8,128)(2,1)} %get-tuple-element.14.refs_0_.att_ref, bf16[256,3072]{1,0:T(8,128)(2,1)} %pair_up.3.refs_1_.refs_0_.refs_5_, ...), custom_call_target="tpu_custom_call" | custom-call | flops 2415919104 | bytes 9437184 | tf_op jit(solution)/shard_map/weight_grad/pallas_call | solution.py:234
  126.7 1.5 collective-permute-start.13
  128.2 2.4 %collective-permute-start.14 = (bf16[96,3072]{1,0:T(8,128)(2,1)}, bf16[96,3072]{1,0:T(8,128)(2,1)}, u32[]{:S(2)}, u32[]{:S(2)}) collective-permute-start(bf16[96,3072]{1,0:T(8,128)(2,1)} %get-tuple-element.20), channel_id=1, source_target_pairs={{0,8},{4,12},{8,0},{12,4},{1,9},{5,13},{9,1},{13,5},{2,10},{6,14},... | collective-permute-start | bytes 1769480 | tf_op jit(solution)/shard_map/ppermute | solution.py:378
  130.6 1.2 collective-permute-start.15
  131.8 9.6 %heads_grad.1.gt_ref = bf16[384,1024]{1,0:T(8,128)(2,1)} custom-call(bf16[384,5120]{1,0:T(8,128)(2,1)} %all-gather.2.cloned.1.call-done.w_ref, bf16[256,2048]{1,0:T(8,128)(2,1)} %pair_up.2.refs_0_, bf16[256,2048]{1,0:T(8,128)(2,1)} %hold.7.refs_1_, bf16[256,2048]{1,0:T(8,128)(2,1)} %copy-done.7, bf16[128,2048]{1,0:T(8,128)(2,1)} %hold.8.refs_3_, ...), custom_call_target="tpu_custom_call" | custom-call | flops 4026531840 | bytes 15204352 | tf_op jit(solution)/shard_map/heads_grad/pallas_call | solution.py:283
  141.4 9.9 %backward.1.refs_1_ = bf16[8,3,128,384]{3,2,1,0:T(8,128)(2,1)} custom-call(s32[8]{0:T(128)} %stack.137.slot_ref, bf16[8,3,128,384]{3,2,1,0:T(8,128)(2,1)} %copy-done.2, bf16[3,1024,1024]{2,1,0:T(8,128)(2,1)} %get-tuple-element.13.prob_ref, bf16[384,1024]{1,0:T(8,128)(2,1)} %heads_grad.1.gt_ref, bf16[384,1024]{1,0:T(8,128)(2,1)} %get-tuple-element.14.refs_0_.att_ref), custom_call_target="tpu_custom_call" | custom-call | flops 3221225472 | bytes 12582912 | tf_op jit(solution)/shard_map/backward/pallas_call | solution.py:182
  151.3 0.0 all-to-all-done.2.refs_0_
  151.3 1.1 copy-done
  152.4 5.8 %all-to-all-start.1 = ((bf16[8,3,128,384]{3,2,1,0:T(8,128)(2,1)}), bf16[8,3,128,384]{3,2,1,0:T(8,128)(2,1)}, u32[]{:S(2)}, u32[]{:S(2)}) async-start(bf16[8,3,128,384]{3,2,1,0:T(8,128)(2,1)} %backward.1.refs_1_), calls=%async_computation.1 | async-start | bytes 4718592 | tf_op jit(solution)/shard_map/all_to_all | solution.py:368
  158.3 1.4 copy-done.1
  159.7 0.3 reduce_sum.12
  160.0 3.1 %collective-permute-start.10 = (bf16[24,2048]{1,0:T(8,128)(2,1)S(1)}, bf16[24,2048]{1,0:T(8,128)(2,1)S(1)}, u32[]{:S(2)}, u32[]{:S(2)}) collective-permute-start(bf16[24,2048]{1,0:T(8,128)(2,1)S(1)} %get-tuple-element.25), channel_id=1, source_target_pairs={{0,1},{1,2},{2,3},{3,0},{4,5},{5,6},{6,7},{7,4},{8,9},{9,10},{10,1... | collective-permute-start | bytes 294920 | tf_op jit(solution)/shard_map/ppermute | solution.py:378
  163.0 2.2 %collective-permute-start.12 = (bf16[24,2048]{1,0:T(8,128)(2,1)S(1)}, bf16[24,2048]{1,0:T(8,128)(2,1)S(1)}, u32[]{:S(2)}, u32[]{:S(2)}) collective-permute-start(bf16[24,2048]{1,0:T(8,128)(2,1)S(1)} %get-tuple-element.26), channel_id=1, source_target_pairs={{0,3},{1,0},{2,1},{3,2},{4,7},{5,4},{6,5},{7,6},{8,11},{9,8},{10,9... | collective-permute-start | bytes 294920 | tf_op jit(solution)/shard_map/ppermute | solution.py:378
  165.2 4.4 %collective-permute-start.11 = (bf16[24,2048]{1,0:T(8,128)(2,1)S(1)}, bf16[24,2048]{1,0:T(8,128)(2,1)S(1)}, u32[]{:S(2)}, u32[]{:S(2)}) collective-permute-start(bf16[24,2048]{1,0:T(8,128)(2,1)S(1)} %get-tuple-element.27), channel_id=1, source_target_pairs={{0,2},{1,3},{2,0},{3,1},{4,6},{5,7},{6,4},{7,5},{8,10},{9,11},{10,... | collective-permute-start | bytes 294920 | tf_op jit(solution)/shard_map/ppermute | solution.py:378
  169.6 0.0 collective-permute-done.15
  169.6 1.6 add_convert_fusion
  171.3 0.1 collective-permute-start.16
  171.4 3.6 %collective-permute-start.18 = (bf16[24,3072]{1,0:T(8,128)(2,1)S(1)}, bf16[24,3072]{1,0:T(8,128)(2,1)S(1)}, u32[]{:S(2)}, u32[]{:S(2)}) collective-permute-start(bf16[24,3072]{1,0:T(8,128)(2,1)S(1)} %get-tuple-element.23), channel_id=1, source_target_pairs={{0,3},{1,0},{2,1},{3,2},{4,7},{5,4},{6,5},{7,6},{8,11},{9,8},{10,9... | collective-permute-start | bytes 442376 | tf_op jit(solution)/shard_map/ppermute | solution.py:378
  174.9 0.0 collective-permute-done.10
  174.9 1.0 collective-permute-start.17
  176.0 2.4 %collective-permute-done.16 = bf16[24,3072]{1,0:T(8,128)(2,1)S(1)} collective-permute-done((bf16[24,3072]{1,0:T(8,128)(2,1)S(1)}, bf16[24,3072]{1,0:T(8,128)(2,1)S(1)}, u32[]{:S(2)}, u32[]{:S(2)}) %collective-permute-start.16) | collective-permute-done | bytes 147488 | tf_op jit(solution)/shard_map/ppermute | solution.py:378
  178.3 9.8 %collective-permute-done.18 = bf16[24,3072]{1,0:T(8,128)(2,1)S(1)} collective-permute-done((bf16[24,3072]{1,0:T(8,128)(2,1)S(1)}, bf16[24,3072]{1,0:T(8,128)(2,1)S(1)}, u32[]{:S(2)}, u32[]{:S(2)}) %collective-permute-start.18) | collective-permute-done | bytes 147488 | tf_op jit(solution)/shard_map/ppermute | solution.py:378
  188.2 0.0 collective-permute-done.17
  188.2 0.1 convert_add_fusion
  188.3 0.8 maximum_bitcast_fusion
  189.1 3.2 %unpack.1 = (bf16[128,3072]{1,0:T(8,128)(2,1)}, bf16[128,3072]{1,0:T(8,128)(2,1)}, bf16[128,3072]{1,0:T(8,128)(2,1)}) custom-call(bf16[8,3,128,384]{3,2,1,0:T(8,128)(2,1)} %all-to-all-done.1.home_ref), custom_call_target="tpu_custom_call" | custom-call | bytes 4718592 | tf_op jit(solution)/shard_map/unpack/pallas_call | solution.py:77
  (30 shorter events, 0.1 us)
Async XLA Ops:
  8.8 32.1 %collective-permute-start = (bf16[128,5120]{1,0:T(8,128)(2,1)}, bf16[128,5120]{1,0:T(8,128)(2,1)}, u32[]{:S(2)}, u32[]{:S(2)}) collective-permute-start(bf16[128,5120]{1,0:T(8,128)(2,1)} %bitcast.52), channel_id=1, source_target_pairs={{0,128},{1,129},{2,130},{3,131},{4,132},{5,133},{6,134},{7,135},{8... | collective-permute-start | bytes 3932168 | tf_op jit(solution)/shard_map/ppermute | solution.py:394
  17.5 34.4 %all-to-all-start = ((bf16[8,3,128,384]{3,2,1,0:T(8,128)(2,1)}), bf16[8,3,128,384]{3,2,1,0:T(8,128)(2,1)S(1)}, u32[]{:S(2)}, u32[]{:S(2)}) async-start(bf16[8,3,128,384]{3,2,1,0:T(8,128)(2,1)} %pack.1.refs_0_), calls=%async_computation | async-start | bytes 4718592 | tf_op jit(solution)/shard_map/all_to_all | solution.py:368
  22.7 109.0 %all-gather.2.cloned.1.call-start = ((), (), s32[]{:S(2)}) async-start(), calls=%async_computation.3 | async-start | bytes 4177920 | tf_op jit(solution)/shard_map/all_gather | solution.py:401
  43.7 8.2 %collective-permute-start.1 = (bf16[128,5120]{1,0:T(8,128)(2,1)}, bf16[128,5120]{1,0:T(8,128)(2,1)}, u32[]{:S(2)}, u32[]{:S(2)}) collective-permute-start(bf16[128,5120]{1,0:T(8,128)(2,1)} %gated.1.own_ref), channel_id=1, source_target_pairs={{0,16},{16,0},{32,48},{48,32},{64,80},{80,64},{96,112},{112,96},{1... | collective-permute-start | bytes 3932168 | tf_op jit(solution)/shard_map/ppermute | solution.py:308
  51.9 1.4 copy-start.2
  55.4 14.2 %collective-permute-start.2 = (bf16[256,2048]{1,0:T(8,128)(2,1)}, bf16[256,2048]{1,0:T(8,128)(2,1)S(1)}, u32[]{:S(2)}, u32[]{:S(2)}) collective-permute-start(bf16[256,2048]{1,0:T(8,128)(2,1)} %pair_up.2.refs_0_), channel_id=1, source_target_pairs={{0,32},{16,112},{32,64},{48,16},{64,96},{80,48},{96,0},{112,80},{1... | collective-permute-start | bytes 3145736 | tf_op jit(solution)/shard_map/ppermute | solution.py:308
  69.6 1.0 copy-start.3
  74.0 19.8 %collective-permute-start.5 = (bf16[256,3072]{1,0:T(8,128)(2,1)}, bf16[256,3072]{1,0:T(8,128)(2,1)S(1)}, u32[]{:S(2)}, u32[]{:S(2)}) collective-permute-start(bf16[256,3072]{1,0:T(8,128)(2,1)} %pair_up.3.refs_1_.refs_0_.refs_5_), channel_id=1, source_target_pairs={{0,32},{16,112},{32,64},{48,16},{64,96},{80,48},{96,0},{112,80},{1... | collective-permute-start | bytes 4718600 | tf_op jit(solution)/shard_map/ppermute | solution.py:308
  76.9 22.9 %collective-permute-start.4 = (bf16[128,2048]{1,0:T(8,128)(2,1)S(1)}, bf16[128,2048]{1,0:T(8,128)(2,1)S(1)}, u32[]{:S(2)}, u32[]{:S(2)}) collective-permute-start(bf16[128,2048]{1,0:T(8,128)(2,1)S(1)} %slice.40), channel_id=1, source_target_pairs={{0,32},{16,112},{32,64},{48,16},{64,96},{80,48},{96,0},{112,80},{1... | collective-permute-start | bytes 1572872 | tf_op jit(solution)/shard_map/ppermute | solution.py:308
  77.0 28.9 %collective-permute-start.3 = (bf16[256,2048]{1,0:T(8,128)(2,1)}, bf16[256,2048]{1,0:T(8,128)(2,1)S(1)}, u32[]{:S(2)}, u32[]{:S(2)}) collective-permute-start(bf16[256,2048]{1,0:T(8,128)(2,1)} %hold.7.refs_1_), channel_id=1, source_target_pairs={{0,16},{16,0},{32,48},{48,32},{64,80},{80,64},{96,112},{112,96},{1... | collective-permute-start | bytes 3145736 | tf_op jit(solution)/shard_map/ppermute | solution.py:308
  93.8 6.0 %copy-start.4 = (bf16[256,3072]{1,0:T(8,128)(2,1)}, bf16[256,3072]{1,0:T(8,128)(2,1)S(1)}, u32[]{:S(2)}) copy-start(bf16[256,3072]{1,0:T(8,128)(2,1)S(1)} %collective-permute-done.5.refs_1_.refs_6_) | copy-start | bytes 4718596
  94.8 19.1 %collective-permute-start.8 = (bf16[128,3072]{1,0:T(8,128)(2,1)}, bf16[128,3072]{1,0:T(8,128)(2,1)}, u32[]{:S(2)}, u32[]{:S(2)}) collective-permute-start(bf16[128,3072]{1,0:T(8,128)(2,1)} %slice.41), channel_id=1, source_target_pairs={{0,32},{16,112},{32,64},{48,16},{64,96},{80,48},{96,0},{112,80},{1... | collective-permute-start | bytes 2359304 | tf_op jit(solution)/shard_map/ppermute | solution.py:308
  97.5 21.6 %collective-permute-start.7 = (bf16[256,3072]{1,0:T(8,128)(2,1)S(1)}, bf16[256,3072]{1,0:T(8,128)(2,1)}, u32[]{:S(2)}, u32[]{:S(2)}) collective-permute-start(bf16[256,3072]{1,0:T(8,128)(2,1)S(1)} %collective-permute-done.5.refs_1_.refs_6_), channel_id=1, source_target_pairs={{0,16},{16,0},{32,48},{48,32},{64,80},{80,64},{96,112},{112,96},{1... | collective-permute-start | bytes 4718600 | tf_op jit(solution)/shard_map/ppermute | solution.py:308
  99.8 0.8 copy-start.6
  100.6 6.3 %collective-permute-start.6 = (bf16[128,2048]{1,0:T(8,128)(2,1)}, bf16[128,2048]{1,0:T(8,128)(2,1)S(1)}, u32[]{:S(2)}, u32[]{:S(2)}) collective-permute-start(bf16[128,2048]{1,0:T(8,128)(2,1)} %hold.8.refs_3_), channel_id=1, source_target_pairs={{0,16},{16,0},{32,48},{48,32},{64,80},{80,64},{96,112},{112,96},{1... | collective-permute-start | bytes 1572872 | tf_op jit(solution)/shard_map/ppermute | solution.py:308
  105.9 1.1 copy-start.7
  107.0 0.8 copy-start.8
  113.9 5.2 %collective-permute-start.9 = (bf16[128,3072]{1,0:T(8,128)(2,1)}, bf16[128,3072]{1,0:T(8,128)(2,1)}, u32[]{:S(2)}, u32[]{:S(2)}) collective-permute-start(bf16[128,3072]{1,0:T(8,128)(2,1)} %hold.9.refs_3_.refs_8_), channel_id=1, source_target_pairs={{0,16},{16,0},{32,48},{48,32},{64,80},{80,64},{96,112},{112,96},{1... | collective-permute-start | bytes 2359304 | tf_op jit(solution)/shard_map/ppermute | solution.py:308
  114.2 37.1 %all-to-all-start.2 = ((bf16[4,96,2048]{2,1,0:T(8,128)(2,1)}), bf16[4,96,2048]{2,1,0:T(8,128)(2,1)S(1)}, u32[]{:S(2)}, u32[]{:S(2)}) async-start(bf16[4,96,2048]{2,1,0:T(8,128)(2,1)} %weight_grad.2.refs_1_), calls=%async_computation.2 | async-start | bytes 3145728 | tf_op jit(solution)/shard_map/all_to_all | solution.py:368
  126.7 38.6 %collective-permute-start.13 = (bf16[96,3072]{1,0:T(8,128)(2,1)}, bf16[96,3072]{1,0:T(8,128)(2,1)S(1)}, u32[]{:S(2)}, u32[]{:S(2)}) collective-permute-start(bf16[96,3072]{1,0:T(8,128)(2,1)} %get-tuple-element.19), channel_id=1, source_target_pairs={{0,4},{4,8},{8,12},{12,0},{1,5},{5,9},{9,13},{13,1},{2,6},{6,10},{... | collective-permute-start | bytes 1769480 | tf_op jit(solution)/shard_map/ppermute | solution.py:378
  128.2 41.5 %collective-permute-start.14 = (bf16[96,3072]{1,0:T(8,128)(2,1)}, bf16[96,3072]{1,0:T(8,128)(2,1)}, u32[]{:S(2)}, u32[]{:S(2)}) collective-permute-start(bf16[96,3072]{1,0:T(8,128)(2,1)} %get-tuple-element.20), channel_id=1, source_target_pairs={{0,8},{4,12},{8,0},{12,4},{1,9},{5,13},{9,1},{13,5},{2,10},{6,14},... | collective-permute-start | bytes 1769480 | tf_op jit(solution)/shard_map/ppermute | solution.py:378
  130.6 39.1 %collective-permute-start.15 = (bf16[96,3072]{1,0:T(8,128)(2,1)}, bf16[96,3072]{1,0:T(8,128)(2,1)}, u32[]{:S(2)}, u32[]{:S(2)}) collective-permute-start(bf16[96,3072]{1,0:T(8,128)(2,1)} %get-tuple-element.21), channel_id=1, source_target_pairs={{0,12},{4,0},{8,4},{12,8},{1,13},{5,1},{9,5},{13,9},{2,14},{6,2},{... | collective-permute-start | bytes 1769480 | tf_op jit(solution)/shard_map/ppermute | solution.py:378
  151.3 1.1 copy-start
  152.4 36.6 %all-to-all-start.1 = ((bf16[8,3,128,384]{3,2,1,0:T(8,128)(2,1)}), bf16[8,3,128,384]{3,2,1,0:T(8,128)(2,1)}, u32[]{:S(2)}, u32[]{:S(2)}) async-start(bf16[8,3,128,384]{3,2,1,0:T(8,128)(2,1)} %backward.1.refs_1_), calls=%async_computation.1 | async-start | bytes 4718592 | tf_op jit(solution)/shard_map/all_to_all | solution.py:368
  158.3 1.4 copy-start.1
  159.7 10.0 %copy-start.5 = (bf16[96,3072]{1,0:T(8,128)(2,1)S(1)}, bf16[96,3072]{1,0:T(8,128)(2,1)}, u32[]{:S(2)}) copy-start(bf16[96,3072]{1,0:T(8,128)(2,1)} %hold.11) | copy-start | bytes 1769476
  160.0 15.0 %collective-permute-start.10 = (bf16[24,2048]{1,0:T(8,128)(2,1)S(1)}, bf16[24,2048]{1,0:T(8,128)(2,1)S(1)}, u32[]{:S(2)}, u32[]{:S(2)}) collective-permute-start(bf16[24,2048]{1,0:T(8,128)(2,1)S(1)} %get-tuple-element.25), channel_id=1, source_target_pairs={{0,1},{1,2},{2,3},{3,0},{4,5},{5,6},{6,7},{7,4},{8,9},{9,10},{10,1... | collective-permute-start | bytes 294920 | tf_op jit(solution)/shard_map/ppermute | solution.py:378
  163.0 12.9 %collective-permute-start.12 = (bf16[24,2048]{1,0:T(8,128)(2,1)S(1)}, bf16[24,2048]{1,0:T(8,128)(2,1)S(1)}, u32[]{:S(2)}, u32[]{:S(2)}) collective-permute-start(bf16[24,2048]{1,0:T(8,128)(2,1)S(1)} %get-tuple-element.26), channel_id=1, source_target_pairs={{0,3},{1,0},{2,1},{3,2},{4,7},{5,4},{6,5},{7,6},{8,11},{9,8},{10,9... | collective-permute-start | bytes 294920 | tf_op jit(solution)/shard_map/ppermute | solution.py:378
  165.2 10.7 %collective-permute-start.11 = (bf16[24,2048]{1,0:T(8,128)(2,1)S(1)}, bf16[24,2048]{1,0:T(8,128)(2,1)S(1)}, u32[]{:S(2)}, u32[]{:S(2)}) collective-permute-start(bf16[24,2048]{1,0:T(8,128)(2,1)S(1)} %get-tuple-element.27), channel_id=1, source_target_pairs={{0,2},{1,3},{2,0},{3,1},{4,6},{5,7},{6,4},{7,5},{8,10},{9,11},{10,... | collective-permute-start | bytes 294920 | tf_op jit(solution)/shard_map/ppermute | solution.py:378
  171.3 7.0 %collective-permute-start.16 = (bf16[24,3072]{1,0:T(8,128)(2,1)S(1)}, bf16[24,3072]{1,0:T(8,128)(2,1)S(1)}, u32[]{:S(2)}, u32[]{:S(2)}) collective-permute-start(bf16[24,3072]{1,0:T(8,128)(2,1)S(1)} %get-tuple-element.22), channel_id=1, source_target_pairs={{0,1},{1,2},{2,3},{3,0},{4,5},{5,6},{6,7},{7,4},{8,9},{9,10},{10,1... | collective-permute-start | bytes 442376 | tf_op jit(solution)/shard_map/ppermute | solution.py:378
  171.4 16.8 %collective-permute-start.18 = (bf16[24,3072]{1,0:T(8,128)(2,1)S(1)}, bf16[24,3072]{1,0:T(8,128)(2,1)S(1)}, u32[]{:S(2)}, u32[]{:S(2)}) collective-permute-start(bf16[24,3072]{1,0:T(8,128)(2,1)S(1)} %get-tuple-element.23), channel_id=1, source_target_pairs={{0,3},{1,0},{2,1},{3,2},{4,7},{5,4},{6,5},{7,6},{8,11},{9,8},{10,9... | collective-permute-start | bytes 442376 | tf_op jit(solution)/shard_map/ppermute | solution.py:378
  174.9 13.2 %collective-permute-start.17 = (bf16[24,3072]{1,0:T(8,128)(2,1)S(1)}, bf16[24,3072]{1,0:T(8,128)(2,1)S(1)}, u32[]{:S(2)}, u32[]{:S(2)}) collective-permute-start(bf16[24,3072]{1,0:T(8,128)(2,1)S(1)} %get-tuple-element.24), channel_id=1, source_target_pairs={{0,2},{1,3},{2,0},{3,1},{4,6},{5,7},{6,4},{7,5},{8,10},{9,11},{10,... | collective-permute-start | bytes 442376 | tf_op jit(solution)/shard_map/ppermute | solution.py:378
Sparse Core Ops, SparseCore 0:
  53.5 72.6 all-gather.1

commit v5 on v4

--- a/solution.py
+++ b/solution.py
@@ -155,60 +155,11 @@
     )(slots, qkv, *after)
 
 
-def backward_body(slot_ref, qkv_ref, prob_ref, gt_ref, att_ref, *refs):
-    out_ref, q_s, v_s, kt_s = refs[-4:]
-    for s in range(RANKS):
-        rows = pl.ds(s * TOK, TOK)
-        piece = slot_ref[s]
-        q_s[rows, :] = qkv_ref[piece, 0]
-        kt_s[:, rows] = qkv_ref[piece, 1].astype(F32).T.astype(BF16)
-        v_s[rows, :] = qkv_ref[piece, 2]
-    gt = gt_ref[...]
-    prob = prob_ref[0]
-    delta = jnp.sum(gt.astype(F32) * att_ref[...].astype(F32), axis=0, keepdims=True)
-    dprob = dot(v_s[...], gt)
-    dscore = (prob.astype(F32) * (dprob - delta)).astype(BF16)
-    grads = (
-        (dot(kt_s[...], dscore) * SCALE).T.astype(BF16),
-        (dot(dscore, q_s[...]) * SCALE).astype(BF16),
-        dot(prob, gt, NT).astype(BF16),
-    )
-    for s in range(RANKS):
-        for i, grad in enumerate(grads):
-            out_ref[slot_ref[s], i] = grad[s * TOK : (s + 1) * TOK]
-
-
-def backward(slots, qkv, prob, gt, att):
-    return pl.pallas_call(
-        backward_body,
-        grid_spec=pltpu.PrefetchScalarGridSpec(
-            num_scalar_prefetch=1,
-            grid=(NH,),
-            in_specs=[
-                pl.BlockSpec((RANKS, 3, TOK, HD), lambda h, s: (0, 0, 0, h)),
-                pl.BlockSpec((1, SEQ, SEQ), lambda h, s: (h, 0, 0)),
-                pl.BlockSpec((HD, SEQ), lambda h, s: (h, 0)),
-                pl.BlockSpec((HD, SEQ), lambda h, s: (h, 0)),
-            ],
-            out_specs=pl.BlockSpec((RANKS, 3, TOK, HD), lambda h, s: (0, 0, 0, h)),
-            scratch_shapes=[
-                pltpu.VMEM((SEQ, HD), BF16),
-                pltpu.VMEM((SEQ, HD), BF16),
-                pltpu.VMEM((HD, SEQ), BF16),
-            ],
-        ),
-        out_shape=jax.ShapeDtypeStruct((RANKS, 3, TOK, WIDTH), BF16),
-        compiler_params=params(),
-        cost_estimate=cost(8 * NH * SEQ * SEQ * HD, 2 * NH * SEQ * (SEQ + 8 * HD)),
-        name="backward",
-    )(slots, qkv, prob, gt, att)
-
-
 def row_specs(pieces, index):
     return [pl.BlockSpec((p.shape[0], TILE), index) for p in pieces]
 
 
-def weight_body(parts, count, at_ref, att_ref, *refs):
+def weight_body(base, parts, count, at_ref, att_ref, *refs):
     outs, wide_s, att_s = refs[parts + count : -2], refs[-2], refs[-1]
     row = ROW
 
@@ -216,7 +167,7 @@
     def _():
         wide_s[...] = att_ref[...].astype(F32)
         for i in range(YS * ZS):
-            start = pl.multiple_of(at_ref[i] * row, 8)
+            start = pl.multiple_of(at_ref[base + i] * row, 8)
             att_s[pl.ds(i * row, row), :] = wide_s[pl.ds(start, row), :]
 
     rows = jnp.concatenate([ref[...] for ref in refs[:parts]], axis=0)
@@ -229,10 +180,10 @@
             outs[i][...] = block
 
 
-def weight_grad(order, att, pieces, split, after=()):
+def weight_grad(table, base, att, pieces, split, after=()):
     wide = pieces[0].shape[1]
     return pl.pallas_call(
-        functools.partial(weight_body, len(pieces), len(after)),
+        functools.partial(weight_body, base, len(pieces), len(after)),
         grid_spec=pltpu.PrefetchScalarGridSpec(
             num_scalar_prefetch=1,
             grid=(wide // TILE,),
@@ -248,11 +199,12 @@
         compiler_params=params(),
         cost_estimate=cost(2 * WIDTH * SEQ * wide, 2 * (WIDTH * SEQ + SEQ * wide + WIDTH * wide)),
         name="weight_grad",
-    )(order, att, *pieces, *after)
-
-
-def heads_body(counts, parts, w_ref, *refs):
-    out_ref, acc_s = refs[-2:]
+    )(table, att, *pieces, *after)
+
+
+def backward_body(counts, parts, slot_ref, w_ref, *refs):
+    qkv_ref, prob_ref, att_ref = refs[2 * parts : 2 * parts + 3]
+    out_ref, acc_s, gt_s, q_s, v_s, kt_s = refs[-6:]
     step = pl.program_id(0)
 
     @pl.when(step == 0)
@@ -272,28 +224,67 @@
 
     @pl.when(step == begin - 1)
     def _():
-        out_ref[...] = acc_s[...].astype(BF16)
-
-
-def heads_grad(weights, groups, after=()):
+        for h in range(NH):
+            gt_s[h] = acc_s[h * HD : (h + 1) * HD, :].astype(BF16)
+
+    @pl.when(step >= begin)
+    def _():
+        for s in range(RANKS):
+            rows = pl.ds(s * TOK, TOK)
+            piece = slot_ref[s]
+            q_s[rows, :] = qkv_ref[piece, 0]
+            kt_s[:, rows] = qkv_ref[piece, 1].astype(F32).T.astype(BF16)
+            v_s[rows, :] = qkv_ref[piece, 2]
+        gt = gt_s[step - begin]
+        prob = prob_ref[0]
+        delta = jnp.sum(gt.astype(F32) * att_ref[...].astype(F32), axis=0, keepdims=True)
+        dprob = dot(v_s[...], gt)
+        dscore = (prob.astype(F32) * (dprob - delta)).astype(BF16)
+        grads = (
+            (dot(kt_s[...], dscore) * SCALE).T.astype(BF16),
+            (dot(dscore, q_s[...]) * SCALE).astype(BF16),
+            dot(prob, gt, NT).astype(BF16),
+        )
+        for s in range(RANKS):
+            for i, grad in enumerate(grads):
+                out_ref[slot_ref[s], i] = grad[s * TOK : (s + 1) * TOK]
+
+
+def backward(slots, weights, groups, qkv, prob, att, after=()):
     counts = [g[0].shape[1] // TILE for g in groups]
     first, last = counts
-    near = lambda j: (0, jnp.minimum(j, first - 1))
-    far = lambda j: (0, jnp.maximum(j - first, 0))
-    return pl.pallas_call(
-        functools.partial(heads_body, counts, len(groups[0])),
-        grid=(first + last,),
-        in_specs=[pl.BlockSpec((WIDTH, TILE), lambda j: (0, j))]
-        + row_specs(groups[0], near)
-        + row_specs(groups[1], far)
-        + hbm(len(after)),
-        out_specs=pl.BlockSpec((WIDTH, SEQ), lambda j: (0, 0)),
-        scratch_shapes=[pltpu.VMEM((WIDTH, SEQ), F32)],
-        out_shape=jax.ShapeDtypeStruct((WIDTH, SEQ), BF16),
-        compiler_params=params(),
-        cost_estimate=cost(2 * WIDTH * SEQ * D, 2 * (WIDTH * SEQ + SEQ * D + WIDTH * D)),
-        name="heads_grad",
-    )(weights, *groups[0], *groups[1], *after)
+    both = first + last
+    near = lambda j, s: (0, jnp.minimum(j, first - 1))
+    far = lambda j, s: (0, jnp.clip(j - first, 0, last - 1))
+    head = lambda j: jnp.maximum(j - both, 0)
+    return pl.pallas_call(
+        functools.partial(backward_body, counts, len(groups[0])),
+        grid_spec=pltpu.PrefetchScalarGridSpec(
+            num_scalar_prefetch=1,
+            grid=(both + NH,),
+            in_specs=[pl.BlockSpec((WIDTH, TILE), lambda j, s: (0, jnp.minimum(j, both - 1)))]
+            + row_specs(groups[0], near)
+            + row_specs(groups[1], far)
+            + [
+                pl.BlockSpec((RANKS, 3, TOK, HD), lambda j, s: (0, 0, 0, head(j))),
+                pl.BlockSpec((1, SEQ, SEQ), lambda j, s: (head(j), 0, 0)),
+                pl.BlockSpec((HD, SEQ), lambda j, s: (head(j), 0)),
+            ]
+            + hbm(len(after)),
+            out_specs=pl.BlockSpec((RANKS, 3, TOK, HD), lambda j, s: (0, 0, 0, head(j))),
+            scratch_shapes=[
+                pltpu.VMEM((WIDTH, SEQ), F32),
+                pltpu.VMEM((NH, HD, SEQ), BF16),
+                pltpu.VMEM((SEQ, HD), BF16),
+                pltpu.VMEM((SEQ, HD), BF16),
+                pltpu.VMEM((HD, SEQ), BF16),
+            ],
+        ),
+        out_shape=jax.ShapeDtypeStruct((RANKS, 3, TOK, WIDTH), BF16),
+        compiler_params=params(),
+        cost_estimate=cost(2 * WIDTH * SEQ * D + 8 * NH * SEQ * SEQ * HD, 2 * (SEQ * D + WIDTH * D + NH * SEQ * SEQ + 8 * SEQ * WIDTH)),
+        name="backward",
+    )(slots, weights, *groups[0], *groups[1], qkv, prob, att, *after)
 
 
 def rank(x, c):
@@ -350,7 +341,7 @@
     x, c = lax.axis_index("x"), lax.axis_index("c")
     step = 1 - 2 * c
     at = lambda xx, cc: lax.rem(xx + 2 * XS, XS) * CS + cc
-    return jnp.stack(
+    return (
         [
             at(x, c),
             at(x, 1 - c),
@@ -361,7 +352,7 @@
             at(x + 2, c),
             at(x + 2, 1 - c),
         ]
-    ).astype(jnp.int32)
+    )
 
 
 def exchange(value, axis):
@@ -370,7 +361,7 @@
 
 def clip_order(seen):
     y, z = seen * lax.axis_index("y"), lax.axis_index("z")
-    return jnp.stack([(y + i) % YS * ZS + (z + j) % ZS for i in range(YS) for j in range(ZS)]).astype(jnp.int32)
+    return [(y + i) % YS * ZS + (z + j) % ZS for i in range(YS) for j in range(ZS)]
 
 
 def around(parts, axis, size):
@@ -389,7 +380,7 @@
 
 
 def local(queries, keys, values, cotangent, gate, w_out):
-    slots = slot_table()
+    table = jnp.stack(slot_table() + clip_order(0) + clip_order(1)).astype(jnp.int32)
     cot = cotangent[0, 0]
     to_context = lambda value: lax.ppermute(value, "b", [(0, 1)])
 
@@ -401,19 +392,18 @@
     weights = lax.all_gather(hold(w_out[0], sib, qkv), ("y", "z"), axis=0, tiled=True)
     pair0 = pair_up(own, sib, STARTS[0], CHUNKS[0], [])
     near0 = send(pair0, ONWARD)
-    prob, att = forward(slots, qkv, after=[pair0])
-    pair1 = pair_up(own, sib, STARTS[1], CHUNKS[1], [att, near0])
+    prob, att = forward(table, qkv, after=[pair0])
+    pair1 = hold(pair_up(own, sib, STARTS[1], CHUNKS[1], []), near0, att)
     near1 = send(pair1, ONWARD)
     near0 = hold(near0, pair1)
     far0 = hold(send(near0[:TOK], ONWARD), near1)
     pieces0 = [pair0, near0, send(near0, SIBLING), far0, send(far0, SIBLING)]
-    (first_term,) = weight_grad(clip_order(0), att, pieces0, False)
+    (first_term,) = weight_grad(table, RANKS, att, pieces0, False)
     far1 = send(near1[:TOK], ONWARD)
     far1 = hold(far1, first_term)
     pieces1 = [pair1, near1, send(near1, SIBLING), far1, send(far1, SIBLING)]
-    last_term = weight_grad(clip_order(1), att, pieces1, True)
-    gt = heads_grad(weights, (pieces0, pieces1), after=last_term[:1])
-    home = backward(slots, qkv, prob, gt, att)
+    last_term = weight_grad(table, RANKS + YS * ZS, att, pieces1, True)
+    home = backward(table, weights, (pieces0, pieces1), qkv, prob, att, after=last_term[:1])
     got = hold(exchange(first_term, "y"), home)
     last = around(last_term, "y", YS)
     last[0] = hold(last[0], got)

time: 200 us -> 196 us (0.980)
  waiting for transfers between devices: 57.4 us -> 52 us
    ppermute x9, waiting for transfers between devices: 20.3 us -> 17.6 us  [send(): return lax.ppermute(value, ('x', 'c'), perm)]
    unnamed x19 -> x25, local copies, waits for them, and re-layouts: 8.3 us -> 10.7 us
    pallas_call x4 -> x3, Pallas kernels: 33.1 us -> 31.9 us  [the longest x1 18.2 us: backward(): pl.pallas_call(functools.partial(backward_body, counts, len(groups[0])),...]
where the time goes in v5:
time: 196 us; the launch traced here: 193 us
  Pallas kernels  55.6 us (28%)
  starting transfers between devices  54.8 us (28%)
  waiting for transfers between devices  52 us (27%)
  between operations  14.2 us (7%)
  local copies, waits for them, and re-layouts  13.8 us (7%)
  other arithmetic  2.99 us (2%)
    ppermute x9, starting transfers between devices, around(): lax.ppermute(parts[i], axis, [(a, (a + i) % size) for a in range(size)])  19.9 us
    ppermute x1, waiting for transfers between devices, local(): to_context = lambda value: lax.ppermute(value, 'b', [(0, 1)])  19.2 us
    pallas_call x1, Pallas kernels, backward(): pl.pallas_call(functools.partial(backward_body, counts, len(groups[0])),...  18.2 us
    ppermute x9, waiting for transfers between devices, send(): return lax.ppermute(value, ('x', 'c'), perm)  17.6 us
    all_to_all x3, starting transfers between devices, exchange(): return lax.all_to_all(value, axis, split_axis=0, concat_axis=0, tiled=True)  15.3 us
    ppermute x9, starting transfers between devices, send(): return lax.ppermute(value, ('x', 'c'), perm)  15.2 us
    pallas_call x2, Pallas kernels, weight_grad(): pl.pallas_call(functools.partial(weight_body, base, len(pieces), len(afte...  13.7 us
    unnamed x25, local copies, waits for them, and re-layouts  10.7 us
  transfers between devices with their start and end apart: 23, of which 7 were waited for; matrix products, arithmetic and copies ran while one was open for 3% of the time, Pallas kernels for 27%

profile of v5, /device:TPU:1, one launch (start us, length us, event | category | flops | bytes accessed | tf_op | source)
XLA Modules:
  0.0 193.3 jit_solution(743646119051338822)
XLA Ops:
  7.2 1.7 copy.25
  8.8 4.4 %collective-permute-start = (bf16[128,5120]{1,0:T(8,128)(2,1)}, bf16[128,5120]{1,0:T(8,128)(2,1)S(1)}, u32[]{:S(2)}, u32[]{:S(2)}) collective-permute-start(bf16[128,5120]{1,0:T(8,128)(2,1)} %bitcast.52), channel_id=1, source_target_pairs={{0,128},{1,129},{2,130},{3,131},{4,132},{5,133},{6,134},{7,135},{8... | collective-permute-start | bytes 3932168 | tf_op jit(solution)/shard_map/ppermute | solution.py:385
  13.3 3.2 %pack.1.refs_0_ = bf16[8,3,128,384]{3,2,1,0:T(8,128)(2,1)} custom-call(bf16[128,3072]{1,0:T(8,128)(2,1)} %bitcast.54, bf16[128,3072]{1,0:T(8,128)(2,1)} %bitcast.55, bf16[128,3072]{1,0:T(8,128)(2,1)} %bitcast.56), custom_call_target="tpu_custom_call" | custom-call | bytes 4718592 | tf_op jit(solution)/shard_map/pack/pallas_call | solution.py:57
  16.5 5.3 %all-to-all-start = ((bf16[8,3,128,384]{3,2,1,0:T(8,128)(2,1)}), bf16[8,3,128,384]{3,2,1,0:T(8,128)(2,1)}, u32[]{:S(2)}, u32[]{:S(2)}) async-start(bf16[8,3,128,384]{3,2,1,0:T(8,128)(2,1)} %pack.1.refs_0_), calls=%async_computation | async-start | bytes 4718592 | tf_op jit(solution)/shard_map/all_to_all | solution.py:359
  21.8 19.2 %collective-permute-done.other_ref = bf16[128,5120]{1,0:T(8,128)(2,1)S(1)} collective-permute-done((bf16[128,5120]{1,0:T(8,128)(2,1)}, bf16[128,5120]{1,0:T(8,128)(2,1)S(1)}, u32[]{:S(2)}, u32[]{:S(2)}) %collective-permute-start) | collective-permute-done | bytes 1310752 | tf_op jit(solution)/shard_map/ppermute | solution.py:385
  40.9 1.1 copy-done.6
  42.0 2.8 %gated.1.own_ref = bf16[128,5120]{1,0:T(8,128)(2,1)} custom-call(f32[1,5120]{1,0:T(1,128)} %bitcast.57, bf16[128,5120]{1,0:T(8,128)(2,1)} %bitcast.53, bf16[128,5120]{1,0:T(8,128)(2,1)} %copy-done.6, bf16[8,3,128,384]{3,2,1,0:T(8,128)(2,1)} %pack.1.refs_0_), custom_call_target="tpu_custom_call" | custom-call | flops 1310720 | bytes 3932160 | tf_op jit(solution)/shard_map/gated/pallas_call | solution.py:97
  44.8 1.5 collective-permute-start.1
  46.3 4.7 %all-to-all-done.refs_2_.qkv_ref.refs_10_ = bf16[8,3,128,384]{3,2,1,0:T(8,128)(2,1)} async-done(((bf16[8,3,128,384]{3,2,1,0:T(8,128)(2,1)}), bf16[8,3,128,384]{3,2,1,0:T(8,128)(2,1)}, u32[]{:S(2)}, u32[]{:S(2)}) %all-to-all-start) | async-done | bytes 2359328 | tf_op jit(solution)/shard_map/all_to_all | solution.py:359
  51.0 1.1 copy-done.3
  52.1 0.0 all-gather.2.cloned.1.call-update
  52.1 2.1 %pair_up.2.refs_0_ = bf16[256,2048]{1,0:T(8,128)(2,1)} custom-call(bf16[128,5120]{1,0:T(8,128)(2,1)} %gated.1.own_ref, bf16[128,5120]{1,0:T(8,128)(2,1)} %copy-done.3), custom_call_target="tpu_custom_call" | custom-call | bytes 2097152 | tf_op jit(solution)/shard_map/pair_up/pallas_call | solution.py:328
  54.2 0.9 collective-permute-start.2
  55.1 0.7 stack.163.slot_ref.at_ref
  55.8 3.4 %pair_up.3.refs_0_ = bf16[256,3072]{1,0:T(8,128)(2,1)} custom-call(bf16[128,5120]{1,0:T(8,128)(2,1)} %gated.1.own_ref, bf16[128,5120]{1,0:T(8,128)(2,1)} %copy-done.3), custom_call_target="tpu_custom_call" | custom-call | bytes 3145728 | tf_op jit(solution)/shard_map/pair_up/pallas_call | solution.py:328
  59.2 9.0 %forward.1 = (bf16[3,1024,1024]{2,1,0:T(8,128)(2,1)}, bf16[384,1024]{1,0:T(8,128)(2,1)}) custom-call(s32[40]{0:T(128)} %stack.163.slot_ref.at_ref, bf16[8,3,128,384]{3,2,1,0:T(8,128)(2,1)} %all-to-all-done.refs_2_.qkv_ref.refs_10_, bf16[256,2048]{1,0:T(8,128)(2,1)} %pair_up.2.refs_0_), custom_call_target="tpu_custom_call" | custom-call | flops 1610612736 | bytes 9437184 | tf_op jit(solution)/shard_map/forward/pallas_call | solution.py:132
  68.2 0.2 collective-permute-done.2.refs_1_.refs_0_
  68.4 1.0 copy-done.2
  69.4 1.8 collective-permute-start.5
  71.2 1.1 slice.40
  72.3 0.1 collective-permute-start.4
  72.4 1.2 collective-permute-start.3
  73.6 15.7 %collective-permute-done.5.refs_1_.refs_6_ = bf16[256,3072]{1,0:T(8,128)(2,1)} collective-permute-done((bf16[256,3072]{1,0:T(8,128)(2,1)}, bf16[256,3072]{1,0:T(8,128)(2,1)}, u32[]{:S(2)}, u32[]{:S(2)}) %collective-permute-start.5) | collective-permute-done | bytes 1572896 | tf_op jit(solution)/shard_map/ppermute | solution.py:299
  89.3 1.2 slice.41
  90.5 2.8 %collective-permute-start.8 = (bf16[128,3072]{1,0:T(8,128)(2,1)S(1)}, bf16[128,3072]{1,0:T(8,128)(2,1)S(1)}, u32[]{:S(2)}, u32[]{:S(2)}) collective-permute-start(bf16[128,3072]{1,0:T(8,128)(2,1)S(1)} %slice.41), channel_id=1, source_target_pairs={{0,32},{16,112},{32,64},{48,16},{64,96},{80,48},{96,0},{112,80},{1... | collective-permute-start | bytes 2359304 | tf_op jit(solution)/shard_map/ppermute | solution.py:299
  93.2 2.4 %collective-permute-start.7 = (bf16[256,3072]{1,0:T(8,128)(2,1)}, bf16[256,3072]{1,0:T(8,128)(2,1)}, u32[]{:S(2)}, u32[]{:S(2)}) collective-permute-start(bf16[256,3072]{1,0:T(8,128)(2,1)} %collective-permute-done.5.refs_1_.refs_6_), channel_id=1, source_target_pairs={{0,16},{16,0},{32,48},{48,32},{64,80},{80,64},{96,112},{112,96},{1... | collective-permute-start | bytes 4718600 | tf_op jit(solution)/shard_map/ppermute | solution.py:299
  95.6 0.8 copy-done.5
  96.4 4.1 %collective-permute-start.6 = (bf16[128,2048]{1,0:T(8,128)(2,1)}, bf16[128,2048]{1,0:T(8,128)(2,1)S(1)}, u32[]{:S(2)}, u32[]{:S(2)}) collective-permute-start(bf16[128,2048]{1,0:T(8,128)(2,1)} %hold.10.refs_3_), channel_id=1, source_target_pairs={{0,16},{16,0},{32,48},{48,32},{64,80},{80,64},{96,112},{112,96},{1... | collective-permute-start | bytes 1572872 | tf_op jit(solution)/shard_map/ppermute | solution.py:299
  100.6 0.0 collective-permute-done.3.refs_2_
  100.6 1.7 collective-permute-done.6.refs_4_
  102.3 0.8 copy-done.10
  103.1 6.0 %weight_grad.2.refs_1_ = bf16[4,96,2048]{2,1,0:T(8,128)(2,1)} custom-call(s32[40]{0:T(128)} %stack.163.slot_ref.at_ref, bf16[384,1024]{1,0:T(8,128)(2,1)} %get-tuple-element.13.refs_2_.att_ref.refs_12_, bf16[256,2048]{1,0:T(8,128)(2,1)} %pair_up.2.refs_0_, bf16[256,2048]{1,0:T(8,128)(2,1)} %hold.9.refs_1_, bf16[256,2048]{1,0:T(8,128)(2,1)} %copy-done.7, ...), custom_call_target="tpu_custom_call" | custom-call | flops 1610612736 | bytes 6553600 | tf_op jit(solution)/shard_map/weight_grad/pallas_call | solution.py:185
  109.2 0.0 collective-permute-done.8.refs_0_
  109.2 0.9 copy-done.8
  110.1 0.3 collective-permute-start.9
  110.4 4.2 %all-to-all-start.2 = ((bf16[4,96,2048]{2,1,0:T(8,128)(2,1)}), bf16[4,96,2048]{2,1,0:T(8,128)(2,1)S(1)}, u32[]{:S(2)}, u32[]{:S(2)}) async-start(bf16[4,96,2048]{2,1,0:T(8,128)(2,1)} %weight_grad.2.refs_1_), calls=%async_computation.2 | async-start | bytes 3145728 | tf_op jit(solution)/shard_map/all_to_all | solution.py:359
  114.5 0.0 collective-permute-done.9.refs_4_.refs_9_
  114.5 0.0 collective-permute-done.7.refs_2_.refs_7_
  114.5 0.9 copy-done.11
  115.4 7.7 %weight_grad.3 = (bf16[96,3072]{1,0:T(8,128)(2,1)}, bf16[96,3072]{1,0:T(8,128)(2,1)}, bf16[96,3072]{1,0:T(8,128)(2,1)}, bf16[96,3072]{1,0:T(8,128)(2,1)}) custom-call(s32[40]{0:T(128)} %stack.163.slot_ref.at_ref, bf16[384,1024]{1,0:T(8,128)(2,1)} %get-tuple-element.13.refs_2_.att_ref.refs_12_, bf16[256,3072]{1,0:T(8,128)(2,1)} %hold.8.refs_1_.refs_0_.refs_5_, ...), custom_call_target="tpu_custom_call" | custom-call | flops 2415919104 | bytes 9437184 | tf_op jit(solution)/shard_map/weight_grad/pallas_call | solution.py:185
  123.1 1.4 collective-permute-start.13
  124.5 2.4 %collective-permute-start.14 = (bf16[96,3072]{1,0:T(8,128)(2,1)}, bf16[96,3072]{1,0:T(8,128)(2,1)}, u32[]{:S(2)}, u32[]{:S(2)}) collective-permute-start(bf16[96,3072]{1,0:T(8,128)(2,1)} %get-tuple-element.20), channel_id=1, source_target_pairs={{0,8},{4,12},{8,0},{12,4},{1,9},{5,13},{9,1},{13,5},{2,10},{6,14},... | collective-permute-start | bytes 1769480 | tf_op jit(solution)/shard_map/ppermute | solution.py:369
  126.9 1.2 collective-permute-start.15
  128.1 18.2 %backward.1.refs_1_ = bf16[8,3,128,384]{3,2,1,0:T(8,128)(2,1)} custom-call(s32[40]{0:T(128)} %stack.163.slot_ref.at_ref, bf16[384,5120]{1,0:T(8,128)(2,1)} %all-gather.2.cloned.1.call-done.w_ref, bf16[256,2048]{1,0:T(8,128)(2,1)} %pair_up.2.refs_0_, bf16[256,2048]{1,0:T(8,128)(2,1)} %hold.9.refs_1_, bf16[256,2048]{1,0:T(8,128)(2,1)} %copy-done.7, ...), custom_call_target="tpu_custom_call" | custom-call | flops 7247757312 | bytes 27000832 | tf_op jit(solution)/shard_map/backward/pallas_call | solution.py:260
  146.3 0.0 all-to-all-done.2.refs_0_
  146.4 1.1 copy-done
  147.5 5.9 %all-to-all-start.1 = ((bf16[8,3,128,384]{3,2,1,0:T(8,128)(2,1)}), bf16[8,3,128,384]{3,2,1,0:T(8,128)(2,1)}, u32[]{:S(2)}, u32[]{:S(2)}) async-start(bf16[8,3,128,384]{3,2,1,0:T(8,128)(2,1)} %backward.1.refs_1_), calls=%async_computation.1 | async-start | bytes 4718592 | tf_op jit(solution)/shard_map/all_to_all | solution.py:359
  153.4 1.4 copy-done.1
  154.8 0.3 reduce_sum.12
  155.1 3.0 %collective-permute-start.10 = (bf16[24,2048]{1,0:T(8,128)(2,1)S(1)}, bf16[24,2048]{1,0:T(8,128)(2,1)S(1)}, u32[]{:S(2)}, u32[]{:S(2)}) collective-permute-start(bf16[24,2048]{1,0:T(8,128)(2,1)S(1)} %get-tuple-element.25), channel_id=1, source_target_pairs={{0,1},{1,2},{2,3},{3,0},{4,5},{5,6},{6,7},{7,4},{8,9},{9,10},{10,1... | collective-permute-start | bytes 294920 | tf_op jit(solution)/shard_map/ppermute | solution.py:369
  158.1 2.3 %collective-permute-start.12 = (bf16[24,2048]{1,0:T(8,128)(2,1)S(1)}, bf16[24,2048]{1,0:T(8,128)(2,1)S(1)}, u32[]{:S(2)}, u32[]{:S(2)}) collective-permute-start(bf16[24,2048]{1,0:T(8,128)(2,1)S(1)} %get-tuple-element.26), channel_id=1, source_target_pairs={{0,3},{1,0},{2,1},{3,2},{4,7},{5,4},{6,5},{7,6},{8,11},{9,8},{10,9... | collective-permute-start | bytes 294920 | tf_op jit(solution)/shard_map/ppermute | solution.py:369
  160.4 4.3 %collective-permute-start.11 = (bf16[24,2048]{1,0:T(8,128)(2,1)S(1)}, bf16[24,2048]{1,0:T(8,128)(2,1)S(1)}, u32[]{:S(2)}, u32[]{:S(2)}) collective-permute-start(bf16[24,2048]{1,0:T(8,128)(2,1)S(1)} %get-tuple-element.27), channel_id=1, source_target_pairs={{0,2},{1,3},{2,0},{3,1},{4,6},{5,7},{6,4},{7,5},{8,10},{9,11},{10,... | collective-permute-start | bytes 294920 | tf_op jit(solution)/shard_map/ppermute | solution.py:369
  164.7 0.0 collective-permute-done.14
  164.7 1.8 add_convert_fusion
  166.6 0.2 collective-permute-start.16
  166.7 3.5 %collective-permute-start.18 = (bf16[24,3072]{1,0:T(8,128)(2,1)S(1)}, bf16[24,3072]{1,0:T(8,128)(2,1)S(1)}, u32[]{:S(2)}, u32[]{:S(2)}) collective-permute-start(bf16[24,3072]{1,0:T(8,128)(2,1)S(1)} %get-tuple-element.23), channel_id=1, source_target_pairs={{0,3},{1,0},{2,1},{3,2},{4,7},{5,4},{6,5},{7,6},{8,11},{9,8},{10,9... | collective-permute-start | bytes 442376 | tf_op jit(solution)/shard_map/ppermute | solution.py:369
  170.2 0.0 collective-permute-done.10
  170.2 1.6 collective-permute-start.17
  171.9 2.6 %collective-permute-done.16 = bf16[24,3072]{1,0:T(8,128)(2,1)S(1)} collective-permute-done((bf16[24,3072]{1,0:T(8,128)(2,1)S(1)}, bf16[24,3072]{1,0:T(8,128)(2,1)S(1)}, u32[]{:S(2)}, u32[]{:S(2)}) %collective-permute-start.16) | collective-permute-done | bytes 147488 | tf_op jit(solution)/shard_map/ppermute | solution.py:369
  174.5 7.9 %collective-permute-done.18 = bf16[24,3072]{1,0:T(8,128)(2,1)S(1)} collective-permute-done((bf16[24,3072]{1,0:T(8,128)(2,1)S(1)}, bf16[24,3072]{1,0:T(8,128)(2,1)S(1)}, u32[]{:S(2)}, u32[]{:S(2)}) %collective-permute-start.18) | collective-permute-done | bytes 147488 | tf_op jit(solution)/shard_map/ppermute | solution.py:369
  182.4 0.1 convert_add_fusion
  182.4 0.8 maximum_bitcast_fusion
  183.2 0.0 all-to-all-done.1.home_ref
  183.2 3.2 %unpack.1 = (bf16[128,3072]{1,0:T(8,128)(2,1)}, bf16[128,3072]{1,0:T(8,128)(2,1)}, bf16[128,3072]{1,0:T(8,128)(2,1)}) custom-call(bf16[8,3,128,384]{3,2,1,0:T(8,128)(2,1)} %all-to-all-done.1.home_ref), custom_call_target="tpu_custom_call" | custom-call | bytes 4718592 | tf_op jit(solution)/shard_map/unpack/pallas_call | solution.py:77
  (34 shorter events, 0.2 us)
Async XLA Ops:
  8.8 32.1 %collective-permute-start = (bf16[128,5120]{1,0:T(8,128)(2,1)}, bf16[128,5120]{1,0:T(8,128)(2,1)S(1)}, u32[]{:S(2)}, u32[]{:S(2)}) collective-permute-start(bf16[128,5120]{1,0:T(8,128)(2,1)} %bitcast.52), channel_id=1, source_target_pairs={{0,128},{1,129},{2,130},{3,131},{4,132},{5,133},{6,134},{7,135},{8... | collective-permute-start | bytes 3932168 | tf_op jit(solution)/shard_map/ppermute | solution.py:385
  16.5 34.5 %all-to-all-start = ((bf16[8,3,128,384]{3,2,1,0:T(8,128)(2,1)}), bf16[8,3,128,384]{3,2,1,0:T(8,128)(2,1)}, u32[]{:S(2)}, u32[]{:S(2)}) async-start(bf16[8,3,128,384]{3,2,1,0:T(8,128)(2,1)} %pack.1.refs_0_), calls=%async_computation | async-start | bytes 4718592 | tf_op jit(solution)/shard_map/all_to_all | solution.py:359
  21.8 106.4 %all-gather.2.cloned.1.call-start = ((), (), s32[]{:S(2)}) async-start(), calls=%async_computation.3 | async-start | bytes 4177920 | tf_op jit(solution)/shard_map/all_gather | solution.py:392
  40.9 1.1 copy-start.6
  44.8 6.2 %collective-permute-start.1 = (bf16[128,5120]{1,0:T(8,128)(2,1)}, bf16[128,5120]{1,0:T(8,128)(2,1)S(1)}, u32[]{:S(2)}, u32[]{:S(2)}) collective-permute-start(bf16[128,5120]{1,0:T(8,128)(2,1)} %gated.1.own_ref), channel_id=1, source_target_pairs={{0,16},{16,0},{32,48},{48,32},{64,80},{80,64},{96,112},{112,96},{1... | collective-permute-start | bytes 3932168 | tf_op jit(solution)/shard_map/ppermute | solution.py:299
  51.0 1.1 copy-start.3
  54.2 14.2 %collective-permute-start.2 = (bf16[256,2048]{1,0:T(8,128)(2,1)}, bf16[256,2048]{1,0:T(8,128)(2,1)S(1)}, u32[]{:S(2)}, u32[]{:S(2)}) collective-permute-start(bf16[256,2048]{1,0:T(8,128)(2,1)} %pair_up.2.refs_0_), channel_id=1, source_target_pairs={{0,32},{16,112},{32,64},{48,16},{64,96},{80,48},{96,0},{112,80},{1... | collective-permute-start | bytes 3145736 | tf_op jit(solution)/shard_map/ppermute | solution.py:299
  68.4 1.0 copy-start.2
  69.4 19.9 %collective-permute-start.5 = (bf16[256,3072]{1,0:T(8,128)(2,1)}, bf16[256,3072]{1,0:T(8,128)(2,1)}, u32[]{:S(2)}, u32[]{:S(2)}) collective-permute-start(bf16[256,3072]{1,0:T(8,128)(2,1)} %hold.8.refs_1_.refs_0_.refs_5_), channel_id=1, source_target_pairs={{0,32},{16,112},{32,64},{48,16},{64,96},{80,48},{96,0},{112,80},{1... | collective-permute-start | bytes 4718600 | tf_op jit(solution)/shard_map/ppermute | solution.py:299
  72.3 23.4 %collective-permute-start.4 = (bf16[128,2048]{1,0:T(8,128)(2,1)S(1)}, bf16[128,2048]{1,0:T(8,128)(2,1)S(1)}, u32[]{:S(2)}, u32[]{:S(2)}) collective-permute-start(bf16[128,2048]{1,0:T(8,128)(2,1)S(1)} %slice.40), channel_id=1, source_target_pairs={{0,32},{16,112},{32,64},{48,16},{64,96},{80,48},{96,0},{112,80},{1... | collective-permute-start | bytes 1572872 | tf_op jit(solution)/shard_map/ppermute | solution.py:299
  72.4 28.2 %collective-permute-start.3 = (bf16[256,2048]{1,0:T(8,128)(2,1)}, bf16[256,2048]{1,0:T(8,128)(2,1)S(1)}, u32[]{:S(2)}, u32[]{:S(2)}) collective-permute-start(bf16[256,2048]{1,0:T(8,128)(2,1)} %hold.9.refs_1_), channel_id=1, source_target_pairs={{0,16},{16,0},{32,48},{48,32},{64,80},{80,64},{96,112},{112,96},{1... | collective-permute-start | bytes 3145736 | tf_op jit(solution)/shard_map/ppermute | solution.py:299
  90.5 18.7 %collective-permute-start.8 = (bf16[128,3072]{1,0:T(8,128)(2,1)S(1)}, bf16[128,3072]{1,0:T(8,128)(2,1)S(1)}, u32[]{:S(2)}, u32[]{:S(2)}) collective-permute-start(bf16[128,3072]{1,0:T(8,128)(2,1)S(1)} %slice.41), channel_id=1, source_target_pairs={{0,32},{16,112},{32,64},{48,16},{64,96},{80,48},{96,0},{112,80},{1... | collective-permute-start | bytes 2359304 | tf_op jit(solution)/shard_map/ppermute | solution.py:299
  93.2 21.3 %collective-permute-start.7 = (bf16[256,3072]{1,0:T(8,128)(2,1)}, bf16[256,3072]{1,0:T(8,128)(2,1)}, u32[]{:S(2)}, u32[]{:S(2)}) collective-permute-start(bf16[256,3072]{1,0:T(8,128)(2,1)} %collective-permute-done.5.refs_1_.refs_6_), channel_id=1, source_target_pairs={{0,16},{16,0},{32,48},{48,32},{64,80},{80,64},{96,112},{112,96},{1... | collective-permute-start | bytes 4718600 | tf_op jit(solution)/shard_map/ppermute | solution.py:299
  95.6 0.8 copy-start.5
  96.4 5.9 %collective-permute-start.6 = (bf16[128,2048]{1,0:T(8,128)(2,1)}, bf16[128,2048]{1,0:T(8,128)(2,1)S(1)}, u32[]{:S(2)}, u32[]{:S(2)}) collective-permute-start(bf16[128,2048]{1,0:T(8,128)(2,1)} %hold.10.refs_3_), channel_id=1, source_target_pairs={{0,16},{16,0},{32,48},{48,32},{64,80},{80,64},{96,112},{112,96},{1... | collective-permute-start | bytes 1572872 | tf_op jit(solution)/shard_map/ppermute | solution.py:299
  100.6 1.7 copy-start.7
  102.3 0.8 copy-start.10
  109.2 0.9 copy-start.8
  110.1 4.5 %collective-permute-start.9 = (bf16[128,3072]{1,0:T(8,128)(2,1)}, bf16[128,3072]{1,0:T(8,128)(2,1)S(1)}, u32[]{:S(2)}, u32[]{:S(2)}) collective-permute-start(bf16[128,3072]{1,0:T(8,128)(2,1)} %hold.11.refs_3_.refs_8_), channel_id=1, source_target_pairs={{0,16},{16,0},{32,48},{48,32},{64,80},{80,64},{96,112},{112,96},{1... | collective-permute-start | bytes 2359304 | tf_op jit(solution)/shard_map/ppermute | solution.py:299
  110.4 36.0 %all-to-all-start.2 = ((bf16[4,96,2048]{2,1,0:T(8,128)(2,1)}), bf16[4,96,2048]{2,1,0:T(8,128)(2,1)S(1)}, u32[]{:S(2)}, u32[]{:S(2)}) async-start(bf16[4,96,2048]{2,1,0:T(8,128)(2,1)} %weight_grad.2.refs_1_), calls=%async_computation.2 | async-start | bytes 3145728 | tf_op jit(solution)/shard_map/all_to_all | solution.py:359
  114.5 0.9 copy-start.11
  123.1 37.3 %collective-permute-start.13 = (bf16[96,3072]{1,0:T(8,128)(2,1)}, bf16[96,3072]{1,0:T(8,128)(2,1)S(1)}, u32[]{:S(2)}, u32[]{:S(2)}) collective-permute-start(bf16[96,3072]{1,0:T(8,128)(2,1)} %get-tuple-element.19), channel_id=1, source_target_pairs={{0,4},{4,8},{8,12},{12,0},{1,5},{5,9},{9,13},{13,1},{2,6},{6,10},{... | collective-permute-start | bytes 1769480 | tf_op jit(solution)/shard_map/ppermute | solution.py:369
  124.5 40.2 %collective-permute-start.14 = (bf16[96,3072]{1,0:T(8,128)(2,1)}, bf16[96,3072]{1,0:T(8,128)(2,1)}, u32[]{:S(2)}, u32[]{:S(2)}) collective-permute-start(bf16[96,3072]{1,0:T(8,128)(2,1)} %get-tuple-element.20), channel_id=1, source_target_pairs={{0,8},{4,12},{8,0},{12,4},{1,9},{5,13},{9,1},{13,5},{2,10},{6,14},... | collective-permute-start | bytes 1769480 | tf_op jit(solution)/shard_map/ppermute | solution.py:369
  126.9 37.8 %collective-permute-start.15 = (bf16[96,3072]{1,0:T(8,128)(2,1)}, bf16[96,3072]{1,0:T(8,128)(2,1)}, u32[]{:S(2)}, u32[]{:S(2)}) collective-permute-start(bf16[96,3072]{1,0:T(8,128)(2,1)} %get-tuple-element.21), channel_id=1, source_target_pairs={{0,12},{4,0},{8,4},{12,8},{1,13},{5,1},{9,5},{13,9},{2,14},{6,2},{... | collective-permute-start | bytes 1769480 | tf_op jit(solution)/shard_map/ppermute | solution.py:369
  146.3 1.1 copy-start
  147.5 35.8 %all-to-all-start.1 = ((bf16[8,3,128,384]{3,2,1,0:T(8,128)(2,1)}), bf16[8,3,128,384]{3,2,1,0:T(8,128)(2,1)}, u32[]{:S(2)}, u32[]{:S(2)}) async-start(bf16[8,3,128,384]{3,2,1,0:T(8,128)(2,1)} %backward.1.refs_1_), calls=%async_computation.1 | async-start | bytes 4718592 | tf_op jit(solution)/shard_map/all_to_all | solution.py:359
  153.4 1.4 copy-start.1
  154.8 10.0 %copy-start.4 = (bf16[96,3072]{1,0:T(8,128)(2,1)S(1)}, bf16[96,3072]{1,0:T(8,128)(2,1)}, u32[]{:S(2)}) copy-start(bf16[96,3072]{1,0:T(8,128)(2,1)} %hold.13) | copy-start | bytes 1769476
  155.1 15.1 %collective-permute-start.10 = (bf16[24,2048]{1,0:T(8,128)(2,1)S(1)}, bf16[24,2048]{1,0:T(8,128)(2,1)S(1)}, u32[]{:S(2)}, u32[]{:S(2)}) collective-permute-start(bf16[24,2048]{1,0:T(8,128)(2,1)S(1)} %get-tuple-element.25), channel_id=1, source_target_pairs={{0,1},{1,2},{2,3},{3,0},{4,5},{5,6},{6,7},{7,4},{8,9},{9,10},{10,1... | collective-permute-start | bytes 294920 | tf_op jit(solution)/shard_map/ppermute | solution.py:369
  158.1 13.8 %collective-permute-start.12 = (bf16[24,2048]{1,0:T(8,128)(2,1)S(1)}, bf16[24,2048]{1,0:T(8,128)(2,1)S(1)}, u32[]{:S(2)}, u32[]{:S(2)}) collective-permute-start(bf16[24,2048]{1,0:T(8,128)(2,1)S(1)} %get-tuple-element.26), channel_id=1, source_target_pairs={{0,3},{1,0},{2,1},{3,2},{4,7},{5,4},{6,5},{7,6},{8,11},{9,8},{10,9... | collective-permute-start | bytes 294920 | tf_op jit(solution)/shard_map/ppermute | solution.py:369
  160.4 4.4 %copy-start.9 = (bf16[96,3072]{1,0:T(8,128)(2,1)}, bf16[96,3072]{1,0:T(8,128)(2,1)S(1)}, u32[]{:S(2)}) copy-start(bf16[96,3072]{1,0:T(8,128)(2,1)S(1)} %collective-permute-done.13) | copy-start | bytes 1769476
  160.4 11.4 %collective-permute-start.11 = (bf16[24,2048]{1,0:T(8,128)(2,1)S(1)}, bf16[24,2048]{1,0:T(8,128)(2,1)S(1)}, u32[]{:S(2)}, u32[]{:S(2)}) collective-permute-start(bf16[24,2048]{1,0:T(8,128)(2,1)S(1)} %get-tuple-element.27), channel_id=1, source_target_pairs={{0,2},{1,3},{2,0},{3,1},{4,6},{5,7},{6,4},{7,5},{8,10},{9,11},{10,... | collective-permute-start | bytes 294920 | tf_op jit(solution)/shard_map/ppermute | solution.py:369
  166.6 7.9 %collective-permute-start.16 = (bf16[24,3072]{1,0:T(8,128)(2,1)S(1)}, bf16[24,3072]{1,0:T(8,128)(2,1)S(1)}, u32[]{:S(2)}, u32[]{:S(2)}) collective-permute-start(bf16[24,3072]{1,0:T(8,128)(2,1)S(1)} %get-tuple-element.22), channel_id=1, source_target_pairs={{0,1},{1,2},{2,3},{3,0},{4,5},{5,6},{6,7},{7,4},{8,9},{9,10},{10,1... | collective-permute-start | bytes 442376 | tf_op jit(solution)/shard_map/ppermute | solution.py:369
  166.7 15.6 %collective-permute-start.18 = (bf16[24,3072]{1,0:T(8,128)(2,1)S(1)}, bf16[24,3072]{1,0:T(8,128)(2,1)S(1)}, u32[]{:S(2)}, u32[]{:S(2)}) collective-permute-start(bf16[24,3072]{1,0:T(8,128)(2,1)S(1)} %get-tuple-element.23), channel_id=1, source_target_pairs={{0,3},{1,0},{2,1},{3,2},{4,7},{5,4},{6,5},{7,6},{8,11},{9,8},{10,9... | collective-permute-start | bytes 442376 | tf_op jit(solution)/shard_map/ppermute | solution.py:369
  170.2 12.1 %collective-permute-start.17 = (bf16[24,3072]{1,0:T(8,128)(2,1)S(1)}, bf16[24,3072]{1,0:T(8,128)(2,1)S(1)}, u32[]{:S(2)}, u32[]{:S(2)}) collective-permute-start(bf16[24,3072]{1,0:T(8,128)(2,1)S(1)} %get-tuple-element.24), channel_id=1, source_target_pairs={{0,2},{1,3},{2,0},{3,1},{4,6},{5,7},{6,4},{7,5},{8,10},{9,11},{10,... | collective-permute-start | bytes 442376 | tf_op jit(solution)/shard_map/ppermute | solution.py:369
Sparse Core Ops, SparseCore 0:
  52.3 72.9 all-gather.1

commit v6 on v5

--- a/solution.py
+++ b/solution.py
@@ -67,17 +67,18 @@
 
 
 def unpack_body(home_ref, *outs):
-    for r in range(RANKS):
+    for r in range(home_ref.shape[0]):
         for i, out in enumerate(outs):
             out[:, r * WIDTH : (r + 1) * WIDTH] = home_ref[r, i]
 
 
 def unpack(home):
-    whole = pl.BlockSpec((TOK, RANKS * WIDTH), lambda j: (0, 0))
+    half = RANKS // 2
+    whole = pl.BlockSpec((TOK, half * WIDTH), lambda j: (0, j))
     return pl.pallas_call(
         unpack_body,
-        grid=(1,),
-        in_specs=[pl.BlockSpec(home.shape, lambda j: (0, 0, 0, 0))],
+        grid=(2,),
+        in_specs=[pl.BlockSpec((half, 3, TOK, WIDTH), lambda j: (j, 0, 0, 0))],
         out_specs=[whole] * 3,
         out_shape=[jax.ShapeDtypeStruct((TOK, RANKS * WIDTH), BF16)] * 3,
         compiler_params=params(),

time: 196 us -> 195 us (level)
  no operation moved by 1% of the time
where the time goes in v6:
time: 195 us; the launch traced here: 193 us
  Pallas kernels  55.2 us (28%)
  starting transfers between devices  54.8 us (28%)
  waiting for transfers between devices  52 us (27%)
  between operations  14.2 us (7%)
  local copies, waits for them, and re-layouts  13.8 us (7%)
  other arithmetic  2.99 us (2%)
    ppermute x9, starting transfers between devices, around(): lax.ppermute(parts[i], axis, [(a, (a + i) % size) for a in range(size)])  19.9 us
    ppermute x1, waiting for transfers between devices, local(): to_context = lambda value: lax.ppermute(value, 'b', [(0, 1)])  19.2 us
    pallas_call x1, Pallas kernels, backward(): pl.pallas_call(functools.partial(backward_body, counts, len(groups[0])),...  18.2 us
    ppermute x9, waiting for transfers between devices, send(): return lax.ppermute(value, ('x', 'c'), perm)  17.6 us
    all_to_all x3, starting transfers between devices, exchange(): return lax.all_to_all(value, axis, split_axis=0, concat_axis=0, tiled=True)  15.3 us
    ppermute x9, starting transfers between devices, send(): return lax.ppermute(value, ('x', 'c'), perm)  15.2 us
    pallas_call x2, Pallas kernels, weight_grad(): pl.pallas_call(functools.partial(weight_body, base, len(pieces), len(afte...  13.7 us
    unnamed x25, local copies, waits for them, and re-layouts  10.7 us
  transfers between devices with their start and end apart: 23, of which 7 were waited for; matrix products, arithmetic and copies ran while one was open for 3% of the time, Pallas kernels for 27%

profile of v6, /device:TPU:1, one launch (start us, length us, event | category | flops | bytes accessed | tf_op | source)
XLA Modules:
  0.0 192.9 jit_solution(16731306774959159826)
XLA Ops:
  7.2 1.7 copy.25
  8.8 4.4 %collective-permute-start = (bf16[128,5120]{1,0:T(8,128)(2,1)}, bf16[128,5120]{1,0:T(8,128)(2,1)S(1)}, u32[]{:S(2)}, u32[]{:S(2)}) collective-permute-start(bf16[128,5120]{1,0:T(8,128)(2,1)} %bitcast.52), channel_id=1, source_target_pairs={{0,128},{1,129},{2,130},{3,131},{4,132},{5,133},{6,134},{7,135},{8... | collective-permute-start | bytes 3932168 | tf_op jit(solution)/shard_map/ppermute | solution.py:386
  13.3 3.2 %pack.1.refs_0_ = bf16[8,3,128,384]{3,2,1,0:T(8,128)(2,1)} custom-call(bf16[128,3072]{1,0:T(8,128)(2,1)} %bitcast.54, bf16[128,3072]{1,0:T(8,128)(2,1)} %bitcast.55, bf16[128,3072]{1,0:T(8,128)(2,1)} %bitcast.56), custom_call_target="tpu_custom_call" | custom-call | bytes 4718592 | tf_op jit(solution)/shard_map/pack/pallas_call | solution.py:57
  16.5 5.3 %all-to-all-start = ((bf16[8,3,128,384]{3,2,1,0:T(8,128)(2,1)}), bf16[8,3,128,384]{3,2,1,0:T(8,128)(2,1)}, u32[]{:S(2)}, u32[]{:S(2)}) async-start(bf16[8,3,128,384]{3,2,1,0:T(8,128)(2,1)} %pack.1.refs_0_), calls=%async_computation | async-start | bytes 4718592 | tf_op jit(solution)/shard_map/all_to_all | solution.py:360
  21.8 19.2 %collective-permute-done.other_ref = bf16[128,5120]{1,0:T(8,128)(2,1)S(1)} collective-permute-done((bf16[128,5120]{1,0:T(8,128)(2,1)}, bf16[128,5120]{1,0:T(8,128)(2,1)S(1)}, u32[]{:S(2)}, u32[]{:S(2)}) %collective-permute-start) | collective-permute-done | bytes 1310752 | tf_op jit(solution)/shard_map/ppermute | solution.py:386
  40.9 1.1 copy-done.6
  42.0 2.8 %gated.1.own_ref = bf16[128,5120]{1,0:T(8,128)(2,1)} custom-call(f32[1,5120]{1,0:T(1,128)} %bitcast.57, bf16[128,5120]{1,0:T(8,128)(2,1)} %bitcast.53, bf16[128,5120]{1,0:T(8,128)(2,1)} %copy-done.6, bf16[8,3,128,384]{3,2,1,0:T(8,128)(2,1)} %pack.1.refs_0_), custom_call_target="tpu_custom_call" | custom-call | flops 1310720 | bytes 3932160 | tf_op jit(solution)/shard_map/gated/pallas_call | solution.py:98
  44.8 1.5 collective-permute-start.1
  46.3 4.7 %all-to-all-done.refs_2_.qkv_ref.refs_10_ = bf16[8,3,128,384]{3,2,1,0:T(8,128)(2,1)} async-done(((bf16[8,3,128,384]{3,2,1,0:T(8,128)(2,1)}), bf16[8,3,128,384]{3,2,1,0:T(8,128)(2,1)}, u32[]{:S(2)}, u32[]{:S(2)}) %all-to-all-start) | async-done | bytes 2359328 | tf_op jit(solution)/shard_map/all_to_all | solution.py:360
  51.0 1.1 copy-done.3
  52.1 0.0 all-gather.2.cloned.1.call-update
  52.1 2.1 %pair_up.2.refs_0_ = bf16[256,2048]{1,0:T(8,128)(2,1)} custom-call(bf16[128,5120]{1,0:T(8,128)(2,1)} %gated.1.own_ref, bf16[128,5120]{1,0:T(8,128)(2,1)} %copy-done.3), custom_call_target="tpu_custom_call" | custom-call | bytes 2097152 | tf_op jit(solution)/shard_map/pair_up/pallas_call | solution.py:329
  54.2 0.9 collective-permute-start.2
  55.1 0.7 stack.163.slot_ref.at_ref
  55.8 3.4 %pair_up.3.refs_0_ = bf16[256,3072]{1,0:T(8,128)(2,1)} custom-call(bf16[128,5120]{1,0:T(8,128)(2,1)} %gated.1.own_ref, bf16[128,5120]{1,0:T(8,128)(2,1)} %copy-done.3), custom_call_target="tpu_custom_call" | custom-call | bytes 3145728 | tf_op jit(solution)/shard_map/pair_up/pallas_call | solution.py:329
  59.2 9.0 %forward.1 = (bf16[3,1024,1024]{2,1,0:T(8,128)(2,1)}, bf16[384,1024]{1,0:T(8,128)(2,1)}) custom-call(s32[40]{0:T(128)} %stack.163.slot_ref.at_ref, bf16[8,3,128,384]{3,2,1,0:T(8,128)(2,1)} %all-to-all-done.refs_2_.qkv_ref.refs_10_, bf16[256,2048]{1,0:T(8,128)(2,1)} %pair_up.2.refs_0_), custom_call_target="tpu_custom_call" | custom-call | flops 1610612736 | bytes 9437184 | tf_op jit(solution)/shard_map/forward/pallas_call | solution.py:133
  68.2 0.2 collective-permute-done.2.refs_1_.refs_0_
  68.4 1.0 copy-done.2
  69.4 1.8 collective-permute-start.5
  71.2 1.1 slice.40
  72.3 0.1 collective-permute-start.4
  72.4 1.2 collective-permute-start.3
  73.6 15.7 %collective-permute-done.5.refs_1_.refs_6_ = bf16[256,3072]{1,0:T(8,128)(2,1)} collective-permute-done((bf16[256,3072]{1,0:T(8,128)(2,1)}, bf16[256,3072]{1,0:T(8,128)(2,1)}, u32[]{:S(2)}, u32[]{:S(2)}) %collective-permute-start.5) | collective-permute-done | bytes 1572896 | tf_op jit(solution)/shard_map/ppermute | solution.py:300
  89.3 1.2 slice.41
  90.5 2.8 %collective-permute-start.8 = (bf16[128,3072]{1,0:T(8,128)(2,1)S(1)}, bf16[128,3072]{1,0:T(8,128)(2,1)S(1)}, u32[]{:S(2)}, u32[]{:S(2)}) collective-permute-start(bf16[128,3072]{1,0:T(8,128)(2,1)S(1)} %slice.41), channel_id=1, source_target_pairs={{0,32},{16,112},{32,64},{48,16},{64,96},{80,48},{96,0},{112,80},{1... | collective-permute-start | bytes 2359304 | tf_op jit(solution)/shard_map/ppermute | solution.py:300
  93.2 2.4 %collective-permute-start.7 = (bf16[256,3072]{1,0:T(8,128)(2,1)}, bf16[256,3072]{1,0:T(8,128)(2,1)}, u32[]{:S(2)}, u32[]{:S(2)}) collective-permute-start(bf16[256,3072]{1,0:T(8,128)(2,1)} %collective-permute-done.5.refs_1_.refs_6_), channel_id=1, source_target_pairs={{0,16},{16,0},{32,48},{48,32},{64,80},{80,64},{96,112},{112,96},{1... | collective-permute-start | bytes 4718600 | tf_op jit(solution)/shard_map/ppermute | solution.py:300
  95.6 0.8 copy-done.5
  96.4 4.1 %collective-permute-start.6 = (bf16[128,2048]{1,0:T(8,128)(2,1)}, bf16[128,2048]{1,0:T(8,128)(2,1)S(1)}, u32[]{:S(2)}, u32[]{:S(2)}) collective-permute-start(bf16[128,2048]{1,0:T(8,128)(2,1)} %hold.10.refs_3_), channel_id=1, source_target_pairs={{0,16},{16,0},{32,48},{48,32},{64,80},{80,64},{96,112},{112,96},{1... | collective-permute-start | bytes 1572872 | tf_op jit(solution)/shard_map/ppermute | solution.py:300
  100.6 0.0 collective-permute-done.3.refs_2_
  100.6 1.7 collective-permute-done.6.refs_4_
  102.3 0.8 copy-done.10
  103.1 6.0 %weight_grad.2.refs_1_ = bf16[4,96,2048]{2,1,0:T(8,128)(2,1)} custom-call(s32[40]{0:T(128)} %stack.163.slot_ref.at_ref, bf16[384,1024]{1,0:T(8,128)(2,1)} %get-tuple-element.13.refs_2_.att_ref.refs_12_, bf16[256,2048]{1,0:T(8,128)(2,1)} %pair_up.2.refs_0_, bf16[256,2048]{1,0:T(8,128)(2,1)} %hold.9.refs_1_, bf16[256,2048]{1,0:T(8,128)(2,1)} %copy-done.7, ...), custom_call_target="tpu_custom_call" | custom-call | flops 1610612736 | bytes 6553600 | tf_op jit(solution)/shard_map/weight_grad/pallas_call | solution.py:186
  109.2 0.0 collective-permute-done.8.refs_0_
  109.2 0.9 copy-done.8
  110.1 0.3 collective-permute-start.9
  110.4 4.2 %all-to-all-start.2 = ((bf16[4,96,2048]{2,1,0:T(8,128)(2,1)}), bf16[4,96,2048]{2,1,0:T(8,128)(2,1)S(1)}, u32[]{:S(2)}, u32[]{:S(2)}) async-start(bf16[4,96,2048]{2,1,0:T(8,128)(2,1)} %weight_grad.2.refs_1_), calls=%async_computation.2 | async-start | bytes 3145728 | tf_op jit(solution)/shard_map/all_to_all | solution.py:360
  114.5 0.0 collective-permute-done.9.refs_4_.refs_9_
  114.5 0.0 collective-permute-done.7.refs_2_.refs_7_
  114.5 0.9 copy-done.11
  115.4 7.7 %weight_grad.3 = (bf16[96,3072]{1,0:T(8,128)(2,1)}, bf16[96,3072]{1,0:T(8,128)(2,1)}, bf16[96,3072]{1,0:T(8,128)(2,1)}, bf16[96,3072]{1,0:T(8,128)(2,1)}) custom-call(s32[40]{0:T(128)} %stack.163.slot_ref.at_ref, bf16[384,1024]{1,0:T(8,128)(2,1)} %get-tuple-element.13.refs_2_.att_ref.refs_12_, bf16[256,3072]{1,0:T(8,128)(2,1)} %hold.8.refs_1_.refs_0_.refs_5_, ...), custom_call_target="tpu_custom_call" | custom-call | flops 2415919104 | bytes 9437184 | tf_op jit(solution)/shard_map/weight_grad/pallas_call | solution.py:186
  123.1 1.4 collective-permute-start.13
  124.5 2.4 %collective-permute-start.14 = (bf16[96,3072]{1,0:T(8,128)(2,1)}, bf16[96,3072]{1,0:T(8,128)(2,1)}, u32[]{:S(2)}, u32[]{:S(2)}) collective-permute-start(bf16[96,3072]{1,0:T(8,128)(2,1)} %get-tuple-element.20), channel_id=1, source_target_pairs={{0,8},{4,12},{8,0},{12,4},{1,9},{5,13},{9,1},{13,5},{2,10},{6,14},... | collective-permute-start | bytes 1769480 | tf_op jit(solution)/shard_map/ppermute | solution.py:370
  126.9 1.2 collective-permute-start.15
  128.1 18.2 %backward.1.refs_1_ = bf16[8,3,128,384]{3,2,1,0:T(8,128)(2,1)} custom-call(s32[40]{0:T(128)} %stack.163.slot_ref.at_ref, bf16[384,5120]{1,0:T(8,128)(2,1)} %all-gather.2.cloned.1.call-done.w_ref, bf16[256,2048]{1,0:T(8,128)(2,1)} %pair_up.2.refs_0_, bf16[256,2048]{1,0:T(8,128)(2,1)} %hold.9.refs_1_, bf16[256,2048]{1,0:T(8,128)(2,1)} %copy-done.7, ...), custom_call_target="tpu_custom_call" | custom-call | flops 7247757312 | bytes 27000832 | tf_op jit(solution)/shard_map/backward/pallas_call | solution.py:261
  146.3 0.0 all-to-all-done.2.refs_0_
  146.4 1.1 copy-done
  147.5 5.9 %all-to-all-start.1 = ((bf16[8,3,128,384]{3,2,1,0:T(8,128)(2,1)}), bf16[8,3,128,384]{3,2,1,0:T(8,128)(2,1)}, u32[]{:S(2)}, u32[]{:S(2)}) async-start(bf16[8,3,128,384]{3,2,1,0:T(8,128)(2,1)} %backward.1.refs_1_), calls=%async_computation.1 | async-start | bytes 4718592 | tf_op jit(solution)/shard_map/all_to_all | solution.py:360
  153.4 1.4 copy-done.1
  154.8 0.3 reduce_sum.12
  155.1 3.0 %collective-permute-start.10 = (bf16[24,2048]{1,0:T(8,128)(2,1)S(1)}, bf16[24,2048]{1,0:T(8,128)(2,1)S(1)}, u32[]{:S(2)}, u32[]{:S(2)}) collective-permute-start(bf16[24,2048]{1,0:T(8,128)(2,1)S(1)} %get-tuple-element.25), channel_id=1, source_target_pairs={{0,1},{1,2},{2,3},{3,0},{4,5},{5,6},{6,7},{7,4},{8,9},{9,10},{10,1... | collective-permute-start | bytes 294920 | tf_op jit(solution)/shard_map/ppermute | solution.py:370
  158.1 2.3 %collective-permute-start.12 = (bf16[24,2048]{1,0:T(8,128)(2,1)S(1)}, bf16[24,2048]{1,0:T(8,128)(2,1)S(1)}, u32[]{:S(2)}, u32[]{:S(2)}) collective-permute-start(bf16[24,2048]{1,0:T(8,128)(2,1)S(1)} %get-tuple-element.26), channel_id=1, source_target_pairs={{0,3},{1,0},{2,1},{3,2},{4,7},{5,4},{6,5},{7,6},{8,11},{9,8},{10,9... | collective-permute-start | bytes 294920 | tf_op jit(solution)/shard_map/ppermute | solution.py:370
  160.4 4.3 %collective-permute-start.11 = (bf16[24,2048]{1,0:T(8,128)(2,1)S(1)}, bf16[24,2048]{1,0:T(8,128)(2,1)S(1)}, u32[]{:S(2)}, u32[]{:S(2)}) collective-permute-start(bf16[24,2048]{1,0:T(8,128)(2,1)S(1)} %get-tuple-element.27), channel_id=1, source_target_pairs={{0,2},{1,3},{2,0},{3,1},{4,6},{5,7},{6,4},{7,5},{8,10},{9,11},{10,... | collective-permute-start | bytes 294920 | tf_op jit(solution)/shard_map/ppermute | solution.py:370
  164.7 0.0 collective-permute-done.14
  164.7 1.8 add_convert_fusion
  166.6 0.2 collective-permute-start.16
  166.7 3.5 %collective-permute-start.18 = (bf16[24,3072]{1,0:T(8,128)(2,1)S(1)}, bf16[24,3072]{1,0:T(8,128)(2,1)S(1)}, u32[]{:S(2)}, u32[]{:S(2)}) collective-permute-start(bf16[24,3072]{1,0:T(8,128)(2,1)S(1)} %get-tuple-element.23), channel_id=1, source_target_pairs={{0,3},{1,0},{2,1},{3,2},{4,7},{5,4},{6,5},{7,6},{8,11},{9,8},{10,9... | collective-permute-start | bytes 442376 | tf_op jit(solution)/shard_map/ppermute | solution.py:370
  170.2 0.0 collective-permute-done.10
  170.2 1.6 collective-permute-start.17
  171.9 2.6 %collective-permute-done.16 = bf16[24,3072]{1,0:T(8,128)(2,1)S(1)} collective-permute-done((bf16[24,3072]{1,0:T(8,128)(2,1)S(1)}, bf16[24,3072]{1,0:T(8,128)(2,1)S(1)}, u32[]{:S(2)}, u32[]{:S(2)}) %collective-permute-start.16) | collective-permute-done | bytes 147488 | tf_op jit(solution)/shard_map/ppermute | solution.py:370
  174.5 7.9 %collective-permute-done.18 = bf16[24,3072]{1,0:T(8,128)(2,1)S(1)} collective-permute-done((bf16[24,3072]{1,0:T(8,128)(2,1)S(1)}, bf16[24,3072]{1,0:T(8,128)(2,1)S(1)}, u32[]{:S(2)}, u32[]{:S(2)}) %collective-permute-start.18) | collective-permute-done | bytes 147488 | tf_op jit(solution)/shard_map/ppermute | solution.py:370
  182.4 0.1 convert_add_fusion
  182.4 0.8 maximum_bitcast_fusion
  183.2 0.0 all-to-all-done.1.home_ref
  183.2 2.8 %unpack.1 = (bf16[128,3072]{1,0:T(8,128)(2,1)}, bf16[128,3072]{1,0:T(8,128)(2,1)}, bf16[128,3072]{1,0:T(8,128)(2,1)}) custom-call(bf16[8,3,128,384]{3,2,1,0:T(8,128)(2,1)} %all-to-all-done.1.home_ref), custom_call_target="tpu_custom_call" | custom-call | bytes 4718592 | tf_op jit(solution)/shard_map/unpack/pallas_call | solution.py:78
  (34 shorter events, 0.2 us)
Async XLA Ops:
  8.8 32.1 %collective-permute-start = (bf16[128,5120]{1,0:T(8,128)(2,1)}, bf16[128,5120]{1,0:T(8,128)(2,1)S(1)}, u32[]{:S(2)}, u32[]{:S(2)}) collective-permute-start(bf16[128,5120]{1,0:T(8,128)(2,1)} %bitcast.52), channel_id=1, source_target_pairs={{0,128},{1,129},{2,130},{3,131},{4,132},{5,133},{6,134},{7,135},{8... | collective-permute-start | bytes 3932168 | tf_op jit(solution)/shard_map/ppermute | solution.py:386
  16.5 34.5 %all-to-all-start = ((bf16[8,3,128,384]{3,2,1,0:T(8,128)(2,1)}), bf16[8,3,128,384]{3,2,1,0:T(8,128)(2,1)}, u32[]{:S(2)}, u32[]{:S(2)}) async-start(bf16[8,3,128,384]{3,2,1,0:T(8,128)(2,1)} %pack.1.refs_0_), calls=%async_computation | async-start | bytes 4718592 | tf_op jit(solution)/shard_map/all_to_all | solution.py:360
  21.8 106.4 %all-gather.2.cloned.1.call-start = ((), (), s32[]{:S(2)}) async-start(), calls=%async_computation.3 | async-start | bytes 4177920 | tf_op jit(solution)/shard_map/all_gather | solution.py:393
  40.9 1.1 copy-start.6
  44.8 6.2 %collective-permute-start.1 = (bf16[128,5120]{1,0:T(8,128)(2,1)}, bf16[128,5120]{1,0:T(8,128)(2,1)S(1)}, u32[]{:S(2)}, u32[]{:S(2)}) collective-permute-start(bf16[128,5120]{1,0:T(8,128)(2,1)} %gated.1.own_ref), channel_id=1, source_target_pairs={{0,16},{16,0},{32,48},{48,32},{64,80},{80,64},{96,112},{112,96},{1... | collective-permute-start | bytes 3932168 | tf_op jit(solution)/shard_map/ppermute | solution.py:300
  51.0 1.1 copy-start.3
  54.2 14.2 %collective-permute-start.2 = (bf16[256,2048]{1,0:T(8,128)(2,1)}, bf16[256,2048]{1,0:T(8,128)(2,1)S(1)}, u32[]{:S(2)}, u32[]{:S(2)}) collective-permute-start(bf16[256,2048]{1,0:T(8,128)(2,1)} %pair_up.2.refs_0_), channel_id=1, source_target_pairs={{0,32},{16,112},{32,64},{48,16},{64,96},{80,48},{96,0},{112,80},{1... | collective-permute-start | bytes 3145736 | tf_op jit(solution)/shard_map/ppermute | solution.py:300
  68.4 1.0 copy-start.2
  69.4 19.9 %collective-permute-start.5 = (bf16[256,3072]{1,0:T(8,128)(2,1)}, bf16[256,3072]{1,0:T(8,128)(2,1)}, u32[]{:S(2)}, u32[]{:S(2)}) collective-permute-start(bf16[256,3072]{1,0:T(8,128)(2,1)} %hold.8.refs_1_.refs_0_.refs_5_), channel_id=1, source_target_pairs={{0,32},{16,112},{32,64},{48,16},{64,96},{80,48},{96,0},{112,80},{1... | collective-permute-start | bytes 4718600 | tf_op jit(solution)/shard_map/ppermute | solution.py:300
  72.3 23.4 %collective-permute-start.4 = (bf16[128,2048]{1,0:T(8,128)(2,1)S(1)}, bf16[128,2048]{1,0:T(8,128)(2,1)S(1)}, u32[]{:S(2)}, u32[]{:S(2)}) collective-permute-start(bf16[128,2048]{1,0:T(8,128)(2,1)S(1)} %slice.40), channel_id=1, source_target_pairs={{0,32},{16,112},{32,64},{48,16},{64,96},{80,48},{96,0},{112,80},{1... | collective-permute-start | bytes 1572872 | tf_op jit(solution)/shard_map/ppermute | solution.py:300
  72.4 28.2 %collective-permute-start.3 = (bf16[256,2048]{1,0:T(8,128)(2,1)}, bf16[256,2048]{1,0:T(8,128)(2,1)S(1)}, u32[]{:S(2)}, u32[]{:S(2)}) collective-permute-start(bf16[256,2048]{1,0:T(8,128)(2,1)} %hold.9.refs_1_), channel_id=1, source_target_pairs={{0,16},{16,0},{32,48},{48,32},{64,80},{80,64},{96,112},{112,96},{1... | collective-permute-start | bytes 3145736 | tf_op jit(solution)/shard_map/ppermute | solution.py:300
  90.5 18.7 %collective-permute-start.8 = (bf16[128,3072]{1,0:T(8,128)(2,1)S(1)}, bf16[128,3072]{1,0:T(8,128)(2,1)S(1)}, u32[]{:S(2)}, u32[]{:S(2)}) collective-permute-start(bf16[128,3072]{1,0:T(8,128)(2,1)S(1)} %slice.41), channel_id=1, source_target_pairs={{0,32},{16,112},{32,64},{48,16},{64,96},{80,48},{96,0},{112,80},{1... | collective-permute-start | bytes 2359304 | tf_op jit(solution)/shard_map/ppermute | solution.py:300
  93.2 21.3 %collective-permute-start.7 = (bf16[256,3072]{1,0:T(8,128)(2,1)}, bf16[256,3072]{1,0:T(8,128)(2,1)}, u32[]{:S(2)}, u32[]{:S(2)}) collective-permute-start(bf16[256,3072]{1,0:T(8,128)(2,1)} %collective-permute-done.5.refs_1_.refs_6_), channel_id=1, source_target_pairs={{0,16},{16,0},{32,48},{48,32},{64,80},{80,64},{96,112},{112,96},{1... | collective-permute-start | bytes 4718600 | tf_op jit(solution)/shard_map/ppermute | solution.py:300
  95.6 0.8 copy-start.5
  96.4 5.9 %collective-permute-start.6 = (bf16[128,2048]{1,0:T(8,128)(2,1)}, bf16[128,2048]{1,0:T(8,128)(2,1)S(1)}, u32[]{:S(2)}, u32[]{:S(2)}) collective-permute-start(bf16[128,2048]{1,0:T(8,128)(2,1)} %hold.10.refs_3_), channel_id=1, source_target_pairs={{0,16},{16,0},{32,48},{48,32},{64,80},{80,64},{96,112},{112,96},{1... | collective-permute-start | bytes 1572872 | tf_op jit(solution)/shard_map/ppermute | solution.py:300
  100.6 1.7 copy-start.7
  102.3 0.8 copy-start.10
  109.2 0.9 copy-start.8
  110.1 4.5 %collective-permute-start.9 = (bf16[128,3072]{1,0:T(8,128)(2,1)}, bf16[128,3072]{1,0:T(8,128)(2,1)S(1)}, u32[]{:S(2)}, u32[]{:S(2)}) collective-permute-start(bf16[128,3072]{1,0:T(8,128)(2,1)} %hold.11.refs_3_.refs_8_), channel_id=1, source_target_pairs={{0,16},{16,0},{32,48},{48,32},{64,80},{80,64},{96,112},{112,96},{1... | collective-permute-start | bytes 2359304 | tf_op jit(solution)/shard_map/ppermute | solution.py:300
  110.4 36.0 %all-to-all-start.2 = ((bf16[4,96,2048]{2,1,0:T(8,128)(2,1)}), bf16[4,96,2048]{2,1,0:T(8,128)(2,1)S(1)}, u32[]{:S(2)}, u32[]{:S(2)}) async-start(bf16[4,96,2048]{2,1,0:T(8,128)(2,1)} %weight_grad.2.refs_1_), calls=%async_computation.2 | async-start | bytes 3145728 | tf_op jit(solution)/shard_map/all_to_all | solution.py:360
  114.5 0.9 copy-start.11
  123.1 37.3 %collective-permute-start.13 = (bf16[96,3072]{1,0:T(8,128)(2,1)}, bf16[96,3072]{1,0:T(8,128)(2,1)S(1)}, u32[]{:S(2)}, u32[]{:S(2)}) collective-permute-start(bf16[96,3072]{1,0:T(8,128)(2,1)} %get-tuple-element.19), channel_id=1, source_target_pairs={{0,4},{4,8},{8,12},{12,0},{1,5},{5,9},{9,13},{13,1},{2,6},{6,10},{... | collective-permute-start | bytes 1769480 | tf_op jit(solution)/shard_map/ppermute | solution.py:370
  124.5 40.2 %collective-permute-start.14 = (bf16[96,3072]{1,0:T(8,128)(2,1)}, bf16[96,3072]{1,0:T(8,128)(2,1)}, u32[]{:S(2)}, u32[]{:S(2)}) collective-permute-start(bf16[96,3072]{1,0:T(8,128)(2,1)} %get-tuple-element.20), channel_id=1, source_target_pairs={{0,8},{4,12},{8,0},{12,4},{1,9},{5,13},{9,1},{13,5},{2,10},{6,14},... | collective-permute-start | bytes 1769480 | tf_op jit(solution)/shard_map/ppermute | solution.py:370
  126.9 37.8 %collective-permute-start.15 = (bf16[96,3072]{1,0:T(8,128)(2,1)}, bf16[96,3072]{1,0:T(8,128)(2,1)}, u32[]{:S(2)}, u32[]{:S(2)}) collective-permute-start(bf16[96,3072]{1,0:T(8,128)(2,1)} %get-tuple-element.21), channel_id=1, source_target_pairs={{0,12},{4,0},{8,4},{12,8},{1,13},{5,1},{9,5},{13,9},{2,14},{6,2},{... | collective-permute-start | bytes 1769480 | tf_op jit(solution)/shard_map/ppermute | solution.py:370
  146.3 1.1 copy-start
  147.5 35.8 %all-to-all-start.1 = ((bf16[8,3,128,384]{3,2,1,0:T(8,128)(2,1)}), bf16[8,3,128,384]{3,2,1,0:T(8,128)(2,1)}, u32[]{:S(2)}, u32[]{:S(2)}) async-start(bf16[8,3,128,384]{3,2,1,0:T(8,128)(2,1)} %backward.1.refs_1_), calls=%async_computation.1 | async-start | bytes 4718592 | tf_op jit(solution)/shard_map/all_to_all | solution.py:360
  153.4 1.4 copy-start.1
  154.8 10.0 %copy-start.4 = (bf16[96,3072]{1,0:T(8,128)(2,1)S(1)}, bf16[96,3072]{1,0:T(8,128)(2,1)}, u32[]{:S(2)}) copy-start(bf16[96,3072]{1,0:T(8,128)(2,1)} %hold.13) | copy-start | bytes 1769476
  155.1 15.1 %collective-permute-start.10 = (bf16[24,2048]{1,0:T(8,128)(2,1)S(1)}, bf16[24,2048]{1,0:T(8,128)(2,1)S(1)}, u32[]{:S(2)}, u32[]{:S(2)}) collective-permute-start(bf16[24,2048]{1,0:T(8,128)(2,1)S(1)} %get-tuple-element.25), channel_id=1, source_target_pairs={{0,1},{1,2},{2,3},{3,0},{4,5},{5,6},{6,7},{7,4},{8,9},{9,10},{10,1... | collective-permute-start | bytes 294920 | tf_op jit(solution)/shard_map/ppermute | solution.py:370
  158.1 13.8 %collective-permute-start.12 = (bf16[24,2048]{1,0:T(8,128)(2,1)S(1)}, bf16[24,2048]{1,0:T(8,128)(2,1)S(1)}, u32[]{:S(2)}, u32[]{:S(2)}) collective-permute-start(bf16[24,2048]{1,0:T(8,128)(2,1)S(1)} %get-tuple-element.26), channel_id=1, source_target_pairs={{0,3},{1,0},{2,1},{3,2},{4,7},{5,4},{6,5},{7,6},{8,11},{9,8},{10,9... | collective-permute-start | bytes 294920 | tf_op jit(solution)/shard_map/ppermute | solution.py:370
  160.4 4.4 %copy-start.9 = (bf16[96,3072]{1,0:T(8,128)(2,1)}, bf16[96,3072]{1,0:T(8,128)(2,1)S(1)}, u32[]{:S(2)}) copy-start(bf16[96,3072]{1,0:T(8,128)(2,1)S(1)} %collective-permute-done.13) | copy-start | bytes 1769476
  160.4 11.4 %collective-permute-start.11 = (bf16[24,2048]{1,0:T(8,128)(2,1)S(1)}, bf16[24,2048]{1,0:T(8,128)(2,1)S(1)}, u32[]{:S(2)}, u32[]{:S(2)}) collective-permute-start(bf16[24,2048]{1,0:T(8,128)(2,1)S(1)} %get-tuple-element.27), channel_id=1, source_target_pairs={{0,2},{1,3},{2,0},{3,1},{4,6},{5,7},{6,4},{7,5},{8,10},{9,11},{10,... | collective-permute-start | bytes 294920 | tf_op jit(solution)/shard_map/ppermute | solution.py:370
  166.6 7.9 %collective-permute-start.16 = (bf16[24,3072]{1,0:T(8,128)(2,1)S(1)}, bf16[24,3072]{1,0:T(8,128)(2,1)S(1)}, u32[]{:S(2)}, u32[]{:S(2)}) collective-permute-start(bf16[24,3072]{1,0:T(8,128)(2,1)S(1)} %get-tuple-element.22), channel_id=1, source_target_pairs={{0,1},{1,2},{2,3},{3,0},{4,5},{5,6},{6,7},{7,4},{8,9},{9,10},{10,1... | collective-permute-start | bytes 442376 | tf_op jit(solution)/shard_map/ppermute | solution.py:370
  166.7 15.6 %collective-permute-start.18 = (bf16[24,3072]{1,0:T(8,128)(2,1)S(1)}, bf16[24,3072]{1,0:T(8,128)(2,1)S(1)}, u32[]{:S(2)}, u32[]{:S(2)}) collective-permute-start(bf16[24,3072]{1,0:T(8,128)(2,1)S(1)} %get-tuple-element.23), channel_id=1, source_target_pairs={{0,3},{1,0},{2,1},{3,2},{4,7},{5,4},{6,5},{7,6},{8,11},{9,8},{10,9... | collective-permute-start | bytes 442376 | tf_op jit(solution)/shard_map/ppermute | solution.py:370
  170.2 12.1 %collective-permute-start.17 = (bf16[24,3072]{1,0:T(8,128)(2,1)S(1)}, bf16[24,3072]{1,0:T(8,128)(2,1)S(1)}, u32[]{:S(2)}, u32[]{:S(2)}) collective-permute-start(bf16[24,3072]{1,0:T(8,128)(2,1)S(1)} %get-tuple-element.24), channel_id=1, source_target_pairs={{0,2},{1,3},{2,0},{3,1},{4,6},{5,7},{6,4},{7,5},{8,10},{9,11},{10,... | collective-permute-start | bytes 442376 | tf_op jit(solution)/shard_map/ppermute | solution.py:370
Sparse Core Ops, SparseCore 0:
  52.3 72.9 all-gather.1
